TPU v7x, 32 devices: a whole 2x2x4 slice. The times are simulated.
32 devices in a mesh: segment: 4 (over y, x), feat: 4 (over z), tok: 2 (over core).
Axes of the slice: x: 2, y: 2, z: 4, core: 2. Of those that a mesh axis runs over, the one named last changes fastest.
Arguments:
- layer_inputs: bfloat16 [4, 448, 2304], P('segment', 'feat', 'tok'), may hold values from -6 to 6
- targets: bfloat16 [4, 448, 2304], P('segment', 'tok', 'feat'), may hold values from -6 to 6
- enc_weight: bfloat16 [4, 2304, 12288], P('segment', 'feat', 'tok'), may hold values from -0.125 to 0.125
- enc_bias: float32 [4, 12288], P('segment', 'tok'), may hold values from -3 to 3
- dec_weight: bfloat16 [4, 4, 2304, 12288], P('segment', None, 'feat', 'tok'), may hold values from -0.0546875 to 0.0546875
Outputs:
- features: bfloat16 [4, 448, 12288], P('segment', 'feat', 'tok')
- residual: float32 [4, 448, 2304], P('segment', 'tok', 'feat')
All inputs are finite; a program needn't handle non-finite values.
Results may differ from a plain program's by a relative error of at most 0.01.
Values may be sent and summed in bfloat16 or wider, within the bound.
No kernel may reach another device: no remote copies, remote signals or barrier semaphores. Data moves between devices by JAX's collectives and lax.ppermute only.
A program may use at most 128 MiB of HBM per device.

v0:
```python
import jax
import jax.numpy as jnp
from jax import lax
from jax.sharding import PartitionSpec as P

BF16 = jnp.bfloat16
F32 = jnp.float32
GROUPS = 2
CHUNKS = 2
STREAMS = 2


def local(segments, ring, cores, layer_inputs, targets, enc_weight, enc_bias, dec_weight):
    z = lax.axis_index("feat")
    core = lax.axis_index("tok")
    segment = lax.axis_index("segment")
    odd = z % 2 == 1
    rows = layer_inputs.shape[1] // GROUPS
    width = enc_weight.shape[2] // CHUNKS
    depth = enc_weight.shape[1]
    weight = enc_weight[0]
    decoders = dec_weight[0]
    layers = decoders.shape[0]
    per_core = ring // cores

    own_rows = lax.all_gather(layer_inputs[0], "tok", axis=1, tiled=True)

    def exchanged(group):
        block = own_rows[group * rows : (group + 1) * rows]
        parts = []
        for k in range(ring):
            part = lax.dynamic_slice_in_dim(block, ((z + k) % ring) * depth, depth, axis=1)
            if k:
                part = lax.ppermute(part, "feat", [(i, (i + k) % ring) for i in range(ring)])
            parts.append(part)
        return jnp.concatenate(parts, axis=0)

    columns = [exchanged(group) for group in range(GROUPS)]

    def partial_sums(group, chunk):
        part = jnp.dot(
            columns[group], weight[:, chunk * width : (chunk + 1) * width], preferred_element_type=F32
        )
        return [part[k * rows : (k + 1) * rows] for k in range(ring)]

    units = [(group, chunk) for group in range(GROUPS) for chunk in range(CHUNKS)]
    finished = {}
    decoded = {}

    def decode(unit, codes):
        group, chunk = unit
        all_codes = jnp.concatenate(codes, axis=0)
        out = jnp.einsum(
            "nf,ldf->lnd",
            all_codes,
            decoders[:, :, chunk * width : (chunk + 1) * width],
            preferred_element_type=F32,
        )
        decoded[group] = out if group not in decoded else decoded[group] + out

    class Stream:
        def __init__(self, own):
            self.own = own
            self.step = 0
            self.slot = 1
            self.got = [{}, {}]
            self.sums = partial_sums(*own[0])

        def swap(self, value, side):
            i, k, n = self.step, self.slot, len(self.own)
            pairs = []
            for p in range(side, ring - 1, 2):
                q = ring - 2 - p
                if not (i == 0 and p >= k or i == n and p < k):
                    pairs.append((p, p + 1))
                if not (i == 0 and q >= k or i == n and q < k):
                    pairs.append((p + 1, p))
            return lax.ppermute(value, "feat", pairs) if pairs else None

        def advance(self):
            i, k, n = self.step, self.slot, len(self.own)
            sent = []
            for side in range(2):
                if k == 0:
                    sent.append(finished[self.own[i - 1]])
                    continue
                value = self.got[1 - side].get(k - 1)
                if i < n:
                    rightward = odd == (side == 1)
                    own = jnp.where(
                        rightward,
                        jnp.where(k > z, self.sums[k], 0.0),
                        jnp.where(k > ring - 1 - z, self.sums[ring - k], 0.0),
                    )
                    value = (own if value is None else own + value.astype(F32)).astype(BF16)
                sent.append(value)
            for side in range(2):
                got = self.swap(sent[side], side) if sent[side] is not None else None
                if got is not None:
                    self.got[side][k] = got
            if i and k == ring - 2:
                unit = self.own[i - 1]
                codes = [finished[unit]]
                zero = jnp.zeros_like(codes[0])
                for m in range(1, ring):
                    a, b = m - 1, ring - m - 1
                    left = jnp.where(odd, self.got[0].get(a, zero), self.got[1].get(a, zero))
                    right = jnp.where(odd, self.got[1].get(b, zero), self.got[0].get(b, zero))
                    codes.append(jnp.where(m <= z, left, right))
                decode(unit, codes)
            self.slot += 1
            if i < n and k == ring - 1:
                chunk = self.own[i][1]
                bias = enc_bias[0, chunk * width : (chunk + 1) * width][None, :]
                total = self.sums[0] + self.got[0][k].astype(F32) + self.got[1][k].astype(F32)
                finished[self.own[i]] = jax.nn.relu(total + bias).astype(BF16)
                self.slot, self.step = 0, i + 1
                if i + 1 < n:
                    self.sums = partial_sums(*self.own[i + 1])
                self.got = [{}, {}]
                return True
            return not (i == n and k == ring - 2)

    def residual_rows(group):
        blocks = decoded[group].reshape(layers, ring, rows, depth)

        def share(index):
            first = index * per_core
            return jnp.stack(
                [
                    lax.dynamic_index_in_dim(blocks, (z - first - b) % ring, axis=1, keepdims=False)
                    for b in range(per_core)
                ],
                axis=1,
            )

        total = share(core)
        for k in range(1, cores):
            sent = share((core + k) % cores).astype(BF16)
            total += lax.ppermute(sent, "tok", [(i, (i + k) % cores) for i in range(cores)]).astype(F32)
        own = lax.dynamic_index_in_dim(total, segment, axis=0, keepdims=False)
        for k in range(1, segments):
            place = jnp.minimum(segment + k, layers - 1)
            sent = lax.dynamic_index_in_dim(total, place, axis=0, keepdims=False).astype(BF16)
            own += lax.ppermute(sent, "segment", [(i, i + k) for i in range(segments - k)]).astype(F32)
        return own

    streams = [Stream(units[i::STREAMS]) for i in range(STREAMS)]
    going = [True] * STREAMS
    while any(going):
        for i, stream in enumerate(streams):
            if going[i]:
                going[i] = stream.advance()
    own = jnp.stack([residual_rows(group) for group in range(GROUPS)], axis=1)
    residual = targets[0].astype(F32) - own.reshape(targets.shape[1:])
    features = jnp.concatenate(
        [
            jnp.concatenate([finished[group, chunk] for chunk in range(CHUNKS)], axis=1)
            for group in range(GROUPS)
        ],
        axis=0,
    )
    return (features[None], residual[None])


def solution(mesh):
    in_specs = (
        P("segment", "feat", "tok"),
        P("segment", "tok", "feat"),
        P("segment", "feat", "tok"),
        P("segment", "tok"),
        P("segment", None, "feat", "tok"),
    )
    out_specs = (P("segment", "feat", "tok"), P("segment", "tok", "feat"))
    sizes = (mesh.shape["segment"], mesh.shape["feat"], mesh.shape["tok"])
    return jax.shard_map(
        lambda *args: local(*sizes, *args), mesh=mesh, in_specs=in_specs, out_specs=out_specs, check_vma=False
    )
```

profile of v0, /device:TPU:0, one launch (start us, length us, event | category | flops | bytes accessed | tf_op | source)
XLA Modules:
  0.0 232.5 jit_solution(12702623082901046530)
XLA Ops:
  0.7 2.5 %all-gather = bf16[1,112,2304]{2,1,0:T(8,128)(2,1)S(1)} all-gather(bf16[1,112,1152]{2,1,0:T(8,128)(2,1)} %param.5), channel_id=2, replica_groups=mesh['segment'=4,'feat'=4,'tok'=2] {'tok'}, dimensions={2}, use_global_device_ids=true | all-gather | bytes 774144 | tf_op jit(solution)/shard_map/all_gather | solution.py:26
  3.4 4.0 %collective-permute-start.14 = (bf16[56,576]{1,0:T(8,128)(2,1)S(1)}, bf16[56,576]{1,0:T(8,128)(2,1)S(1)}, u32[]{:S(2)}, u32[]{:S(2)}) collective-permute-start(bf16[56,576]{1,0:T(8,128)(2,1)S(1)} %get-tuple-element.51), channel_id=1, source_target_pairs={{0,4},{2,6},{4,0},{6,2},{1,5},{3,7},{5,1},{7,3},{8,12},{10,14},{12... | collective-permute-start | bytes 193544 | tf_op jit(solution)/shard_map/ppermute | solution.py:34
  9.6 2.5 %collective-permute-start = (bf16[56,576]{1,0:T(8,128)(2,1)S(1)}, bf16[56,576]{1,0:T(8,128)(2,1)S(1)}, u32[]{:S(2)}, u32[]{:S(2)}) collective-permute-start(bf16[56,576]{1,0:T(8,128)(2,1)S(1)} %get-tuple-element.48), channel_id=1, source_target_pairs={{0,2},{2,4},{4,6},{6,0},{1,3},{3,5},{5,7},{7,1},{8,10},{10,12},{12... | collective-permute-start | bytes 193544 | tf_op jit(solution)/shard_map/ppermute | solution.py:34
  13.4 4.5 %collective-permute-done.1 = bf16[56,576]{1,0:T(8,128)(2,1)S(1)} collective-permute-done((bf16[56,576]{1,0:T(8,128)(2,1)S(1)}, bf16[56,576]{1,0:T(8,128)(2,1)S(1)}, u32[]{:S(2)}, u32[]{:S(2)}) %collective-permute-start.1) | collective-permute-done | bytes 64544 | tf_op jit(solution)/shard_map/ppermute | solution.py:34
  17.9 3.3 %collective-permute-start.15 = (bf16[56,576]{1,0:T(8,128)(2,1)S(1)}, bf16[56,576]{1,0:T(8,128)(2,1)S(1)}, u32[]{:S(2)}, u32[]{:S(2)}) collective-permute-start(bf16[56,576]{1,0:T(8,128)(2,1)S(1)} %get-tuple-element.53), channel_id=1, source_target_pairs={{0,6},{2,0},{4,2},{6,4},{1,7},{3,1},{5,3},{7,5},{8,14},{10,8},{12,... | collective-permute-start | bytes 193544 | tf_op jit(solution)/shard_map/ppermute | solution.py:34
  21.3 3.4 %fusion.10 = f32[224,3072]{1,0:T(8,128)S(1)} fusion(bf16[576,6144]{1,0:T(8,128)(2,1)} %bitcast.86, bf16[56,576]{1,0:T(8,128)(2,1)S(1)} %collective-permute-done.2, bf16[56,576]{1,0:T(8,128)(2,1)S(1)} %collective-permute-done.1, bf16[56,576]{1,0:T(8,128)(2,1)S(1)} %collective-permute-done, bf16[56,576]{1,0:T(8,128)(2,1)S(1)} %get-tuple-element.46), kind=kOutput, calls=%fused_computation.10 | convolution fusion | flops 793755648 | bytes 6549504 | tf_op jit(solution)/shard_map/dot_general | solution.py:41
  35.4 13.9 %collective-permute-done.3 = bf16[56,3072]{1,0:T(8,128)(2,1)S(1)} collective-permute-done((bf16[56,3072]{1,0:T(8,128)(2,1)S(1)}, bf16[56,3072]{1,0:T(8,128)(2,1)S(1)}, u32[]{:S(2)}, u32[]{:S(2)}) %collective-permute-start.3) | collective-permute-done | bytes 344096 | tf_op jit(solution)/shard_map/ppermute | solution.py:78
  50.4 5.5 %collective-permute-start.10 = (bf16[56,3072]{1,0:T(8,128)(2,1)S(1)}, bf16[56,3072]{1,0:T(8,128)(2,1)S(1)}, u32[]{:S(2)}, u32[]{:S(2)}) collective-permute-start(bf16[56,3072]{1,0:T(8,128)(2,1)S(1)} %get-tuple-element.18), channel_id=1, source_target_pairs={{0,2},{2,0},{4,6},{6,4},{1,3},{3,1},{5,7},{7,5},{8,10},{10,8},{12,... | collective-permute-start | bytes 1032200 | tf_op jit(solution)/shard_map/ppermute | solution.py:78
  56.9 8.2 %collective-permute-start.5 = (bf16[56,3072]{1,0:T(8,128)(2,1)S(1)}, bf16[56,3072]{1,0:T(8,128)(2,1)S(1)}, u32[]{:S(2)}, u32[]{:S(2)}) collective-permute-start(bf16[56,3072]{1,0:T(8,128)(2,1)S(1)} %get-tuple-element.8), channel_id=1, source_target_pairs={{0,2},{2,0},{4,6},{6,4},{1,3},{3,1},{5,7},{7,5},{8,10},{10,8},{12,... | collective-permute-start | bytes 1032200 | tf_op jit(solution)/shard_map/ppermute | solution.py:78
  66.0 6.5 %collective-permute-start.28 = (bf16[56,3072]{1,0:T(8,128)(2,1)S(1)}, bf16[56,3072]{1,0:T(8,128)(2,1)S(1)}, u32[]{:S(2)}, u32[]{:S(2)}) collective-permute-start(bf16[56,3072]{1,0:T(8,128)(2,1)S(1)} %fusion.57), channel_id=1, source_target_pairs={{0,2},{2,0},{4,6},{6,4},{1,3},{3,1},{5,7},{7,5},{8,10},{10,8},{12,... | collective-permute-start | bytes 1032200 | tf_op jit(solution)/shard_map/ppermute | solution.py:78
  73.8 6.0 %collective-permute-start.20 = (bf16[56,3072]{1,0:T(8,128)(2,1)S(1)}, bf16[56,3072]{1,0:T(8,128)(2,1)S(1)}, u32[]{:S(2)}, u32[]{:S(2)}) collective-permute-start(bf16[56,3072]{1,0:T(8,128)(2,1)S(1)} %fusion.61), channel_id=1, source_target_pairs={{0,2},{2,0},{4,6},{6,4},{1,3},{3,1},{5,7},{7,5},{8,10},{10,8},{12,... | collective-permute-start | bytes 1032200 | tf_op jit(solution)/shard_map/ppermute | solution.py:78
  81.2 6.0 %collective-permute-start.25 = (bf16[56,3072]{1,0:T(8,128)(2,1)S(1)}, bf16[56,3072]{1,0:T(8,128)(2,1)S(1)}, u32[]{:S(2)}, u32[]{:S(2)}) collective-permute-start(bf16[56,3072]{1,0:T(8,128)(2,1)S(1)} %get-tuple-element.16), channel_id=1, source_target_pairs={{0,2},{2,0},{4,6},{6,4},{1,3},{3,1},{5,7},{7,5},{8,10},{10,8},{12,... | collective-permute-start | bytes 1032200 | tf_op jit(solution)/shard_map/ppermute | solution.py:78
  88.6 6.0 %collective-permute-start.17 = (bf16[56,3072]{1,0:T(8,128)(2,1)S(1)}, bf16[56,3072]{1,0:T(8,128)(2,1)S(1)}, u32[]{:S(2)}, u32[]{:S(2)}) collective-permute-start(bf16[56,3072]{1,0:T(8,128)(2,1)S(1)} %get-tuple-element.6), channel_id=1, source_target_pairs={{0,2},{2,0},{4,6},{6,4},{1,3},{3,1},{5,7},{7,5},{8,10},{10,8},{12,... | collective-permute-start | bytes 1032200 | tf_op jit(solution)/shard_map/ppermute | solution.py:78
  96.7 8.9 %collective-permute-start.30 = (bf16[56,3072]{1,0:T(8,128)(2,1)S(1)}, bf16[56,3072]{1,0:T(8,128)(2,1)S(1)}, u32[]{:S(2)}, u32[]{:S(2)}) collective-permute-start(bf16[56,3072]{1,0:T(8,128)(2,1)S(1)} %get-tuple-element.15), channel_id=1, source_target_pairs={{0,2},{2,0},{4,6},{6,4},{1,3},{3,1},{5,7},{7,5},{8,10},{10,8},{12,... | collective-permute-start | bytes 1032200 | tf_op jit(solution)/shard_map/ppermute | solution.py:78
  106.5 6.5 %collective-permute-start.22 = (bf16[56,3072]{1,0:T(8,128)(2,1)S(1)}, bf16[56,3072]{1,0:T(8,128)(2,1)S(1)}, u32[]{:S(2)}, u32[]{:S(2)}) collective-permute-start(bf16[56,3072]{1,0:T(8,128)(2,1)S(1)} %get-tuple-element.5), channel_id=1, source_target_pairs={{0,2},{2,0},{4,6},{6,4},{1,3},{3,1},{5,7},{7,5},{8,10},{10,8},{12,... | collective-permute-start | bytes 1032200 | tf_op jit(solution)/shard_map/ppermute | solution.py:78
  115.6 1.9 collective-permute-start.27
  118.9 3.0 %collective-permute-done.22 = bf16[56,3072]{1,0:T(8,128)(2,1)S(1)} collective-permute-done((bf16[56,3072]{1,0:T(8,128)(2,1)S(1)}, bf16[56,3072]{1,0:T(8,128)(2,1)S(1)}, u32[]{:S(2)}, u32[]{:S(2)}) %collective-permute-start.22) | collective-permute-done | bytes 344096 | tf_op jit(solution)/shard_map/ppermute | solution.py:78
  123.1 2.0 collective-permute-start.19
  127.4 11.2 %fusion.2 = f32[224,4,576]{2,0,1:T(8,128)} fusion(bf16[4,576,6144]{2,1,0:T(8,128)(2,1)} %bitcast.82, bf16[56,3072]{1,0:T(8,128)(2,1)} %get-tuple-element.33, bf16[56,3072]{1,0:T(8,128)(2,1)} %select_select_fusion.7, bf16[56,3072]{1,0:T(8,128)(2,1)} %get-tuple-element.32, bf16[56,3072]{1,0:T(8,128)(2,1)} %copy-done.1), kind=kOutput, calls=%fused_computation.2 | convolution fusion | flops 3176398848 | bytes 17596416 | tf_op jit(solution)/shard_map/nf,ldf->lnd/dot_general | solution.py:53
  143.3 3.3 %collective-permute-start.41 = (bf16[56,3072]{1,0:T(8,128)(2,1)S(1)}, bf16[56,3072]{1,0:T(8,128)(2,1)}, u32[]{:S(2)}, u32[]{:S(2)}) collective-permute-start(bf16[56,3072]{1,0:T(8,128)(2,1)S(1)} %fusion.49), channel_id=1, source_target_pairs={{0,2},{2,0},{4,6},{6,4},{1,3},{3,1},{5,7},{7,5},{8,10},{10,8},{12,... | collective-permute-start | bytes 1032200 | tf_op jit(solution)/shard_map/ppermute | solution.py:78
  149.2 2.2 collective-permute-start.36
  152.7 3.0 %collective-permute-done.41 = bf16[56,3072]{1,0:T(8,128)(2,1)} collective-permute-done((bf16[56,3072]{1,0:T(8,128)(2,1)S(1)}, bf16[56,3072]{1,0:T(8,128)(2,1)}, u32[]{:S(2)}, u32[]{:S(2)}) %collective-permute-start.41) | collective-permute-done | bytes 344096 | tf_op jit(solution)/shard_map/ppermute | solution.py:78
  157.1 10.4 %fusion.16 = f32[224,4,576]{2,0,1:T(8,128)S(1)} fusion(f32[224,4,576]{2,0,1:T(8,128)} %fusion.2, bf16[4,576,6144]{2,1,0:T(8,128)(2,1)} %bitcast.83, bf16[56,3072]{1,0:T(8,128)(2,1)} %get-tuple-element.31, bf16[56,3072]{1,0:T(8,128)(2,1)S(1)} %copy-done.6, bf16[56,3072]{1,0:T(8,128)(2,1)} %get-tuple-element.30, bf16[56,3072]{1,0:T(8,128)(2,1)S(1)} %copy-done.4), kind=kOutput, calls=%fused_computation.16 | convolution fusion | flops 3176914944 | bytes 19890176 | tf_op jit(solution)/shard_map/nf,ldf->lnd/dot_general | solution.py:53
  173.5 7.2 %collective-permute-done.40 = bf16[56,3072]{1,0:T(8,128)(2,1)S(1)} collective-permute-done((bf16[56,3072]{1,0:T(8,128)(2,1)}, bf16[56,3072]{1,0:T(8,128)(2,1)S(1)}, u32[]{:S(2)}, u32[]{:S(2)}) %collective-permute-start.40) | collective-permute-done | bytes 344096 | tf_op jit(solution)/shard_map/ppermute | solution.py:78
  180.8 3.6 %collective-permute-done.44 = bf16[56,3072]{1,0:T(8,128)(2,1)S(1)} collective-permute-done((bf16[56,3072]{1,0:T(8,128)(2,1)}, bf16[56,3072]{1,0:T(8,128)(2,1)S(1)}, u32[]{:S(2)}, u32[]{:S(2)}) %collective-permute-start.44) | collective-permute-done | bytes 344096 | tf_op jit(solution)/shard_map/ppermute | solution.py:78
  186.3 10.9 %fusion = f32[224,4,576]{2,0,1:T(8,128)} fusion(bf16[4,576,6144]{2,1,0:T(8,128)(2,1)} %bitcast.84, bf16[56,3072]{1,0:T(8,128)(2,1)} %get-tuple-element.43, bf16[56,3072]{1,0:T(8,128)(2,1)S(1)} %select_select_fusion.1, bf16[56,3072]{1,0:T(8,128)(2,1)S(1)} %get-tuple-element.42, bf16[56,3072]{1,0:T(8,128)(2,1)S(1)} %fusion.49), kind=kOutput, calls=%fused_computation | convolution fusion | flops 3176398848 | bytes 17596416 | tf_op jit(solution)/shard_map/nf,ldf->lnd/dot_general | solution.py:53
  197.2 2.0 select_select_fusion.5
  199.2 11.7 %fusion.19 = f32[224,4,576]{2,0,1:T(8,128)} fusion(f32[224,4,576]{2,0,1:T(8,128)} %fusion, bf16[4,576,6144]{2,1,0:T(8,128)(2,1)} %bitcast.85, bf16[56,3072]{1,0:T(8,128)(2,1)} %get-tuple-element.41, bf16[56,3072]{1,0:T(8,128)(2,1)S(1)} %select_select_fusion.4, bf16[56,3072]{1,0:T(8,128)(2,1)} %get-tuple-element.40, bf16[56,3072]{1,0:T(8,128)(2,1)S(1)} %fusion.53), kind=kOutput, calls=%fused_computation.17 | convolution fusion | flops 3176914944 | bytes 19890176 | tf_op jit(solution)/shard_map/nf,ldf->lnd/dot_general | solution.py:53
  214.8 3.4 %collective-permute-start.33 = (bf16[2,56,576]{2,1,0:T(8,128)(2,1)S(1)}, bf16[2,56,576]{2,1,0:T(8,128)(2,1)S(1)}, u32[]{:S(2)}, u32[]{:S(2)}) collective-permute-start(bf16[2,56,576]{2,1,0:T(8,128)(2,1)S(1)} %get-tuple-element.34), channel_id=1, source_target_pairs={{0,8},{8,16},{16,24},{1,9},{9,17},{17,25},{2,10},{10,18},{18,26},{... | collective-permute-start | bytes 387080 | tf_op jit(solution)/shard_map/ppermute | solution.py:145
  218.2 2.3 collective-permute-start.35
  222.5 1.9 collective-permute-start.47
  227.1 2.0 collective-permute-done.34
  (140 shorter events, 61.6 us)
Async XLA Ops:
  3.4 25.5 %collective-permute-start.14 = (bf16[56,576]{1,0:T(8,128)(2,1)S(1)}, bf16[56,576]{1,0:T(8,128)(2,1)S(1)}, u32[]{:S(2)}, u32[]{:S(2)}) collective-permute-start(bf16[56,576]{1,0:T(8,128)(2,1)S(1)} %get-tuple-element.51), channel_id=1, source_target_pairs={{0,4},{2,6},{4,0},{6,2},{1,5},{3,7},{5,1},{7,3},{8,12},{10,14},{12... | collective-permute-start | bytes 193544 | tf_op jit(solution)/shard_map/ppermute | solution.py:34
  7.4 22.8 %collective-permute-start.13 = (bf16[56,576]{1,0:T(8,128)(2,1)S(1)}, bf16[56,576]{1,0:T(8,128)(2,1)S(1)}, u32[]{:S(2)}, u32[]{:S(2)}) collective-permute-start(bf16[56,576]{1,0:T(8,128)(2,1)S(1)} %get-tuple-element.52), channel_id=1, source_target_pairs={{0,2},{2,4},{4,6},{6,0},{1,3},{3,5},{5,7},{7,1},{8,10},{10,12},{12... | collective-permute-start | bytes 193544 | tf_op jit(solution)/shard_map/ppermute | solution.py:34
  9.6 11.7 %collective-permute-start = (bf16[56,576]{1,0:T(8,128)(2,1)S(1)}, bf16[56,576]{1,0:T(8,128)(2,1)S(1)}, u32[]{:S(2)}, u32[]{:S(2)}) collective-permute-start(bf16[56,576]{1,0:T(8,128)(2,1)S(1)} %get-tuple-element.48), channel_id=1, source_target_pairs={{0,2},{2,4},{4,6},{6,0},{1,3},{3,5},{5,7},{7,1},{8,10},{10,12},{12... | collective-permute-start | bytes 193544 | tf_op jit(solution)/shard_map/ppermute | solution.py:34
  17.9 13.7 %collective-permute-start.15 = (bf16[56,576]{1,0:T(8,128)(2,1)S(1)}, bf16[56,576]{1,0:T(8,128)(2,1)S(1)}, u32[]{:S(2)}, u32[]{:S(2)}) collective-permute-start(bf16[56,576]{1,0:T(8,128)(2,1)S(1)} %get-tuple-element.53), channel_id=1, source_target_pairs={{0,6},{2,0},{4,2},{6,4},{1,7},{3,1},{5,3},{7,5},{8,14},{10,8},{12,... | collective-permute-start | bytes 193544 | tf_op jit(solution)/shard_map/ppermute | solution.py:34
  26.2 24.0 %collective-permute-start.11 = (bf16[56,3072]{1,0:T(8,128)(2,1)S(1)}, bf16[56,3072]{1,0:T(8,128)(2,1)S(1)}, u32[]{:S(2)}, u32[]{:S(2)}) collective-permute-start(bf16[56,3072]{1,0:T(8,128)(2,1)S(1)} %get-tuple-element.21), channel_id=1, source_target_pairs={{0,2},{6,4},{1,3},{7,5},{8,10},{14,12},{9,11},{15,13},{16,18},{22,... | collective-permute-start | bytes 1032200 | tf_op jit(solution)/shard_map/ppermute | solution.py:78
  28.9 20.4 %collective-permute-start.3 = (bf16[56,3072]{1,0:T(8,128)(2,1)S(1)}, bf16[56,3072]{1,0:T(8,128)(2,1)S(1)}, u32[]{:S(2)}, u32[]{:S(2)}) collective-permute-start(bf16[56,3072]{1,0:T(8,128)(2,1)S(1)} %get-tuple-element.10), channel_id=1, source_target_pairs={{0,2},{6,4},{1,3},{7,5},{8,10},{14,12},{9,11},{15,13},{16,18},{22,... | collective-permute-start | bytes 1032200 | tf_op jit(solution)/shard_map/ppermute | solution.py:78
  30.3 26.4 %collective-permute-start.6 = (bf16[56,3072]{1,0:T(8,128)(2,1)S(1)}, bf16[56,3072]{1,0:T(8,128)(2,1)S(1)}, u32[]{:S(2)}, u32[]{:S(2)}) collective-permute-start(bf16[56,3072]{1,0:T(8,128)(2,1)S(1)} %get-tuple-element.11), channel_id=1, source_target_pairs={{0,2},{6,4},{1,3},{7,5},{8,10},{14,12},{9,11},{15,13},{16,18},{22,... | collective-permute-start | bytes 1032200 | tf_op jit(solution)/shard_map/ppermute | solution.py:78
  34.7 15.4 %collective-permute-start.9 = (bf16[56,3072]{1,0:T(8,128)(2,1)S(1)}, bf16[56,3072]{1,0:T(8,128)(2,1)S(1)}, u32[]{:S(2)}, u32[]{:S(2)}) collective-permute-start(bf16[56,3072]{1,0:T(8,128)(2,1)S(1)} %add_convert_fusion.14), channel_id=1, source_target_pairs={{2,4},{4,2},{3,5},{5,3},{10,12},{12,10},{11,13},{13,11},{18,20},{2... | collective-permute-start | bytes 1032200 | tf_op jit(solution)/shard_map/ppermute | solution.py:78
  50.4 15.4 %collective-permute-start.10 = (bf16[56,3072]{1,0:T(8,128)(2,1)S(1)}, bf16[56,3072]{1,0:T(8,128)(2,1)S(1)}, u32[]{:S(2)}, u32[]{:S(2)}) collective-permute-start(bf16[56,3072]{1,0:T(8,128)(2,1)S(1)} %get-tuple-element.18), channel_id=1, source_target_pairs={{0,2},{2,0},{4,6},{6,4},{1,3},{3,1},{5,7},{7,5},{8,10},{10,8},{12,... | collective-permute-start | bytes 1032200 | tf_op jit(solution)/shard_map/ppermute | solution.py:78
  56.9 16.7 %collective-permute-start.5 = (bf16[56,3072]{1,0:T(8,128)(2,1)S(1)}, bf16[56,3072]{1,0:T(8,128)(2,1)S(1)}, u32[]{:S(2)}, u32[]{:S(2)}) collective-permute-start(bf16[56,3072]{1,0:T(8,128)(2,1)S(1)} %get-tuple-element.8), channel_id=1, source_target_pairs={{0,2},{2,0},{4,6},{6,4},{1,3},{3,1},{5,7},{7,5},{8,10},{10,8},{12,... | collective-permute-start | bytes 1032200 | tf_op jit(solution)/shard_map/ppermute | solution.py:78
  66.0 15.0 %collective-permute-start.28 = (bf16[56,3072]{1,0:T(8,128)(2,1)S(1)}, bf16[56,3072]{1,0:T(8,128)(2,1)S(1)}, u32[]{:S(2)}, u32[]{:S(2)}) collective-permute-start(bf16[56,3072]{1,0:T(8,128)(2,1)S(1)} %fusion.57), channel_id=1, source_target_pairs={{0,2},{2,0},{4,6},{6,4},{1,3},{3,1},{5,7},{7,5},{8,10},{10,8},{12,... | collective-permute-start | bytes 1032200 | tf_op jit(solution)/shard_map/ppermute | solution.py:78
  73.8 14.6 %collective-permute-start.20 = (bf16[56,3072]{1,0:T(8,128)(2,1)S(1)}, bf16[56,3072]{1,0:T(8,128)(2,1)S(1)}, u32[]{:S(2)}, u32[]{:S(2)}) collective-permute-start(bf16[56,3072]{1,0:T(8,128)(2,1)S(1)} %fusion.61), channel_id=1, source_target_pairs={{0,2},{2,0},{4,6},{6,4},{1,3},{3,1},{5,7},{7,5},{8,10},{10,8},{12,... | collective-permute-start | bytes 1032200 | tf_op jit(solution)/shard_map/ppermute | solution.py:78
  81.2 14.5 %collective-permute-start.25 = (bf16[56,3072]{1,0:T(8,128)(2,1)S(1)}, bf16[56,3072]{1,0:T(8,128)(2,1)S(1)}, u32[]{:S(2)}, u32[]{:S(2)}) collective-permute-start(bf16[56,3072]{1,0:T(8,128)(2,1)S(1)} %get-tuple-element.16), channel_id=1, source_target_pairs={{0,2},{2,0},{4,6},{6,4},{1,3},{3,1},{5,7},{7,5},{8,10},{10,8},{12,... | collective-permute-start | bytes 1032200 | tf_op jit(solution)/shard_map/ppermute | solution.py:78
  88.6 17.0 %collective-permute-start.17 = (bf16[56,3072]{1,0:T(8,128)(2,1)S(1)}, bf16[56,3072]{1,0:T(8,128)(2,1)S(1)}, u32[]{:S(2)}, u32[]{:S(2)}) collective-permute-start(bf16[56,3072]{1,0:T(8,128)(2,1)S(1)} %get-tuple-element.6), channel_id=1, source_target_pairs={{0,2},{2,0},{4,6},{6,4},{1,3},{3,1},{5,7},{7,5},{8,10},{10,8},{12,... | collective-permute-start | bytes 1032200 | tf_op jit(solution)/shard_map/ppermute | solution.py:78
  94.6 11.0 %collective-permute-start.21 = (bf16[56,3072]{1,0:T(8,128)(2,1)S(1)}, bf16[56,3072]{1,0:T(8,128)(2,1)S(1)}, u32[]{:S(2)}, u32[]{:S(2)}) collective-permute-start(bf16[56,3072]{1,0:T(8,128)(2,1)S(1)} %get-tuple-element.7), channel_id=1, source_target_pairs={{2,4},{4,2},{3,5},{5,3},{10,12},{12,10},{11,13},{13,11},{18,20},{2... | collective-permute-start | bytes 1032200 | tf_op jit(solution)/shard_map/ppermute | solution.py:78
  96.0 18.5 %collective-permute-start.26 = (bf16[56,3072]{1,0:T(8,128)(2,1)S(1)}, bf16[56,3072]{1,0:T(8,128)(2,1)S(1)}, u32[]{:S(2)}, u32[]{:S(2)}) collective-permute-start(bf16[56,3072]{1,0:T(8,128)(2,1)S(1)} %get-tuple-element.14), channel_id=1, source_target_pairs={{2,4},{4,2},{3,5},{5,3},{10,12},{12,10},{11,13},{13,11},{18,20},{2... | collective-permute-start | bytes 1032200 | tf_op jit(solution)/shard_map/ppermute | solution.py:78
  96.7 17.9 %collective-permute-start.30 = (bf16[56,3072]{1,0:T(8,128)(2,1)S(1)}, bf16[56,3072]{1,0:T(8,128)(2,1)S(1)}, u32[]{:S(2)}, u32[]{:S(2)}) collective-permute-start(bf16[56,3072]{1,0:T(8,128)(2,1)S(1)} %get-tuple-element.15), channel_id=1, source_target_pairs={{0,2},{2,0},{4,6},{6,4},{1,3},{3,1},{5,7},{7,5},{8,10},{10,8},{12,... | collective-permute-start | bytes 1032200 | tf_op jit(solution)/shard_map/ppermute | solution.py:78
  105.8 13.1 %collective-permute-start.18 = (bf16[56,3072]{1,0:T(8,128)(2,1)S(1)}, bf16[56,3072]{1,0:T(8,128)(2,1)S(1)}, u32[]{:S(2)}, u32[]{:S(2)}) collective-permute-start(bf16[56,3072]{1,0:T(8,128)(2,1)S(1)} %get-tuple-element.4), channel_id=1, source_target_pairs={{2,4},{4,2},{3,5},{5,3},{10,12},{12,10},{11,13},{13,11},{18,20},{2... | collective-permute-start | bytes 1032200 | tf_op jit(solution)/shard_map/ppermute | solution.py:78
  106.5 15.4 %collective-permute-start.22 = (bf16[56,3072]{1,0:T(8,128)(2,1)S(1)}, bf16[56,3072]{1,0:T(8,128)(2,1)S(1)}, u32[]{:S(2)}, u32[]{:S(2)}) collective-permute-start(bf16[56,3072]{1,0:T(8,128)(2,1)S(1)} %get-tuple-element.5), channel_id=1, source_target_pairs={{0,2},{2,0},{4,6},{6,4},{1,3},{3,1},{5,7},{7,5},{8,10},{10,8},{12,... | collective-permute-start | bytes 1032200 | tf_op jit(solution)/shard_map/ppermute | solution.py:78
  115.6 24.9 %collective-permute-start.27 = (bf16[56,3072]{1,0:T(8,128)(2,1)}, bf16[56,3072]{1,0:T(8,128)(2,1)}, u32[]{:S(2)}, u32[]{:S(2)}) collective-permute-start(bf16[56,3072]{1,0:T(8,128)(2,1)} %get-tuple-element.12), channel_id=1, source_target_pairs={{0,2},{2,0},{4,6},{6,4},{1,3},{3,1},{5,7},{7,5},{8,10},{10,8},{12,... | collective-permute-start | bytes 1032200 | tf_op jit(solution)/shard_map/ppermute | solution.py:78
  117.5 23.0 %collective-permute-start.31 = (bf16[56,3072]{1,0:T(8,128)(2,1)}, bf16[56,3072]{1,0:T(8,128)(2,1)}, u32[]{:S(2)}, u32[]{:S(2)}) collective-permute-start(bf16[56,3072]{1,0:T(8,128)(2,1)} %get-tuple-element.13), channel_id=1, source_target_pairs={{2,4},{4,2},{3,5},{5,3},{10,12},{12,10},{11,13},{13,11},{18,20},{2... | collective-permute-start | bytes 1032200 | tf_op jit(solution)/shard_map/ppermute | solution.py:78
  123.1 23.5 %collective-permute-start.19 = (bf16[56,3072]{1,0:T(8,128)(2,1)}, bf16[56,3072]{1,0:T(8,128)(2,1)}, u32[]{:S(2)}, u32[]{:S(2)}) collective-permute-start(bf16[56,3072]{1,0:T(8,128)(2,1)} %get-tuple-element.2), channel_id=1, source_target_pairs={{0,2},{2,0},{4,6},{6,4},{1,3},{3,1},{5,7},{7,5},{8,10},{10,8},{12,... | collective-permute-start | bytes 1032200 | tf_op jit(solution)/shard_map/ppermute | solution.py:78
  125.1 21.5 %collective-permute-start.23 = (bf16[56,3072]{1,0:T(8,128)(2,1)}, bf16[56,3072]{1,0:T(8,128)(2,1)}, u32[]{:S(2)}, u32[]{:S(2)}) collective-permute-start(bf16[56,3072]{1,0:T(8,128)(2,1)} %get-tuple-element.3), channel_id=1, source_target_pairs={{2,4},{4,2},{3,5},{5,3},{10,12},{12,10},{11,13},{13,11},{18,20},{2... | collective-permute-start | bytes 1032200 | tf_op jit(solution)/shard_map/ppermute | solution.py:78
  143.3 12.4 %collective-permute-start.41 = (bf16[56,3072]{1,0:T(8,128)(2,1)S(1)}, bf16[56,3072]{1,0:T(8,128)(2,1)}, u32[]{:S(2)}, u32[]{:S(2)}) collective-permute-start(bf16[56,3072]{1,0:T(8,128)(2,1)S(1)} %fusion.49), channel_id=1, source_target_pairs={{0,2},{2,0},{4,6},{6,4},{1,3},{3,1},{5,7},{7,5},{8,10},{10,8},{12,... | collective-permute-start | bytes 1032200 | tf_op jit(solution)/shard_map/ppermute | solution.py:78
  147.8 19.7 %collective-permute-start.37 = (bf16[56,3072]{1,0:T(8,128)(2,1)S(1)}, bf16[56,3072]{1,0:T(8,128)(2,1)}, u32[]{:S(2)}, u32[]{:S(2)}) collective-permute-start(bf16[56,3072]{1,0:T(8,128)(2,1)S(1)} %fusion.53), channel_id=1, source_target_pairs={{2,4},{4,2},{3,5},{5,3},{10,12},{12,10},{11,13},{13,11},{18,20},{2... | collective-permute-start | bytes 1032200 | tf_op jit(solution)/shard_map/ppermute | solution.py:78
  149.2 19.6 %collective-permute-start.36 = (bf16[56,3072]{1,0:T(8,128)(2,1)S(1)}, bf16[56,3072]{1,0:T(8,128)(2,1)}, u32[]{:S(2)}, u32[]{:S(2)}) collective-permute-start(bf16[56,3072]{1,0:T(8,128)(2,1)S(1)} %fusion.53), channel_id=1, source_target_pairs={{0,2},{2,0},{4,6},{6,4},{1,3},{3,1},{5,7},{7,5},{8,10},{10,8},{12,... | collective-permute-start | bytes 1032200 | tf_op jit(solution)/shard_map/ppermute | solution.py:78
  151.4 19.5 %collective-permute-start.45 = (bf16[56,3072]{1,0:T(8,128)(2,1)}, bf16[56,3072]{1,0:T(8,128)(2,1)}, u32[]{:S(2)}, u32[]{:S(2)}) collective-permute-start(bf16[56,3072]{1,0:T(8,128)(2,1)} %collective-permute-done.42), channel_id=1, source_target_pairs={{2,0},{4,6},{3,1},{5,7},{10,8},{12,14},{11,9},{13,15},{18,16},{20,... | collective-permute-start | bytes 1032200 | tf_op jit(solution)/shard_map/ppermute | solution.py:78
  155.7 13.9 %collective-permute-start.43 = (bf16[56,3072]{1,0:T(8,128)(2,1)}, bf16[56,3072]{1,0:T(8,128)(2,1)}, u32[]{:S(2)}, u32[]{:S(2)}) collective-permute-start(bf16[56,3072]{1,0:T(8,128)(2,1)} %collective-permute-done.41), channel_id=1, source_target_pairs={{2,4},{4,2},{3,5},{5,3},{10,12},{12,10},{11,13},{13,11},{18,20},{2... | collective-permute-start | bytes 1032200 | tf_op jit(solution)/shard_map/ppermute | solution.py:78
  167.6 13.2 %collective-permute-start.40 = (bf16[56,3072]{1,0:T(8,128)(2,1)}, bf16[56,3072]{1,0:T(8,128)(2,1)S(1)}, u32[]{:S(2)}, u32[]{:S(2)}) collective-permute-start(bf16[56,3072]{1,0:T(8,128)(2,1)} %collective-permute-done.37), channel_id=1, source_target_pairs={{2,0},{4,6},{3,1},{5,7},{10,8},{12,14},{11,9},{13,15},{18,16},{20,... | collective-permute-start | bytes 1032200 | tf_op jit(solution)/shard_map/ppermute | solution.py:78
  169.6 14.8 %collective-permute-start.44 = (bf16[56,3072]{1,0:T(8,128)(2,1)}, bf16[56,3072]{1,0:T(8,128)(2,1)S(1)}, u32[]{:S(2)}, u32[]{:S(2)}) collective-permute-start(bf16[56,3072]{1,0:T(8,128)(2,1)} %collective-permute-done.43), channel_id=1, source_target_pairs={{2,0},{4,6},{3,1},{5,7},{10,8},{12,14},{11,9},{13,15},{18,16},{20,... | collective-permute-start | bytes 1032200 | tf_op jit(solution)/shard_map/ppermute | solution.py:78
  172.0 25.1 %collective-permute-start.39 = (bf16[56,3072]{1,0:T(8,128)(2,1)S(1)}, bf16[56,3072]{1,0:T(8,128)(2,1)S(1)}, u32[]{:S(2)}, u32[]{:S(2)}) collective-permute-start(bf16[56,3072]{1,0:T(8,128)(2,1)S(1)} %collective-permute-done.38), channel_id=1, source_target_pairs={{2,0},{4,6},{3,1},{5,7},{10,8},{12,14},{11,9},{13,15},{18,16},{20,... | collective-permute-start | bytes 1032200 | tf_op jit(solution)/shard_map/ppermute | solution.py:78
  214.8 11.0 %collective-permute-start.33 = (bf16[2,56,576]{2,1,0:T(8,128)(2,1)S(1)}, bf16[2,56,576]{2,1,0:T(8,128)(2,1)S(1)}, u32[]{:S(2)}, u32[]{:S(2)}) collective-permute-start(bf16[2,56,576]{2,1,0:T(8,128)(2,1)S(1)} %get-tuple-element.34), channel_id=1, source_target_pairs={{0,8},{8,16},{16,24},{1,9},{9,17},{17,25},{2,10},{10,18},{18,26},{... | collective-permute-start | bytes 387080 | tf_op jit(solution)/shard_map/ppermute | solution.py:145
  (28 other events, 238.8 us)
where the time goes:
time: 235 us; the launch traced here: 233 us
  starting transfers between devices  114 us (49%)
  matrix products  51.3 us (22%)
  waiting for transfers between devices  42.2 us (18%)
  other arithmetic  19 us (8%)
  blocking collectives  2.47 us (1%)
  local copies, waits for them, and re-layouts  2.4 us (1%)
    ppermute x36, starting transfers between devices, swap(): return lax.ppermute(value, 'feat', pairs) if pairs else None  88 us
    dot_general x4, matrix products, decode(): jnp.einsum('nf,ldf->lnd', all_codes, decoders[:, :, chunk * width:(chunk...  44.1 us
    ppermute x36, waiting for transfers between devices, swap(): return lax.ppermute(value, 'feat', pairs) if pairs else None  33.3 us
    ppermute x6, starting transfers between devices, exchanged(): lax.ppermute(part, 'feat', [(i, (i + k) % ring) for i in range(ring)])  13.2 us
    ppermute x6, starting transfers between devices, residual_rows(): lax.ppermute(sent, 'segment', [(i, i + k) for i in range(segments - k)])  12 us
    select_n x8, other arithmetic, advance(): codes.append(jnp.where(m <= z, left, right))  9.42 us
    dot_general x4, matrix products, partial_sums(): jnp.dot(columns[group], weight[:, chunk * width:(chunk + 1) * width], pre...  7.13 us
  transfers between devices with their start and end apart: 50, of which 15 were waited for; matrix products, arithmetic and copies ran while one was open for 24% of the time, Pallas kernels for 0%

commit v1 on v0

--- a/solution.py
+++ b/solution.py
@@ -46,17 +46,43 @@
     units = [(group, chunk) for group in range(GROUPS) for chunk in range(CHUNKS)]
     finished = {}
     decoded = {}
+    waiting = []
+    ordered = [None]
+    left = {group: CHUNKS * layers for group in range(GROUPS)}
+    totals = {}
+    residuals = {}
+
+    def after(values, others):
+        others = [x for x in jax.tree.leaves(others) if x is not None]
+        return lax.optimization_barrier((values, others))[0] if others else values
+
+    def background(sent):
+        if waiting:
+            ordered[0] = waiting.pop(0)(sent)
 
     def decode(unit, codes):
         group, chunk = unit
-        all_codes = jnp.concatenate(codes, axis=0)
-        out = jnp.einsum(
-            "nf,ldf->lnd",
-            all_codes,
-            decoders[:, :, chunk * width : (chunk + 1) * width],
-            preferred_element_type=F32,
-        )
-        decoded[group] = out if group not in decoded else decoded[group] + out
+
+        def piece(layer):
+            def run(sent):
+                all_codes = after(codes_of[0], sent)
+                out = lax.dot_general(
+                    all_codes,
+                    decoders[layer, :, chunk * width : (chunk + 1) * width],
+                    (((1,), (1,)), ((), ())),
+                    preferred_element_type=F32,
+                )
+                key = group, layer
+                decoded[key] = out if key not in decoded else decoded[key] + out
+                left[group] -= 1
+                if not left[group]:
+                    waiting.extend([lambda sent: share_cores(group, sent), lambda sent: share_segments(group, sent)])
+                return decoded[key]
+
+            return run
+
+        codes_of = [jnp.concatenate(codes, axis=0)]
+        waiting.extend(piece(layer) for layer in reversed(range(layers)))
 
     class Stream:
         def __init__(self, own):
@@ -85,6 +111,8 @@
                     sent.append(finished[self.own[i - 1]])
                     continue
                 value = self.got[1 - side].get(k - 1)
+                if value is not None:
+                    value = after(value, ordered)
                 if i < n:
                     rightward = odd == (side == 1)
                     own = jnp.where(
@@ -98,6 +126,7 @@
                 got = self.swap(sent[side], side) if sent[side] is not None else None
                 if got is not None:
                     self.got[side][k] = got
+            background(sent)
             if i and k == ring - 2:
                 unit = self.own[i - 1]
                 codes = [finished[unit]]
@@ -121,8 +150,9 @@
                 return True
             return not (i == n and k == ring - 2)
 
-    def residual_rows(group):
-        blocks = decoded[group].reshape(layers, ring, rows, depth)
+    def share_cores(group, sent):
+        blocks = after([decoded[group, layer] for layer in range(layers)], sent)
+        blocks = jnp.stack(blocks).reshape(layers, ring, rows, depth)
 
         def share(index):
             first = index * per_core
@@ -135,15 +165,25 @@
             )
 
         total = share(core)
+        given = []
         for k in range(1, cores):
-            sent = share((core + k) % cores).astype(BF16)
-            total += lax.ppermute(sent, "tok", [(i, (i + k) % cores) for i in range(cores)]).astype(F32)
+            given.append(share((core + k) % cores).astype(BF16))
+            got = lax.ppermute(given[-1], "tok", [(i, (i + k) % cores) for i in range(cores)])
+            total += got.astype(F32)
+        totals[group] = total
+        return given
+
+    def share_segments(group, sent):
+        total = after(totals[group], sent)
         own = lax.dynamic_index_in_dim(total, segment, axis=0, keepdims=False)
+        given = []
         for k in range(1, segments):
             place = jnp.minimum(segment + k, layers - 1)
-            sent = lax.dynamic_index_in_dim(total, place, axis=0, keepdims=False).astype(BF16)
-            own += lax.ppermute(sent, "segment", [(i, i + k) for i in range(segments - k)]).astype(F32)
-        return own
+            given.append(lax.dynamic_index_in_dim(total, place, axis=0, keepdims=False).astype(BF16))
+            got = lax.ppermute(given[-1], "segment", [(i, i + k) for i in range(segments - k)])
+            own += got.astype(F32)
+        residuals[group] = own
+        return given
 
     streams = [Stream(units[i::STREAMS]) for i in range(STREAMS)]
     going = [True] * STREAMS
@@ -151,7 +191,9 @@
         for i, stream in enumerate(streams):
             if going[i]:
                 going[i] = stream.advance()
-    own = jnp.stack([residual_rows(group) for group in range(GROUPS)], axis=1)
+    while waiting:
+        background(None)
+    own = jnp.stack([residuals[group] for group in range(GROUPS)], axis=1)
     residual = targets[0].astype(F32) - own.reshape(targets.shape[1:])
     features = jnp.concatenate(
         [

time: 235 us -> 219 us (0.932)
  matrix products: 51.3 us -> 30.2 us
  waiting for transfers between devices: 42.2 us -> 56.3 us
  other arithmetic: 19 us -> 6.88 us
  starting transfers between devices: 114 us -> 119 us
    dot_general x4 -> x16, matrix products: 44.1 us -> 23.1 us  [run(): lax.dot_general(all_codes, decoders[layer, :, chunk * width:(chunk + 1) *...]
    ppermute x36, waiting for transfers between devices: 33.3 us -> 51.4 us  [swap(): return lax.ppermute(value, 'feat', pairs) if pairs else None]
    select_n x8, other arithmetic: 9.42 us -> 0.59 us  [advance(): codes.append(jnp.where(m <= z, left, right))]
    ppermute x36, starting transfers between devices: 88 us -> 95.6 us  [swap(): return lax.ppermute(value, 'feat', pairs) if pairs else None]
    ppermute x6, waiting for transfers between devices: 4.52 us -> 0.02 us  [exchanged(): lax.ppermute(part, 'feat', [(i, (i + k) % ring) for i in range(ring)])]
  transfers between devices with their start and end apart: 50 -> 50, of which waited for: 15 -> 17; matrix products, arithmetic and copies ran while one was open for 24% -> 11% of each run, Pallas kernels for 0% -> 0%
where the time goes in v1:
time: 219 us; the launch traced here: 218 us
  starting transfers between devices  119 us (54%)
  waiting for transfers between devices  56.3 us (26%)
  matrix products  30.2 us (14%)
  other arithmetic  6.88 us (3%)
  blocking collectives  2.47 us (1%)
    ppermute x36, starting transfers between devices, swap(): return lax.ppermute(value, 'feat', pairs) if pairs else None  95.6 us
    ppermute x36, waiting for transfers between devices, swap(): return lax.ppermute(value, 'feat', pairs) if pairs else None  51.4 us
    dot_general x16, matrix products, run(): lax.dot_general(all_codes, decoders[layer, :, chunk * width:(chunk + 1) *...  23.1 us
    ppermute x6, starting transfers between devices, share_segments(): lax.ppermute(given[-1], 'segment', [(i, i + k) for i in range(segments -...  12 us
    ppermute x6, starting transfers between devices, exchanged(): lax.ppermute(part, 'feat', [(i, (i + k) % ring) for i in range(ring)])  11 us
    dot_general x4, matrix products, partial_sums(): jnp.dot(columns[group], weight[:, chunk * width:(chunk + 1) * width], pre...  7.15 us
    ppermute x6, waiting for transfers between devices, share_segments(): lax.ppermute(given[-1], 'segment', [(i, i + k) for i in range(segments -...  4.87 us
  transfers between devices with their start and end apart: 50, of which 17 were waited for; matrix products, arithmetic and copies ran while one was open for 11% of the time, Pallas kernels for 0%

profile of v1, /device:TPU:0, one launch (start us, length us, event | category | flops | bytes accessed | tf_op | source)
XLA Modules:
  0.0 217.8 jit_solution(15549837832368465669)
XLA Ops:
  0.7 2.5 %all-gather = bf16[1,112,2304]{2,1,0:T(8,128)(2,1)S(1)} all-gather(bf16[1,112,1152]{2,1,0:T(8,128)(2,1)} %param.5), channel_id=2, replica_groups=mesh['segment'=4,'feat'=4,'tok'=2] {'tok'}, dimensions={2}, use_global_device_ids=true | all-gather | bytes 774144 | tf_op jit(solution)/shard_map/all_gather | solution.py:26
  3.4 3.0 %collective-permute-start = (bf16[56,576]{1,0:T(8,128)(2,1)S(1)}, bf16[56,576]{1,0:T(8,128)(2,1)S(1)}, u32[]{:S(2)}, u32[]{:S(2)}) collective-permute-start(bf16[56,576]{1,0:T(8,128)(2,1)S(1)} %get-tuple-element.90), channel_id=1, source_target_pairs={{0,2},{2,4},{4,6},{6,0},{1,3},{3,5},{5,7},{7,1},{8,10},{10,12},{12... | collective-permute-start | bytes 193544 | tf_op jit(solution)/shard_map/ppermute | solution.py:34
  6.4 2.6 %collective-permute-start.1 = (bf16[56,576]{1,0:T(8,128)(2,1)S(1)}, bf16[56,576]{1,0:T(8,128)(2,1)S(1)}, u32[]{:S(2)}, u32[]{:S(2)}) collective-permute-start(bf16[56,576]{1,0:T(8,128)(2,1)S(1)} %get-tuple-element.89), channel_id=1, source_target_pairs={{0,4},{2,6},{4,0},{6,2},{1,5},{3,7},{5,1},{7,3},{8,12},{10,14},{12... | collective-permute-start | bytes 193544 | tf_op jit(solution)/shard_map/ppermute | solution.py:34
  11.6 3.0 %collective-permute-start.15 = (bf16[56,576]{1,0:T(8,128)(2,1)S(1)}, bf16[56,576]{1,0:T(8,128)(2,1)S(1)}, u32[]{:S(2)}, u32[]{:S(2)}) collective-permute-start(bf16[56,576]{1,0:T(8,128)(2,1)S(1)} %get-tuple-element.95), channel_id=1, source_target_pairs={{0,6},{2,0},{4,2},{6,4},{1,7},{3,1},{5,3},{7,5},{8,14},{10,8},{12,... | collective-permute-start | bytes 193544 | tf_op jit(solution)/shard_map/ppermute | solution.py:34
  14.6 3.4 %fusion.18 = f32[224,3072]{1,0:T(8,128)S(1)} fusion(bf16[576,6144]{1,0:T(8,128)(2,1)} %bitcast.150, bf16[56,576]{1,0:T(8,128)(2,1)S(1)} %collective-permute-done.2, bf16[56,576]{1,0:T(8,128)(2,1)S(1)} %collective-permute-done.1, bf16[56,576]{1,0:T(8,128)(2,1)S(1)} %collective-permute-done, bf16[56,576]{1,0:T(8,128)(2,1)S(1)} %get-tuple-element.88), kind=kOutput, calls=%fused_computation.26 | convolution fusion | flops 793755648 | bytes 6549504 | tf_op jit(solution)/shard_map/dot_general | solution.py:41
  18.2 6.6 %collective-permute-start.8 = (bf16[56,3072]{1,0:T(8,128)(2,1)S(1)}, bf16[56,3072]{1,0:T(8,128)(2,1)S(1)}, u32[]{:S(2)}, u32[]{:S(2)}) collective-permute-start(bf16[56,3072]{1,0:T(8,128)(2,1)S(1)} %get-tuple-element.62), channel_id=1, source_target_pairs={{0,2},{6,4},{1,3},{7,5},{8,10},{14,12},{9,11},{15,13},{16,18},{22,... | collective-permute-start | bytes 1032200 | tf_op jit(solution)/shard_map/ppermute | solution.py:104
  34.0 13.9 %collective-permute-done.3 = bf16[56,3072]{1,0:T(8,128)(2,1)S(1)} collective-permute-done((bf16[56,3072]{1,0:T(8,128)(2,1)S(1)}, bf16[56,3072]{1,0:T(8,128)(2,1)S(1)}, u32[]{:S(2)}, u32[]{:S(2)}) %collective-permute-start.3) | collective-permute-done | bytes 344096 | tf_op jit(solution)/shard_map/ppermute | solution.py:104
  49.0 3.8 %collective-permute-start.10 = (bf16[56,3072]{1,0:T(8,128)(2,1)S(1)}, bf16[56,3072]{1,0:T(8,128)(2,1)S(1)}, u32[]{:S(2)}, u32[]{:S(2)}) collective-permute-start(bf16[56,3072]{1,0:T(8,128)(2,1)S(1)} %get-tuple-element.60), channel_id=1, source_target_pairs={{0,2},{2,0},{4,6},{6,4},{1,3},{3,1},{5,7},{7,5},{8,10},{10,8},{12,... | collective-permute-start | bytes 1032200 | tf_op jit(solution)/shard_map/ppermute | solution.py:104
  55.6 8.2 %collective-permute-start.5 = (bf16[56,3072]{1,0:T(8,128)(2,1)S(1)}, bf16[56,3072]{1,0:T(8,128)(2,1)S(1)}, u32[]{:S(2)}, u32[]{:S(2)}) collective-permute-start(bf16[56,3072]{1,0:T(8,128)(2,1)S(1)} %get-tuple-element.56), channel_id=1, source_target_pairs={{0,2},{2,0},{4,6},{6,4},{1,3},{3,1},{5,7},{7,5},{8,10},{10,8},{12,... | collective-permute-start | bytes 1032200 | tf_op jit(solution)/shard_map/ppermute | solution.py:104
  65.3 7.7 %collective-permute-start.22 = (bf16[56,3072]{1,0:T(8,128)(2,1)S(1)}, bf16[56,3072]{1,0:T(8,128)(2,1)S(1)}, u32[]{:S(2)}, u32[]{:S(2)}) collective-permute-start(bf16[56,3072]{1,0:T(8,128)(2,1)S(1)} %fusion.43), channel_id=1, source_target_pairs={{0,2},{2,0},{4,6},{6,4},{1,3},{3,1},{5,7},{7,5},{8,10},{10,8},{12,... | collective-permute-start | bytes 1032200 | tf_op jit(solution)/shard_map/ppermute | solution.py:104
  73.9 6.5 %collective-permute-start.19 = (bf16[56,3072]{1,0:T(8,128)(2,1)S(1)}, bf16[56,3072]{1,0:T(8,128)(2,1)S(1)}, u32[]{:S(2)}, u32[]{:S(2)}) collective-permute-start(bf16[56,3072]{1,0:T(8,128)(2,1)S(1)} %fusion.47), channel_id=1, source_target_pairs={{0,2},{2,0},{4,6},{6,4},{1,3},{3,1},{5,7},{7,5},{8,10},{10,8},{12,... | collective-permute-start | bytes 1032200 | tf_op jit(solution)/shard_map/ppermute | solution.py:104
  80.5 5.3 %collective-permute-start.25 = (bf16[56,3072]{1,0:T(8,128)(2,1)S(1)}, bf16[56,3072]{1,0:T(8,128)(2,1)S(1)}, u32[]{:S(2)}, u32[]{:S(2)}) collective-permute-start(bf16[56,3072]{1,0:T(8,128)(2,1)S(1)} %add_convert_fusion.5), channel_id=1, source_target_pairs={{0,2},{2,0},{4,6},{6,4},{1,3},{3,1},{5,7},{7,5},{8,10},{10,8},{12,... | collective-permute-start | bytes 1032200 | tf_op jit(solution)/shard_map/ppermute | solution.py:104
  85.8 3.6 %collective-permute-done.19 = bf16[56,3072]{1,0:T(8,128)(2,1)S(1)} collective-permute-done((bf16[56,3072]{1,0:T(8,128)(2,1)S(1)}, bf16[56,3072]{1,0:T(8,128)(2,1)S(1)}, u32[]{:S(2)}, u32[]{:S(2)}) %collective-permute-start.19) | collective-permute-done | bytes 344096 | tf_op jit(solution)/shard_map/ppermute | solution.py:104
  89.6 2.1 collective-permute-start.17
  92.4 4.3 %collective-permute-done.25 = bf16[56,3072]{1,0:T(8,128)(2,1)S(1)} collective-permute-done((bf16[56,3072]{1,0:T(8,128)(2,1)S(1)}, bf16[56,3072]{1,0:T(8,128)(2,1)S(1)}, u32[]{:S(2)}, u32[]{:S(2)}) %collective-permute-start.25) | collective-permute-done | bytes 344096 | tf_op jit(solution)/shard_map/ppermute | solution.py:104
  98.5 1.9 collective-permute-done.17
  101.3 8.1 %collective-permute-start.21 = (bf16[56,3072]{1,0:T(8,128)(2,1)S(1)}, bf16[56,3072]{1,0:T(8,128)(2,1)S(1)}, u32[]{:S(2)}, u32[]{:S(2)}) collective-permute-start(bf16[56,3072]{1,0:T(8,128)(2,1)S(1)} %get-tuple-element.53), channel_id=1, source_target_pairs={{0,2},{2,0},{4,6},{6,4},{1,3},{3,1},{5,7},{7,5},{8,10},{10,8},{12,... | collective-permute-start | bytes 1032200 | tf_op jit(solution)/shard_map/ppermute | solution.py:104
  109.5 2.5 %collective-permute-start.30 = (bf16[56,3072]{1,0:T(8,128)(2,1)S(1)}, bf16[56,3072]{1,0:T(8,128)(2,1)S(1)}, u32[]{:S(2)}, u32[]{:S(2)}) collective-permute-start(bf16[56,3072]{1,0:T(8,128)(2,1)S(1)} %add_convert_fusion.6), channel_id=1, source_target_pairs={{0,2},{2,0},{4,6},{6,4},{1,3},{3,1},{5,7},{7,5},{8,10},{10,8},{12,... | collective-permute-start | bytes 1032200 | tf_op jit(solution)/shard_map/ppermute | solution.py:104
  112.1 2.5 %collective-permute-done.21 = bf16[56,3072]{1,0:T(8,128)(2,1)S(1)} collective-permute-done((bf16[56,3072]{1,0:T(8,128)(2,1)S(1)}, bf16[56,3072]{1,0:T(8,128)(2,1)S(1)}, u32[]{:S(2)}, u32[]{:S(2)}) %collective-permute-start.21) | collective-permute-done | bytes 344096 | tf_op jit(solution)/shard_map/ppermute | solution.py:104
  116.6 7.7 %collective-permute-start.26 = (bf16[56,3072]{1,0:T(8,128)(2,1)S(1)}, bf16[56,3072]{1,0:T(8,128)(2,1)S(1)}, u32[]{:S(2)}, u32[]{:S(2)}) collective-permute-start(bf16[56,3072]{1,0:T(8,128)(2,1)S(1)} %get-tuple-element.49), channel_id=1, source_target_pairs={{0,2},{2,0},{4,6},{6,4},{1,3},{3,1},{5,7},{7,5},{8,10},{10,8},{12,... | collective-permute-start | bytes 1032200 | tf_op jit(solution)/shard_map/ppermute | solution.py:104
  126.6 2.9 %collective-permute-done.26 = bf16[56,3072]{1,0:T(8,128)(2,1)S(1)} collective-permute-done((bf16[56,3072]{1,0:T(8,128)(2,1)S(1)}, bf16[56,3072]{1,0:T(8,128)(2,1)S(1)}, u32[]{:S(2)}, u32[]{:S(2)}) %collective-permute-start.26) | collective-permute-done | bytes 344096 | tf_op jit(solution)/shard_map/ppermute | solution.py:104
  129.7 4.3 %collective-permute-start.32 = (bf16[56,3072]{1,0:T(8,128)(2,1)S(1)}, bf16[56,3072]{1,0:T(8,128)(2,1)S(1)}, u32[]{:S(2)}, u32[]{:S(2)}) collective-permute-start(bf16[56,3072]{1,0:T(8,128)(2,1)S(1)} %fusion.39), channel_id=1, source_target_pairs={{0,2},{2,0},{4,6},{6,4},{1,3},{3,1},{5,7},{7,5},{8,10},{10,8},{12,... | collective-permute-start | bytes 1032200 | tf_op jit(solution)/shard_map/ppermute | solution.py:104
  134.9 3.4 %collective-permute-start.29 = (bf16[56,3072]{1,0:T(8,128)(2,1)S(1)}, bf16[56,3072]{1,0:T(8,128)(2,1)S(1)}, u32[]{:S(2)}, u32[]{:S(2)}) collective-permute-start(bf16[56,3072]{1,0:T(8,128)(2,1)S(1)} %get-tuple-element.46), channel_id=1, source_target_pairs={{0,2},{2,0},{4,6},{6,4},{1,3},{3,1},{5,7},{7,5},{8,10},{10,8},{12,... | collective-permute-start | bytes 1032200 | tf_op jit(solution)/shard_map/ppermute | solution.py:104
  142.0 2.2 %collective-permute-done.29 = bf16[56,3072]{1,0:T(8,128)(2,1)S(1)} collective-permute-done((bf16[56,3072]{1,0:T(8,128)(2,1)S(1)}, bf16[56,3072]{1,0:T(8,128)(2,1)S(1)}, u32[]{:S(2)}, u32[]{:S(2)}) %collective-permute-start.29) | collective-permute-done | bytes 344096 | tf_op jit(solution)/shard_map/ppermute | solution.py:104
  145.1 8.5 %collective-permute-start.36 = (bf16[56,3072]{1,0:T(8,128)(2,1)S(1)}, bf16[56,3072]{1,0:T(8,128)(2,1)S(1)}, u32[]{:S(2)}, u32[]{:S(2)}) collective-permute-start(bf16[56,3072]{1,0:T(8,128)(2,1)S(1)} %fusion.35), channel_id=1, source_target_pairs={{0,2},{2,0},{4,6},{6,4},{1,3},{3,1},{5,7},{7,5},{8,10},{10,8},{12,... | collective-permute-start | bytes 1032200 | tf_op jit(solution)/shard_map/ppermute | solution.py:104
  158.6 2.6 %collective-permute-done.36 = bf16[56,3072]{1,0:T(8,128)(2,1)S(1)} collective-permute-done((bf16[56,3072]{1,0:T(8,128)(2,1)S(1)}, bf16[56,3072]{1,0:T(8,128)(2,1)S(1)}, u32[]{:S(2)}, u32[]{:S(2)}) %collective-permute-start.36) | collective-permute-done | bytes 344096 | tf_op jit(solution)/shard_map/ppermute | solution.py:104
  165.9 2.8 %collective-permute-done.43 = bf16[56,3072]{1,0:T(8,128)(2,1)S(1)} collective-permute-done((bf16[56,3072]{1,0:T(8,128)(2,1)S(1)}, bf16[56,3072]{1,0:T(8,128)(2,1)S(1)}, u32[]{:S(2)}, u32[]{:S(2)}) %collective-permute-start.43) | collective-permute-done | bytes 344096 | tf_op jit(solution)/shard_map/ppermute | solution.py:104
  171.7 9.6 %collective-permute-done.42 = bf16[56,3072]{1,0:T(8,128)(2,1)S(1)} collective-permute-done((bf16[56,3072]{1,0:T(8,128)(2,1)S(1)}, bf16[56,3072]{1,0:T(8,128)(2,1)S(1)}, u32[]{:S(2)}, u32[]{:S(2)}) %collective-permute-start.42) | collective-permute-done | bytes 344096 | tf_op jit(solution)/shard_map/ppermute | solution.py:104
  181.7 3.3 %collective-permute-done.44 = bf16[56,3072]{1,0:T(8,128)(2,1)S(1)} collective-permute-done((bf16[56,3072]{1,0:T(8,128)(2,1)S(1)}, bf16[56,3072]{1,0:T(8,128)(2,1)S(1)}, u32[]{:S(2)}, u32[]{:S(2)}) %collective-permute-start.44) | collective-permute-done | bytes 344096 | tf_op jit(solution)/shard_map/ppermute | solution.py:104
  199.5 3.4 %collective-permute-start.39 = (bf16[2,56,576]{2,1,0:T(8,128)(2,1)S(1)}, bf16[2,56,576]{2,1,0:T(8,128)(2,1)S(1)}, u32[]{:S(2)}, u32[]{:S(2)}) collective-permute-start(bf16[2,56,576]{2,1,0:T(8,128)(2,1)S(1)} %get-tuple-element.76), channel_id=1, source_target_pairs={{0,8},{8,16},{16,24},{1,9},{9,17},{17,25},{2,10},{10,18},{18,26},{... | collective-permute-start | bytes 387080 | tf_op jit(solution)/shard_map/ppermute | solution.py:183
  203.0 3.4 %collective-permute-start.40 = (bf16[2,56,576]{2,1,0:T(8,128)(2,1)S(1)}, bf16[2,56,576]{2,1,0:T(8,128)(2,1)S(1)}, u32[]{:S(2)}, u32[]{:S(2)}) collective-permute-start(bf16[2,56,576]{2,1,0:T(8,128)(2,1)S(1)} %get-tuple-element.78), channel_id=1, source_target_pairs={{0,16},{8,24},{1,17},{9,25},{2,18},{10,26},{3,19},{11,27},{4,20},{... | collective-permute-start | bytes 387080 | tf_op jit(solution)/shard_map/ppermute | solution.py:183
  211.8 1.8 collective-permute-done.40
  (158 shorter events, 68.9 us)
Async XLA Ops:
  10.5 17.1 %collective-permute-start.13 = (bf16[56,576]{1,0:T(8,128)(2,1)S(1)}, bf16[56,576]{1,0:T(8,128)(2,1)S(1)}, u32[]{:S(2)}, u32[]{:S(2)}) collective-permute-start(bf16[56,576]{1,0:T(8,128)(2,1)S(1)} %get-tuple-element.94), channel_id=1, source_target_pairs={{0,2},{2,4},{4,6},{6,0},{1,3},{3,5},{5,7},{7,1},{8,10},{10,12},{12... | collective-permute-start | bytes 193544 | tf_op jit(solution)/shard_map/ppermute | solution.py:34
  11.2 18.0 %collective-permute-start.14 = (bf16[56,576]{1,0:T(8,128)(2,1)S(1)}, bf16[56,576]{1,0:T(8,128)(2,1)S(1)}, u32[]{:S(2)}, u32[]{:S(2)}) collective-permute-start(bf16[56,576]{1,0:T(8,128)(2,1)S(1)} %get-tuple-element.93), channel_id=1, source_target_pairs={{0,4},{2,6},{4,0},{6,2},{1,5},{3,7},{5,1},{7,3},{8,12},{10,14},{12... | collective-permute-start | bytes 193544 | tf_op jit(solution)/shard_map/ppermute | solution.py:34
  11.6 19.0 %collective-permute-start.15 = (bf16[56,576]{1,0:T(8,128)(2,1)S(1)}, bf16[56,576]{1,0:T(8,128)(2,1)S(1)}, u32[]{:S(2)}, u32[]{:S(2)}) collective-permute-start(bf16[56,576]{1,0:T(8,128)(2,1)S(1)} %get-tuple-element.95), channel_id=1, source_target_pairs={{0,6},{2,0},{4,2},{6,4},{1,7},{3,1},{5,3},{7,5},{8,14},{10,8},{12,... | collective-permute-start | bytes 193544 | tf_op jit(solution)/shard_map/ppermute | solution.py:34
  18.2 15.0 %collective-permute-start.8 = (bf16[56,3072]{1,0:T(8,128)(2,1)S(1)}, bf16[56,3072]{1,0:T(8,128)(2,1)S(1)}, u32[]{:S(2)}, u32[]{:S(2)}) collective-permute-start(bf16[56,3072]{1,0:T(8,128)(2,1)S(1)} %get-tuple-element.62), channel_id=1, source_target_pairs={{0,2},{6,4},{1,3},{7,5},{8,10},{14,12},{9,11},{15,13},{16,18},{22,... | collective-permute-start | bytes 1032200 | tf_op jit(solution)/shard_map/ppermute | solution.py:104
  24.8 24.0 %collective-permute-start.11 = (bf16[56,3072]{1,0:T(8,128)(2,1)S(1)}, bf16[56,3072]{1,0:T(8,128)(2,1)S(1)}, u32[]{:S(2)}, u32[]{:S(2)}) collective-permute-start(bf16[56,3072]{1,0:T(8,128)(2,1)S(1)} %get-tuple-element.63), channel_id=1, source_target_pairs={{0,2},{6,4},{1,3},{7,5},{8,10},{14,12},{9,11},{15,13},{16,18},{22,... | collective-permute-start | bytes 1032200 | tf_op jit(solution)/shard_map/ppermute | solution.py:104
  27.6 20.4 %collective-permute-start.3 = (bf16[56,3072]{1,0:T(8,128)(2,1)S(1)}, bf16[56,3072]{1,0:T(8,128)(2,1)S(1)}, u32[]{:S(2)}, u32[]{:S(2)}) collective-permute-start(bf16[56,3072]{1,0:T(8,128)(2,1)S(1)} %get-tuple-element.58), channel_id=1, source_target_pairs={{0,2},{6,4},{1,3},{7,5},{8,10},{14,12},{9,11},{15,13},{16,18},{22,... | collective-permute-start | bytes 1032200 | tf_op jit(solution)/shard_map/ppermute | solution.py:104
  29.3 26.1 %collective-permute-start.6 = (bf16[56,3072]{1,0:T(8,128)(2,1)S(1)}, bf16[56,3072]{1,0:T(8,128)(2,1)S(1)}, u32[]{:S(2)}, u32[]{:S(2)}) collective-permute-start(bf16[56,3072]{1,0:T(8,128)(2,1)S(1)} %get-tuple-element.59), channel_id=1, source_target_pairs={{0,2},{6,4},{1,3},{7,5},{8,10},{14,12},{9,11},{15,13},{16,18},{22,... | collective-permute-start | bytes 1032200 | tf_op jit(solution)/shard_map/ppermute | solution.py:104
  33.4 15.5 %collective-permute-start.9 = (bf16[56,3072]{1,0:T(8,128)(2,1)S(1)}, bf16[56,3072]{1,0:T(8,128)(2,1)S(1)}, u32[]{:S(2)}, u32[]{:S(2)}) collective-permute-start(bf16[56,3072]{1,0:T(8,128)(2,1)S(1)} %add_convert_fusion.14), channel_id=1, source_target_pairs={{2,4},{4,2},{3,5},{5,3},{10,12},{12,10},{11,13},{13,11},{18,20},{2... | collective-permute-start | bytes 1032200 | tf_op jit(solution)/shard_map/ppermute | solution.py:104
  49.0 15.4 %collective-permute-start.10 = (bf16[56,3072]{1,0:T(8,128)(2,1)S(1)}, bf16[56,3072]{1,0:T(8,128)(2,1)S(1)}, u32[]{:S(2)}, u32[]{:S(2)}) collective-permute-start(bf16[56,3072]{1,0:T(8,128)(2,1)S(1)} %get-tuple-element.60), channel_id=1, source_target_pairs={{0,2},{2,0},{4,6},{6,4},{1,3},{3,1},{5,7},{7,5},{8,10},{10,8},{12,... | collective-permute-start | bytes 1032200 | tf_op jit(solution)/shard_map/ppermute | solution.py:104
  52.8 11.6 %collective-permute-start.12 = (bf16[56,3072]{1,0:T(8,128)(2,1)S(1)}, bf16[56,3072]{1,0:T(8,128)(2,1)S(1)}, u32[]{:S(2)}, u32[]{:S(2)}) collective-permute-start(bf16[56,3072]{1,0:T(8,128)(2,1)S(1)} %get-tuple-element.61), channel_id=1, source_target_pairs={{2,4},{4,2},{3,5},{5,3},{10,12},{12,10},{11,13},{13,11},{18,20},{2... | collective-permute-start | bytes 1032200 | tf_op jit(solution)/shard_map/ppermute | solution.py:104
  55.6 17.4 %collective-permute-start.5 = (bf16[56,3072]{1,0:T(8,128)(2,1)S(1)}, bf16[56,3072]{1,0:T(8,128)(2,1)S(1)}, u32[]{:S(2)}, u32[]{:S(2)}) collective-permute-start(bf16[56,3072]{1,0:T(8,128)(2,1)S(1)} %get-tuple-element.56), channel_id=1, source_target_pairs={{0,2},{2,0},{4,6},{6,4},{1,3},{3,1},{5,7},{7,5},{8,10},{10,8},{12,... | collective-permute-start | bytes 1032200 | tf_op jit(solution)/shard_map/ppermute | solution.py:104
  64.6 15.8 %collective-permute-start.24 = (bf16[56,3072]{1,0:T(8,128)(2,1)S(1)}, bf16[56,3072]{1,0:T(8,128)(2,1)S(1)}, u32[]{:S(2)}, u32[]{:S(2)}) collective-permute-start(bf16[56,3072]{1,0:T(8,128)(2,1)S(1)} %fusion.43), channel_id=1, source_target_pairs={{2,4},{4,2},{3,5},{5,3},{10,12},{12,10},{11,13},{13,11},{18,20},{2... | collective-permute-start | bytes 1032200 | tf_op jit(solution)/shard_map/ppermute | solution.py:104
  65.3 27.0 %collective-permute-start.22 = (bf16[56,3072]{1,0:T(8,128)(2,1)S(1)}, bf16[56,3072]{1,0:T(8,128)(2,1)S(1)}, u32[]{:S(2)}, u32[]{:S(2)}) collective-permute-start(bf16[56,3072]{1,0:T(8,128)(2,1)S(1)} %fusion.43), channel_id=1, source_target_pairs={{0,2},{2,0},{4,6},{6,4},{1,3},{3,1},{5,7},{7,5},{8,10},{10,8},{12,... | collective-permute-start | bytes 1032200 | tf_op jit(solution)/shard_map/ppermute | solution.py:104
  73.2 12.6 %collective-permute-start.16 = (bf16[56,3072]{1,0:T(8,128)(2,1)S(1)}, bf16[56,3072]{1,0:T(8,128)(2,1)S(1)}, u32[]{:S(2)}, u32[]{:S(2)}) collective-permute-start(bf16[56,3072]{1,0:T(8,128)(2,1)S(1)} %fusion.47), channel_id=1, source_target_pairs={{2,4},{4,2},{3,5},{5,3},{10,12},{12,10},{11,13},{13,11},{18,20},{2... | collective-permute-start | bytes 1032200 | tf_op jit(solution)/shard_map/ppermute | solution.py:104
  73.9 15.5 %collective-permute-start.19 = (bf16[56,3072]{1,0:T(8,128)(2,1)S(1)}, bf16[56,3072]{1,0:T(8,128)(2,1)S(1)}, u32[]{:S(2)}, u32[]{:S(2)}) collective-permute-start(bf16[56,3072]{1,0:T(8,128)(2,1)S(1)} %fusion.47), channel_id=1, source_target_pairs={{0,2},{2,0},{4,6},{6,4},{1,3},{3,1},{5,7},{7,5},{8,10},{10,8},{12,... | collective-permute-start | bytes 1032200 | tf_op jit(solution)/shard_map/ppermute | solution.py:104
  80.5 16.1 %collective-permute-start.25 = (bf16[56,3072]{1,0:T(8,128)(2,1)S(1)}, bf16[56,3072]{1,0:T(8,128)(2,1)S(1)}, u32[]{:S(2)}, u32[]{:S(2)}) collective-permute-start(bf16[56,3072]{1,0:T(8,128)(2,1)S(1)} %add_convert_fusion.5), channel_id=1, source_target_pairs={{0,2},{2,0},{4,6},{6,4},{1,3},{3,1},{5,7},{7,5},{8,10},{10,8},{12,... | collective-permute-start | bytes 1032200 | tf_op jit(solution)/shard_map/ppermute | solution.py:104
  89.6 10.8 %collective-permute-start.17 = (bf16[56,3072]{1,0:T(8,128)(2,1)S(1)}, bf16[56,3072]{1,0:T(8,128)(2,1)S(1)}, u32[]{:S(2)}, u32[]{:S(2)}) collective-permute-start(bf16[56,3072]{1,0:T(8,128)(2,1)S(1)} %get-tuple-element.54), channel_id=1, source_target_pairs={{0,2},{2,0},{4,6},{6,4},{1,3},{3,1},{5,7},{7,5},{8,10},{10,8},{12,... | collective-permute-start | bytes 1032200 | tf_op jit(solution)/shard_map/ppermute | solution.py:104
  97.0 12.4 %collective-permute-start.23 = (bf16[56,3072]{1,0:T(8,128)(2,1)S(1)}, bf16[56,3072]{1,0:T(8,128)(2,1)S(1)}, u32[]{:S(2)}, u32[]{:S(2)}) collective-permute-start(bf16[56,3072]{1,0:T(8,128)(2,1)S(1)} %get-tuple-element.51), channel_id=1, source_target_pairs={{2,4},{4,2},{3,5},{5,3},{10,12},{12,10},{11,13},{13,11},{18,20},{2... | collective-permute-start | bytes 1032200 | tf_op jit(solution)/shard_map/ppermute | solution.py:104
  97.7 29.0 %collective-permute-start.28 = (bf16[56,3072]{1,0:T(8,128)(2,1)S(1)}, bf16[56,3072]{1,0:T(8,128)(2,1)S(1)}, u32[]{:S(2)}, u32[]{:S(2)}) collective-permute-start(bf16[56,3072]{1,0:T(8,128)(2,1)S(1)} %get-tuple-element.50), channel_id=1, source_target_pairs={{2,4},{4,2},{3,5},{5,3},{10,12},{12,10},{11,13},{13,11},{18,20},{2... | collective-permute-start | bytes 1032200 | tf_op jit(solution)/shard_map/ppermute | solution.py:104
  100.6 11.5 %collective-permute-start.18 = (bf16[56,3072]{1,0:T(8,128)(2,1)S(1)}, bf16[56,3072]{1,0:T(8,128)(2,1)S(1)}, u32[]{:S(2)}, u32[]{:S(2)}) collective-permute-start(bf16[56,3072]{1,0:T(8,128)(2,1)S(1)} %get-tuple-element.52), channel_id=1, source_target_pairs={{2,4},{4,2},{3,5},{5,3},{10,12},{12,10},{11,13},{13,11},{18,20},{2... | collective-permute-start | bytes 1032200 | tf_op jit(solution)/shard_map/ppermute | solution.py:104
  101.3 13.3 %collective-permute-start.21 = (bf16[56,3072]{1,0:T(8,128)(2,1)S(1)}, bf16[56,3072]{1,0:T(8,128)(2,1)S(1)}, u32[]{:S(2)}, u32[]{:S(2)}) collective-permute-start(bf16[56,3072]{1,0:T(8,128)(2,1)S(1)} %get-tuple-element.53), channel_id=1, source_target_pairs={{0,2},{2,0},{4,6},{6,4},{1,3},{3,1},{5,7},{7,5},{8,10},{10,8},{12,... | collective-permute-start | bytes 1032200 | tf_op jit(solution)/shard_map/ppermute | solution.py:104
  109.5 25.1 %collective-permute-start.30 = (bf16[56,3072]{1,0:T(8,128)(2,1)S(1)}, bf16[56,3072]{1,0:T(8,128)(2,1)S(1)}, u32[]{:S(2)}, u32[]{:S(2)}) collective-permute-start(bf16[56,3072]{1,0:T(8,128)(2,1)S(1)} %add_convert_fusion.6), channel_id=1, source_target_pairs={{0,2},{2,0},{4,6},{6,4},{1,3},{3,1},{5,7},{7,5},{8,10},{10,8},{12,... | collective-permute-start | bytes 1032200 | tf_op jit(solution)/shard_map/ppermute | solution.py:104
  116.6 13.0 %collective-permute-start.26 = (bf16[56,3072]{1,0:T(8,128)(2,1)S(1)}, bf16[56,3072]{1,0:T(8,128)(2,1)S(1)}, u32[]{:S(2)}, u32[]{:S(2)}) collective-permute-start(bf16[56,3072]{1,0:T(8,128)(2,1)S(1)} %get-tuple-element.49), channel_id=1, source_target_pairs={{0,2},{2,0},{4,6},{6,4},{1,3},{3,1},{5,7},{7,5},{8,10},{10,8},{12,... | collective-permute-start | bytes 1032200 | tf_op jit(solution)/shard_map/ppermute | solution.py:104
  129.7 25.4 %collective-permute-start.32 = (bf16[56,3072]{1,0:T(8,128)(2,1)S(1)}, bf16[56,3072]{1,0:T(8,128)(2,1)S(1)}, u32[]{:S(2)}, u32[]{:S(2)}) collective-permute-start(bf16[56,3072]{1,0:T(8,128)(2,1)S(1)} %fusion.39), channel_id=1, source_target_pairs={{0,2},{2,0},{4,6},{6,4},{1,3},{3,1},{5,7},{7,5},{8,10},{10,8},{12,... | collective-permute-start | bytes 1032200 | tf_op jit(solution)/shard_map/ppermute | solution.py:104
  134.0 21.1 %collective-permute-start.35 = (bf16[56,3072]{1,0:T(8,128)(2,1)S(1)}, bf16[56,3072]{1,0:T(8,128)(2,1)S(1)}, u32[]{:S(2)}, u32[]{:S(2)}) collective-permute-start(bf16[56,3072]{1,0:T(8,128)(2,1)S(1)} %fusion.39), channel_id=1, source_target_pairs={{2,4},{4,2},{3,5},{5,3},{10,12},{12,10},{11,13},{13,11},{18,20},{2... | collective-permute-start | bytes 1032200 | tf_op jit(solution)/shard_map/ppermute | solution.py:104
  144.4 14.2 %collective-permute-start.34 = (bf16[56,3072]{1,0:T(8,128)(2,1)S(1)}, bf16[56,3072]{1,0:T(8,128)(2,1)S(1)}, u32[]{:S(2)}, u32[]{:S(2)}) collective-permute-start(bf16[56,3072]{1,0:T(8,128)(2,1)S(1)} %fusion.35), channel_id=1, source_target_pairs={{2,4},{4,2},{3,5},{5,3},{10,12},{12,10},{11,13},{13,11},{18,20},{2... | collective-permute-start | bytes 1032200 | tf_op jit(solution)/shard_map/ppermute | solution.py:104
  145.1 16.0 %collective-permute-start.36 = (bf16[56,3072]{1,0:T(8,128)(2,1)S(1)}, bf16[56,3072]{1,0:T(8,128)(2,1)S(1)}, u32[]{:S(2)}, u32[]{:S(2)}) collective-permute-start(bf16[56,3072]{1,0:T(8,128)(2,1)S(1)} %fusion.35), channel_id=1, source_target_pairs={{0,2},{2,0},{4,6},{6,4},{1,3},{3,1},{5,7},{7,5},{8,10},{10,8},{12,... | collective-permute-start | bytes 1032200 | tf_op jit(solution)/shard_map/ppermute | solution.py:104
  155.8 12.9 %collective-permute-start.43 = (bf16[56,3072]{1,0:T(8,128)(2,1)S(1)}, bf16[56,3072]{1,0:T(8,128)(2,1)S(1)}, u32[]{:S(2)}, u32[]{:S(2)}) collective-permute-start(bf16[56,3072]{1,0:T(8,128)(2,1)S(1)} %collective-permute-done.35), channel_id=1, source_target_pairs={{2,0},{4,6},{3,1},{5,7},{10,8},{12,14},{11,9},{13,15},{18,16},{20,... | collective-permute-start | bytes 1032200 | tf_op jit(solution)/shard_map/ppermute | solution.py:104
  161.8 19.6 %collective-permute-start.45 = (bf16[56,3072]{1,0:T(8,128)(2,1)S(1)}, bf16[56,3072]{1,0:T(8,128)(2,1)S(1)}, u32[]{:S(2)}, u32[]{:S(2)}) collective-permute-start(bf16[56,3072]{1,0:T(8,128)(2,1)S(1)} %collective-permute-done.34), channel_id=1, source_target_pairs={{2,0},{4,6},{3,1},{5,7},{10,8},{12,14},{11,9},{13,15},{18,16},{20,... | collective-permute-start | bytes 1032200 | tf_op jit(solution)/shard_map/ppermute | solution.py:104
  164.6 16.7 %collective-permute-start.42 = (bf16[56,3072]{1,0:T(8,128)(2,1)S(1)}, bf16[56,3072]{1,0:T(8,128)(2,1)S(1)}, u32[]{:S(2)}, u32[]{:S(2)}) collective-permute-start(bf16[56,3072]{1,0:T(8,128)(2,1)S(1)} %collective-permute-done.33), channel_id=1, source_target_pairs={{2,0},{4,6},{3,1},{5,7},{10,8},{12,14},{11,9},{13,15},{18,16},{20,... | collective-permute-start | bytes 1032200 | tf_op jit(solution)/shard_map/ppermute | solution.py:104
  170.2 14.8 %collective-permute-start.44 = (bf16[56,3072]{1,0:T(8,128)(2,1)S(1)}, bf16[56,3072]{1,0:T(8,128)(2,1)S(1)}, u32[]{:S(2)}, u32[]{:S(2)}) collective-permute-start(bf16[56,3072]{1,0:T(8,128)(2,1)S(1)} %collective-permute-done.37), channel_id=1, source_target_pairs={{2,0},{4,6},{3,1},{5,7},{10,8},{12,14},{11,9},{13,15},{18,16},{20,... | collective-permute-start | bytes 1032200 | tf_op jit(solution)/shard_map/ppermute | solution.py:104
  199.5 11.0 %collective-permute-start.39 = (bf16[2,56,576]{2,1,0:T(8,128)(2,1)S(1)}, bf16[2,56,576]{2,1,0:T(8,128)(2,1)S(1)}, u32[]{:S(2)}, u32[]{:S(2)}) collective-permute-start(bf16[2,56,576]{2,1,0:T(8,128)(2,1)S(1)} %get-tuple-element.76), channel_id=1, source_target_pairs={{0,8},{8,16},{16,24},{1,9},{9,17},{17,25},{2,10},{10,18},{18,26},{... | collective-permute-start | bytes 387080 | tf_op jit(solution)/shard_map/ppermute | solution.py:183
  (28 other events, 624.2 us)

commit v2 on v1

--- a/solution.py
+++ b/solution.py
@@ -8,6 +8,7 @@
 GROUPS = 2
 CHUNKS = 2
 STREAMS = 2
+PIECES = 2
 
 
 def local(segments, ring, cores, layer_inputs, targets, enc_weight, enc_bias, dec_weight):
@@ -25,14 +26,23 @@
 
     own_rows = lax.all_gather(layer_inputs[0], "tok", axis=1, tiled=True)
 
+    swaps = ring & (ring - 1) == 0
+
     def exchanged(group):
         block = own_rows[group * rows : (group + 1) * rows]
         parts = []
         for k in range(ring):
-            part = lax.dynamic_slice_in_dim(block, ((z + k) % ring) * depth, depth, axis=1)
+            to = z ^ k if swaps else (z + k) % ring
+            part = lax.dynamic_slice_in_dim(block, to * depth, depth, axis=1)
             if k:
-                part = lax.ppermute(part, "feat", [(i, (i + k) % ring) for i in range(ring)])
+                pairs = [(i, i ^ k if swaps else (i + k) % ring) for i in range(ring)]
+                part = lax.ppermute(part, "feat", pairs)
             parts.append(part)
+        if swaps:
+            both = jnp.stack(parts)
+            parts = [
+                lax.dynamic_index_in_dim(both, z ^ ((z - k) % ring), axis=0, keepdims=False) for k in range(ring)
+            ]
         return jnp.concatenate(parts, axis=0)
 
     columns = [exchanged(group) for group in range(GROUPS)]
@@ -48,7 +58,7 @@
     decoded = {}
     waiting = []
     ordered = [None]
-    left = {group: CHUNKS * layers for group in range(GROUPS)}
+    left = {g: [(c, t) for c in range(CHUNKS) for t in range(layers)] for g in range(GROUPS)}
     totals = {}
     residuals = {}
 
@@ -57,15 +67,19 @@
         return lax.optimization_barrier((values, others))[0] if others else values
 
     def background(sent):
-        if waiting:
-            ordered[0] = waiting.pop(0)(sent)
+        for _ in range(PIECES):
+            if waiting:
+                work, alone = waiting.pop(0)
+                ordered[0] = sent = work(sent)
+                if alone:
+                    break
 
     def decode(unit, codes):
         group, chunk = unit
 
         def piece(layer):
             def run(sent):
-                all_codes = after(codes_of[0], sent)
+                all_codes = after(codes_of[0], [sent, residuals.get(group - 1)])
                 out = lax.dot_general(
                     all_codes,
                     decoders[layer, :, chunk * width : (chunk + 1) * width],
@@ -74,15 +88,17 @@
                 )
                 key = group, layer
                 decoded[key] = out if key not in decoded else decoded[key] + out
-                left[group] -= 1
+                left[group].remove((chunk, layer))
                 if not left[group]:
-                    waiting.extend([lambda sent: share_cores(group, sent), lambda sent: share_segments(group, sent)])
+                    waiting.append((lambda sent: share_segments(group, sent), True))
+                elif all(other == 0 for _, other in left[group]) and layer:
+                    waiting.insert(0, (lambda sent: share_cores(group, sent), True))
                 return decoded[key]
 
             return run
 
         codes_of = [jnp.concatenate(codes, axis=0)]
-        waiting.extend(piece(layer) for layer in reversed(range(layers)))
+        waiting.extend((piece(layer), False) for layer in reversed(range(layers)))
 
     class Stream:
         def __init__(self, own):
@@ -150,15 +166,15 @@
                 return True
             return not (i == n and k == ring - 2)
 
-    def share_cores(group, sent):
-        blocks = after([decoded[group, layer] for layer in range(layers)], sent)
-        blocks = jnp.stack(blocks).reshape(layers, ring, rows, depth)
+    def share_cores(group, sent, first=1):
+        blocks = after([decoded[group, layer] for layer in range(first, layers if first else 1)], sent)
+        blocks = jnp.stack(blocks).reshape(-1, ring, rows, depth)
 
         def share(index):
-            first = index * per_core
+            begin = index * per_core
             return jnp.stack(
                 [
-                    lax.dynamic_index_in_dim(blocks, (z - first - b) % ring, axis=1, keepdims=False)
+                    lax.dynamic_index_in_dim(blocks, (z - begin - b) % ring, axis=1, keepdims=False)
                     for b in range(per_core)
                 ],
                 axis=1,
@@ -170,19 +186,26 @@
             given.append(share((core + k) % cores).astype(BF16))
             got = lax.ppermute(given[-1], "tok", [(i, (i + k) % cores) for i in range(cores)])
             total += got.astype(F32)
-        totals[group] = total
+        totals[group, first] = total
         return given
 
     def share_segments(group, sent):
-        total = after(totals[group], sent)
-        own = lax.dynamic_index_in_dim(total, segment, axis=0, keepdims=False)
-        given = []
+        total = after(totals[group, 1], sent)
+        paired = segments & (segments - 1) == 0
+        received, given = [], []
         for k in range(1, segments):
-            place = jnp.minimum(segment + k, layers - 1)
-            given.append(lax.dynamic_index_in_dim(total, place, axis=0, keepdims=False).astype(BF16))
-            got = lax.ppermute(given[-1], "segment", [(i, i + k) for i in range(segments - k)])
-            own += got.astype(F32)
-        residuals[group] = own
+            place = segment ^ k if paired else jnp.minimum(segment + k, layers - 1)
+            given.append(lax.dynamic_index_in_dim(total, jnp.maximum(place, 1) - 1, axis=0, keepdims=False).astype(BF16))
+            pairs = [(i, i ^ k if paired else i + k) for i in range(segments)]
+            got = lax.ppermute(given[-1], "segment", [(i, j) for i, j in pairs if i < j < segments])
+            received.append(got)
+        share_cores(group, given, 0)
+        own = jnp.where(
+            segment == 0,
+            totals[group, 0][0],
+            lax.dynamic_index_in_dim(total, jnp.maximum(segment, 1) - 1, axis=0, keepdims=False),
+        )
+        residuals[group] = sum([got.astype(F32) for got in received], own)
         return given
 
     streams = [Stream(units[i::STREAMS]) for i in range(STREAMS)]

time: 219 us -> 245 us (1.12)
  matrix products: 30.2 us -> 57 us
  starting transfers between devices: 119 us -> 108 us
  waiting for transfers between devices: 56.3 us -> 63.1 us
    dot_general x16, matrix products: 23.1 us -> 49.9 us  [run(): lax.dot_general(all_codes, decoders[layer, :, chunk * width:(chunk + 1) *...]
    ppermute x36, starting transfers between devices: 95.6 us -> 81.9 us  [swap(): return lax.ppermute(value, 'feat', pairs) if pairs else None]
    ppermute x12, waiting for transfers between devices: 4.88 us -> 13.4 us  [the longest x6 7.48 us: exchanged(): part = lax.ppermute(part, 'feat', pairs)]
    ppermute x12, starting transfers between devices: 23 us -> 25.5 us  [the longest x6 15.4 us: share_segments(): lax.ppermute(given[-1], 'segment', [(i, j) for i, j in pairs if i < j < s...]
  transfers between devices with their start and end apart: 50 -> 52, of which waited for: 17 -> 16; matrix products, arithmetic and copies ran while one was open for 11% -> 21% of each run, Pallas kernels for 0% -> 0%
where the time goes in v2:
time: 245 us; the launch traced here: 244 us
  starting transfers between devices  108 us (44%)
  waiting for transfers between devices  63.1 us (26%)
  matrix products  57 us (23%)
  other arithmetic  8.74 us (4%)
  local copies, waits for them, and re-layouts  3.07 us (1%)
  blocking collectives  2.47 us (1%)
    ppermute x36, starting transfers between devices, swap(): return lax.ppermute(value, 'feat', pairs) if pairs else None  81.9 us
    dot_general x16, matrix products, run(): lax.dot_general(all_codes, decoders[layer, :, chunk * width:(chunk + 1) *...  49.9 us
    ppermute x36, waiting for transfers between devices, swap(): return lax.ppermute(value, 'feat', pairs) if pairs else None  49.7 us
    ppermute x6, starting transfers between devices, share_segments(): lax.ppermute(given[-1], 'segment', [(i, j) for i, j in pairs if i < j < s...  15.4 us
    ppermute x6, starting transfers between devices, exchanged(): part = lax.ppermute(part, 'feat', pairs)  10.1 us
    ppermute x6, waiting for transfers between devices, exchanged(): part = lax.ppermute(part, 'feat', pairs)  7.48 us
    dot_general x4, matrix products, partial_sums(): jnp.dot(columns[group], weight[:, chunk * width:(chunk + 1) * width], pre...  7.16 us
    ppermute x6, waiting for transfers between devices, share_segments(): lax.ppermute(given[-1], 'segment', [(i, j) for i, j in pairs if i < j < s...  5.95 us
  transfers between devices with their start and end apart: 52, of which 16 were waited for; matrix products, arithmetic and copies ran while one was open for 21% of the time, Pallas kernels for 0%

profile of v2, /device:TPU:0, one launch (start us, length us, event | category | flops | bytes accessed | tf_op | source)
XLA Modules:
  0.0 243.8 jit_solution(3658730744762238164)
XLA Ops:
  10.1 3.5 %collective-permute-start.14 = (bf16[56,576]{1,0:T(8,128)(2,1)S(1)}, bf16[56,576]{1,0:T(8,128)(2,1)S(1)}, u32[]{:S(2)}, u32[]{:S(2)}) collective-permute-start(bf16[56,576]{1,0:T(8,128)(2,1)S(1)} %get-tuple-element.133), channel_id=1, source_target_pairs={{0,4},{2,6},{4,0},{6,2},{1,5},{3,7},{5,1},{7,3},{8,12},{10,14},{12... | collective-permute-start | bytes 193544 | tf_op jit(solution)/shard_map/ppermute | solution.py:39
  16.1 5.1 %collective-permute-done.14 = bf16[56,576]{1,0:T(8,128)(2,1)S(1)} collective-permute-done((bf16[56,576]{1,0:T(8,128)(2,1)S(1)}, bf16[56,576]{1,0:T(8,128)(2,1)S(1)}, u32[]{:S(2)}, u32[]{:S(2)}) %collective-permute-start.14) | collective-permute-done | bytes 64544 | tf_op jit(solution)/shard_map/ppermute | solution.py:39
  21.4 3.4 %fusion.18 = f32[224,3072]{1,0:T(8,128)S(1)} fusion(bf16[576,6144]{1,0:T(8,128)(2,1)} %bitcast.186, bf16[56,576]{1,0:T(8,128)(2,1)S(1)} %get-tuple-element.140, bf16[56,576]{1,0:T(8,128)(2,1)S(1)} %get-tuple-element.139, bf16[56,576]{1,0:T(8,128)(2,1)S(1)} %get-tuple-element.138, bf16[56,576]{1,0:T(8,128)(2,1)S(1)} %get-tuple-element.141), kind=kOutput, calls=%fused_computation.26 | convolution fusion | flops 793755648 | bytes 6549504 | tf_op jit(solution)/shard_map/dot_general | solution.py:51
  39.5 13.9 %collective-permute-done.3 = bf16[56,3072]{1,0:T(8,128)(2,1)S(1)} collective-permute-done((bf16[56,3072]{1,0:T(8,128)(2,1)S(1)}, bf16[56,3072]{1,0:T(8,128)(2,1)S(1)}, u32[]{:S(2)}, u32[]{:S(2)}) %collective-permute-start.3) | collective-permute-done | bytes 344096 | tf_op jit(solution)/shard_map/ppermute | solution.py:120
  54.5 5.3 %collective-permute-start.10 = (bf16[56,3072]{1,0:T(8,128)(2,1)S(1)}, bf16[56,3072]{1,0:T(8,128)(2,1)S(1)}, u32[]{:S(2)}, u32[]{:S(2)}) collective-permute-start(bf16[56,3072]{1,0:T(8,128)(2,1)S(1)} %get-tuple-element.84), channel_id=1, source_target_pairs={{0,2},{2,0},{4,6},{6,4},{1,3},{3,1},{5,7},{7,5},{8,10},{10,8},{12,... | collective-permute-start | bytes 1032200 | tf_op jit(solution)/shard_map/ppermute | solution.py:120
  61.1 8.2 %collective-permute-start.5 = (bf16[56,3072]{1,0:T(8,128)(2,1)S(1)}, bf16[56,3072]{1,0:T(8,128)(2,1)S(1)}, u32[]{:S(2)}, u32[]{:S(2)}) collective-permute-start(bf16[56,3072]{1,0:T(8,128)(2,1)S(1)} %get-tuple-element.80), channel_id=1, source_target_pairs={{0,2},{2,0},{4,6},{6,4},{1,3},{3,1},{5,7},{7,5},{8,10},{10,8},{12,... | collective-permute-start | bytes 1032200 | tf_op jit(solution)/shard_map/ppermute | solution.py:120
  70.8 9.2 %collective-permute-start.22 = (bf16[56,3072]{1,0:T(8,128)(2,1)S(1)}, bf16[56,3072]{1,0:T(8,128)(2,1)S(1)}, u32[]{:S(2)}, u32[]{:S(2)}) collective-permute-start(bf16[56,3072]{1,0:T(8,128)(2,1)S(1)} %fusion.43), channel_id=1, source_target_pairs={{0,2},{2,0},{4,6},{6,4},{1,3},{3,1},{5,7},{7,5},{8,10},{10,8},{12,... | collective-permute-start | bytes 1032200 | tf_op jit(solution)/shard_map/ppermute | solution.py:120
  80.9 6.5 %collective-permute-start.19 = (bf16[56,3072]{1,0:T(8,128)(2,1)S(1)}, bf16[56,3072]{1,0:T(8,128)(2,1)S(1)}, u32[]{:S(2)}, u32[]{:S(2)}) collective-permute-start(bf16[56,3072]{1,0:T(8,128)(2,1)S(1)} %fusion.47), channel_id=1, source_target_pairs={{0,2},{2,0},{4,6},{6,4},{1,3},{3,1},{5,7},{7,5},{8,10},{10,8},{12,... | collective-permute-start | bytes 1032200 | tf_op jit(solution)/shard_map/ppermute | solution.py:120
  87.5 3.4 %collective-permute-start.25 = (bf16[56,3072]{1,0:T(8,128)(2,1)S(1)}, bf16[56,3072]{1,0:T(8,128)(2,1)S(1)}, u32[]{:S(2)}, u32[]{:S(2)}) collective-permute-start(bf16[56,3072]{1,0:T(8,128)(2,1)S(1)} %add_convert_fusion.5), channel_id=1, source_target_pairs={{0,2},{2,0},{4,6},{6,4},{1,3},{3,1},{5,7},{7,5},{8,10},{10,8},{12,... | collective-permute-start | bytes 1032200 | tf_op jit(solution)/shard_map/ppermute | solution.py:120
  90.9 4.3 %collective-permute-done.19 = bf16[56,3072]{1,0:T(8,128)(2,1)S(1)} collective-permute-done((bf16[56,3072]{1,0:T(8,128)(2,1)S(1)}, bf16[56,3072]{1,0:T(8,128)(2,1)S(1)}, u32[]{:S(2)}, u32[]{:S(2)}) %collective-permute-start.19) | collective-permute-done | bytes 344096 | tf_op jit(solution)/shard_map/ppermute | solution.py:120
  105.6 8.9 %collective-permute-start.21 = (bf16[56,3072]{1,0:T(8,128)(2,1)S(1)}, bf16[56,3072]{1,0:T(8,128)(2,1)S(1)}, u32[]{:S(2)}, u32[]{:S(2)}) collective-permute-start(bf16[56,3072]{1,0:T(8,128)(2,1)S(1)} %get-tuple-element.77), channel_id=1, source_target_pairs={{0,2},{2,0},{4,6},{6,4},{1,3},{3,1},{5,7},{7,5},{8,10},{10,8},{12,... | collective-permute-start | bytes 1032200 | tf_op jit(solution)/shard_map/ppermute | solution.py:120
  120.0 3.6 %fusion.1 = f32[224,576]{1,0:T(8,128)S(1)} fusion(bf16[224,3072]{1,0:T(8,128)(2,1)S(1)} %pad_maximum_fusion.2, bf16[4,576,6144]{2,1,0:T(8,128)(2,1)} %bitcast.168), kind=kOutput, calls=%fused_computation.9 | convolution fusion | flops 792723456 | bytes 5431296 | tf_op jit(solution)/shard_map/dot_general | solution.py:83
  123.7 3.6 %fusion.3 = f32[224,576]{1,0:T(8,128)S(1)} fusion(bf16[224,3072]{1,0:T(8,128)(2,1)S(1)} %pad_maximum_fusion.2, bf16[4,576,6144]{2,1,0:T(8,128)(2,1)} %bitcast.169), kind=kOutput, calls=%fused_computation.11 | convolution fusion | flops 792723456 | bytes 5431296 | tf_op jit(solution)/shard_map/dot_general | solution.py:83
  127.5 4.9 %collective-permute-start.26 = (bf16[56,3072]{1,0:T(8,128)(2,1)S(1)}, bf16[56,3072]{1,0:T(8,128)(2,1)S(1)}, u32[]{:S(2)}, u32[]{:S(2)}) collective-permute-start(bf16[56,3072]{1,0:T(8,128)(2,1)S(1)} %get-tuple-element.73), channel_id=1, source_target_pairs={{0,2},{2,0},{4,6},{6,4},{1,3},{3,1},{5,7},{7,5},{8,10},{10,8},{12,... | collective-permute-start | bytes 1032200 | tf_op jit(solution)/shard_map/ppermute | solution.py:120
  133.2 4.7 %fusion.5 = f32[224,576]{1,0:T(8,128)} fusion(bf16[224,3072]{1,0:T(8,128)(2,1)S(1)} %pad_maximum_fusion.2, bf16[4,576,6144]{2,1,0:T(8,128)(2,1)} %bitcast.170), kind=kOutput, calls=%fused_computation.13 | convolution fusion | flops 792723456 | bytes 5431296 | tf_op jit(solution)/shard_map/dot_general | solution.py:83
  137.9 4.4 %fusion.7 = f32[224,576]{1,0:T(8,128)} fusion(bf16[224,3072]{1,0:T(8,128)(2,1)S(1)} %pad_maximum_fusion.2, bf16[4,576,6144]{2,1,0:T(8,128)(2,1)} %bitcast.171), kind=kOutput, calls=%fused_computation.15 | convolution fusion | flops 792723456 | bytes 5431296 | tf_op jit(solution)/shard_map/dot_general | solution.py:83
  146.4 4.9 %collective-permute-start.37 = (bf16[56,3072]{1,0:T(8,128)(2,1)S(1)}, bf16[56,3072]{1,0:T(8,128)(2,1)S(1)}, u32[]{:S(2)}, u32[]{:S(2)}) collective-permute-start(bf16[56,3072]{1,0:T(8,128)(2,1)S(1)} %fusion.39), channel_id=1, source_target_pairs={{0,2},{2,0},{4,6},{6,4},{1,3},{3,1},{5,7},{7,5},{8,10},{10,8},{12,... | collective-permute-start | bytes 1032200 | tf_op jit(solution)/shard_map/ppermute | solution.py:120
  160.1 4.1 %collective-permute-start.34 = (bf16[2,56,576]{2,1,0:T(8,128)(2,1)}, bf16[2,56,576]{2,1,0:T(8,128)(2,1)}, u32[]{:S(2)}, u32[]{:S(2)}) collective-permute-start(bf16[2,56,576]{2,1,0:T(8,128)(2,1)} %get-tuple-element.109), channel_id=1, source_target_pairs={{0,8},{16,24},{1,9},{17,25},{2,10},{18,26},{3,11},{19,27},{4,12},{... | collective-permute-start | bytes 387080 | tf_op jit(solution)/shard_map/ppermute | solution.py:200
  164.1 4.1 %collective-permute-start.35 = (bf16[2,56,576]{2,1,0:T(8,128)(2,1)}, bf16[2,56,576]{2,1,0:T(8,128)(2,1)}, u32[]{:S(2)}, u32[]{:S(2)}) collective-permute-start(bf16[2,56,576]{2,1,0:T(8,128)(2,1)} %get-tuple-element.108), channel_id=1, source_target_pairs={{0,16},{8,24},{1,17},{9,25},{2,18},{10,26},{3,19},{11,27},{4,20},{... | collective-permute-start | bytes 387080 | tf_op jit(solution)/shard_map/ppermute | solution.py:200
  176.3 4.8 %collective-permute-done.42 = bf16[56,3072]{1,0:T(8,128)(2,1)S(1)} collective-permute-done((bf16[56,3072]{1,0:T(8,128)(2,1)S(1)}, bf16[56,3072]{1,0:T(8,128)(2,1)S(1)}, u32[]{:S(2)}, u32[]{:S(2)}) %collective-permute-start.42) | collective-permute-done | bytes 344096 | tf_op jit(solution)/shard_map/ppermute | solution.py:120
  184.4 4.1 %collective-permute-done.41 = bf16[56,3072]{1,0:T(8,128)(2,1)S(1)} collective-permute-done((bf16[56,3072]{1,0:T(8,128)(2,1)S(1)}, bf16[56,3072]{1,0:T(8,128)(2,1)S(1)}, u32[]{:S(2)}, u32[]{:S(2)}) %collective-permute-start.41) | collective-permute-done | bytes 344096 | tf_op jit(solution)/shard_map/ppermute | solution.py:120
  190.1 5.8 %collective-permute-done.46 = bf16[56,3072]{1,0:T(8,128)(2,1)S(1)} collective-permute-done((bf16[56,3072]{1,0:T(8,128)(2,1)S(1)}, bf16[56,3072]{1,0:T(8,128)(2,1)S(1)}, u32[]{:S(2)}, u32[]{:S(2)}) %collective-permute-start.46) | collective-permute-done | bytes 344096 | tf_op jit(solution)/shard_map/ppermute | solution.py:120
  195.9 7.3 %collective-permute-done.40 = bf16[56,3072]{1,0:T(8,128)(2,1)S(1)} collective-permute-done((bf16[56,3072]{1,0:T(8,128)(2,1)S(1)}, bf16[56,3072]{1,0:T(8,128)(2,1)S(1)}, u32[]{:S(2)}, u32[]{:S(2)}) %collective-permute-start.40) | collective-permute-done | bytes 344096 | tf_op jit(solution)/shard_map/ppermute | solution.py:120
  203.4 3.4 %fusion = f32[224,576]{1,0:T(8,128)S(1)} fusion(bf16[224,3072]{1,0:T(8,128)(2,1)S(1)} %pad_maximum_fusion.4, bf16[4,576,6144]{2,1,0:T(8,128)(2,1)} %bitcast.172), kind=kOutput, calls=%fused_computation.8 | convolution fusion | flops 792723456 | bytes 5431296 | tf_op jit(solution)/shard_map/dot_general | solution.py:83
  206.8 3.4 %fusion.2 = f32[224,576]{1,0:T(8,128)S(1)} fusion(bf16[224,3072]{1,0:T(8,128)(2,1)S(1)} %pad_maximum_fusion.4, bf16[4,576,6144]{2,1,0:T(8,128)(2,1)} %bitcast.173), kind=kOutput, calls=%fused_computation.10 | convolution fusion | flops 792723456 | bytes 5431296 | tf_op jit(solution)/shard_map/dot_general | solution.py:83
  210.3 3.4 %fusion.4 = f32[224,576]{1,0:T(8,128)S(1)} fusion(bf16[224,3072]{1,0:T(8,128)(2,1)S(1)} %pad_maximum_fusion.4, bf16[4,576,6144]{2,1,0:T(8,128)(2,1)} %bitcast.174), kind=kOutput, calls=%fused_computation.12 | convolution fusion | flops 792723456 | bytes 5431296 | tf_op jit(solution)/shard_map/dot_general | solution.py:83
  213.7 3.4 %fusion.6 = f32[224,576]{1,0:T(8,128)S(1)} fusion(bf16[224,3072]{1,0:T(8,128)(2,1)S(1)} %pad_maximum_fusion.4, bf16[4,576,6144]{2,1,0:T(8,128)(2,1)} %bitcast.175), kind=kOutput, calls=%fused_computation.14 | convolution fusion | flops 792723456 | bytes 5431296 | tf_op jit(solution)/shard_map/dot_general | solution.py:83
  217.4 3.5 %fusion.27 = f32[224,576]{1,0:T(8,128)S(1)} fusion(f32[224,576]{1,0:T(8,128)S(1)} %fusion, bf16[224,3072]{1,0:T(8,128)(2,1)S(1)} %pad_maximum_fusion.5, bf16[4,576,6144]{2,1,0:T(8,128)(2,1)} %bitcast.176), kind=kOutput, calls=%fused_computation.42 | convolution fusion | flops 792852480 | bytes 5947392 | tf_op jit(solution)/shard_map/dot_general | solution.py:83
  220.9 3.5 %fusion.29 = f32[224,576]{1,0:T(8,128)S(1)} fusion(f32[224,576]{1,0:T(8,128)S(1)} %fusion.4, bf16[224,3072]{1,0:T(8,128)(2,1)S(1)} %pad_maximum_fusion.5, bf16[4,576,6144]{2,1,0:T(8,128)(2,1)} %bitcast.177), kind=kOutput, calls=%fused_computation.44 | convolution fusion | flops 792852480 | bytes 5947392 | tf_op jit(solution)/shard_map/dot_general | solution.py:83
  224.3 3.5 %fusion.25 = f32[224,576]{1,0:T(8,128)S(1)} fusion(f32[224,576]{1,0:T(8,128)S(1)} %fusion.2, bf16[224,3072]{1,0:T(8,128)(2,1)S(1)} %pad_maximum_fusion.5, bf16[4,576,6144]{2,1,0:T(8,128)(2,1)} %bitcast.178), kind=kOutput, calls=%fused_computation.40 | convolution fusion | flops 792852480 | bytes 5947392 | tf_op jit(solution)/shard_map/dot_general | solution.py:83
  228.2 3.5 %fusion.31 = f32[224,576]{1,0:T(8,128)S(1)} fusion(f32[224,576]{1,0:T(8,128)S(1)} %fusion.6, bf16[224,3072]{1,0:T(8,128)(2,1)S(1)} %pad_maximum_fusion.5, bf16[4,576,6144]{2,1,0:T(8,128)(2,1)} %bitcast.179), kind=kOutput, calls=%fused_computation.46 | convolution fusion | flops 792852480 | bytes 5947392 | tf_op jit(solution)/shard_map/dot_general | solution.py:83
  238.8 3.8 %collective-permute-done.50 = bf16[2,56,576]{2,1,0:T(8,128)(2,1)S(1)} collective-permute-done((bf16[2,56,576]{2,1,0:T(8,128)(2,1)S(1)}, bf16[2,56,576]{2,1,0:T(8,128)(2,1)S(1)}, u32[]{:S(2)}, u32[]{:S(2)}) %collective-permute-start.50) | collective-permute-done | bytes 129056 | tf_op jit(solution)/shard_map/ppermute | solution.py:200
  (178 shorter events, 82.8 us)
Async XLA Ops:
  10.1 11.1 %collective-permute-start.14 = (bf16[56,576]{1,0:T(8,128)(2,1)S(1)}, bf16[56,576]{1,0:T(8,128)(2,1)S(1)}, u32[]{:S(2)}, u32[]{:S(2)}) collective-permute-start(bf16[56,576]{1,0:T(8,128)(2,1)S(1)} %get-tuple-element.133), channel_id=1, source_target_pairs={{0,4},{2,6},{4,0},{6,2},{1,5},{3,7},{5,1},{7,3},{8,12},{10,14},{12... | collective-permute-start | bytes 193544 | tf_op jit(solution)/shard_map/ppermute | solution.py:39
  26.9 11.8 %collective-permute-start.8 = (bf16[56,3072]{1,0:T(8,128)(2,1)S(1)}, bf16[56,3072]{1,0:T(8,128)(2,1)S(1)}, u32[]{:S(2)}, u32[]{:S(2)}) collective-permute-start(bf16[56,3072]{1,0:T(8,128)(2,1)S(1)} %get-tuple-element.86), channel_id=1, source_target_pairs={{0,2},{6,4},{1,3},{7,5},{8,10},{14,12},{9,11},{15,13},{16,18},{22,... | collective-permute-start | bytes 1032200 | tf_op jit(solution)/shard_map/ppermute | solution.py:120
  30.2 24.1 %collective-permute-start.11 = (bf16[56,3072]{1,0:T(8,128)(2,1)S(1)}, bf16[56,3072]{1,0:T(8,128)(2,1)S(1)}, u32[]{:S(2)}, u32[]{:S(2)}) collective-permute-start(bf16[56,3072]{1,0:T(8,128)(2,1)S(1)} %get-tuple-element.87), channel_id=1, source_target_pairs={{0,2},{6,4},{1,3},{7,5},{8,10},{14,12},{9,11},{15,13},{16,18},{22,... | collective-permute-start | bytes 1032200 | tf_op jit(solution)/shard_map/ppermute | solution.py:120
  31.7 21.7 %collective-permute-start.3 = (bf16[56,3072]{1,0:T(8,128)(2,1)S(1)}, bf16[56,3072]{1,0:T(8,128)(2,1)S(1)}, u32[]{:S(2)}, u32[]{:S(2)}) collective-permute-start(bf16[56,3072]{1,0:T(8,128)(2,1)S(1)} %get-tuple-element.82), channel_id=1, source_target_pairs={{0,2},{6,4},{1,3},{7,5},{8,10},{14,12},{9,11},{15,13},{16,18},{22,... | collective-permute-start | bytes 1032200 | tf_op jit(solution)/shard_map/ppermute | solution.py:120
  33.0 27.8 %collective-permute-start.6 = (bf16[56,3072]{1,0:T(8,128)(2,1)S(1)}, bf16[56,3072]{1,0:T(8,128)(2,1)S(1)}, u32[]{:S(2)}, u32[]{:S(2)}) collective-permute-start(bf16[56,3072]{1,0:T(8,128)(2,1)S(1)} %get-tuple-element.83), channel_id=1, source_target_pairs={{0,2},{6,4},{1,3},{7,5},{8,10},{14,12},{9,11},{15,13},{16,18},{22,... | collective-permute-start | bytes 1032200 | tf_op jit(solution)/shard_map/ppermute | solution.py:120
  38.8 15.5 %collective-permute-start.9 = (bf16[56,3072]{1,0:T(8,128)(2,1)S(1)}, bf16[56,3072]{1,0:T(8,128)(2,1)S(1)}, u32[]{:S(2)}, u32[]{:S(2)}) collective-permute-start(bf16[56,3072]{1,0:T(8,128)(2,1)S(1)} %add_convert_fusion.14), channel_id=1, source_target_pairs={{2,4},{4,2},{3,5},{5,3},{10,12},{12,10},{11,13},{13,11},{18,20},{2... | collective-permute-start | bytes 1032200 | tf_op jit(solution)/shard_map/ppermute | solution.py:120
  54.5 15.4 %collective-permute-start.10 = (bf16[56,3072]{1,0:T(8,128)(2,1)S(1)}, bf16[56,3072]{1,0:T(8,128)(2,1)S(1)}, u32[]{:S(2)}, u32[]{:S(2)}) collective-permute-start(bf16[56,3072]{1,0:T(8,128)(2,1)S(1)} %get-tuple-element.84), channel_id=1, source_target_pairs={{0,2},{2,0},{4,6},{6,4},{1,3},{3,1},{5,7},{7,5},{8,10},{10,8},{12,... | collective-permute-start | bytes 1032200 | tf_op jit(solution)/shard_map/ppermute | solution.py:120
  61.1 18.9 %collective-permute-start.5 = (bf16[56,3072]{1,0:T(8,128)(2,1)S(1)}, bf16[56,3072]{1,0:T(8,128)(2,1)S(1)}, u32[]{:S(2)}, u32[]{:S(2)}) collective-permute-start(bf16[56,3072]{1,0:T(8,128)(2,1)S(1)} %get-tuple-element.80), channel_id=1, source_target_pairs={{0,2},{2,0},{4,6},{6,4},{1,3},{3,1},{5,7},{7,5},{8,10},{10,8},{12,... | collective-permute-start | bytes 1032200 | tf_op jit(solution)/shard_map/ppermute | solution.py:120
  69.3 10.7 %collective-permute-start.7 = (bf16[56,3072]{1,0:T(8,128)(2,1)S(1)}, bf16[56,3072]{1,0:T(8,128)(2,1)S(1)}, u32[]{:S(2)}, u32[]{:S(2)}) collective-permute-start(bf16[56,3072]{1,0:T(8,128)(2,1)S(1)} %get-tuple-element.81), channel_id=1, source_target_pairs={{2,4},{4,2},{3,5},{5,3},{10,12},{12,10},{11,13},{13,11},{18,20},{2... | collective-permute-start | bytes 1032200 | tf_op jit(solution)/shard_map/ppermute | solution.py:120
  70.1 17.2 %collective-permute-start.24 = (bf16[56,3072]{1,0:T(8,128)(2,1)S(1)}, bf16[56,3072]{1,0:T(8,128)(2,1)S(1)}, u32[]{:S(2)}, u32[]{:S(2)}) collective-permute-start(bf16[56,3072]{1,0:T(8,128)(2,1)S(1)} %fusion.43), channel_id=1, source_target_pairs={{2,4},{4,2},{3,5},{5,3},{10,12},{12,10},{11,13},{13,11},{18,20},{2... | collective-permute-start | bytes 1032200 | tf_op jit(solution)/shard_map/ppermute | solution.py:120
  70.8 27.0 %collective-permute-start.22 = (bf16[56,3072]{1,0:T(8,128)(2,1)S(1)}, bf16[56,3072]{1,0:T(8,128)(2,1)S(1)}, u32[]{:S(2)}, u32[]{:S(2)}) collective-permute-start(bf16[56,3072]{1,0:T(8,128)(2,1)S(1)} %fusion.43), channel_id=1, source_target_pairs={{0,2},{2,0},{4,6},{6,4},{1,3},{3,1},{5,7},{7,5},{8,10},{10,8},{12,... | collective-permute-start | bytes 1032200 | tf_op jit(solution)/shard_map/ppermute | solution.py:120
  80.2 10.7 %collective-permute-start.16 = (bf16[56,3072]{1,0:T(8,128)(2,1)S(1)}, bf16[56,3072]{1,0:T(8,128)(2,1)S(1)}, u32[]{:S(2)}, u32[]{:S(2)}) collective-permute-start(bf16[56,3072]{1,0:T(8,128)(2,1)S(1)} %fusion.47), channel_id=1, source_target_pairs={{2,4},{4,2},{3,5},{5,3},{10,12},{12,10},{11,13},{13,11},{18,20},{2... | collective-permute-start | bytes 1032200 | tf_op jit(solution)/shard_map/ppermute | solution.py:120
  80.9 14.3 %collective-permute-start.19 = (bf16[56,3072]{1,0:T(8,128)(2,1)S(1)}, bf16[56,3072]{1,0:T(8,128)(2,1)S(1)}, u32[]{:S(2)}, u32[]{:S(2)}) collective-permute-start(bf16[56,3072]{1,0:T(8,128)(2,1)S(1)} %fusion.47), channel_id=1, source_target_pairs={{0,2},{2,0},{4,6},{6,4},{1,3},{3,1},{5,7},{7,5},{8,10},{10,8},{12,... | collective-permute-start | bytes 1032200 | tf_op jit(solution)/shard_map/ppermute | solution.py:120
  87.5 13.2 %collective-permute-start.25 = (bf16[56,3072]{1,0:T(8,128)(2,1)S(1)}, bf16[56,3072]{1,0:T(8,128)(2,1)S(1)}, u32[]{:S(2)}, u32[]{:S(2)}) collective-permute-start(bf16[56,3072]{1,0:T(8,128)(2,1)S(1)} %add_convert_fusion.5), channel_id=1, source_target_pairs={{0,2},{2,0},{4,6},{6,4},{1,3},{3,1},{5,7},{7,5},{8,10},{10,8},{12,... | collective-permute-start | bytes 1032200 | tf_op jit(solution)/shard_map/ppermute | solution.py:120
  101.0 13.6 %collective-permute-start.23 = (bf16[56,3072]{1,0:T(8,128)(2,1)S(1)}, bf16[56,3072]{1,0:T(8,128)(2,1)S(1)}, u32[]{:S(2)}, u32[]{:S(2)}) collective-permute-start(bf16[56,3072]{1,0:T(8,128)(2,1)S(1)} %get-tuple-element.75), channel_id=1, source_target_pairs={{2,4},{4,2},{3,5},{5,3},{10,12},{12,10},{11,13},{13,11},{18,20},{2... | collective-permute-start | bytes 1032200 | tf_op jit(solution)/shard_map/ppermute | solution.py:120
  101.7 40.7 %collective-permute-start.28 = (bf16[56,3072]{1,0:T(8,128)(2,1)S(1)}, bf16[56,3072]{1,0:T(8,128)(2,1)S(1)}, u32[]{:S(2)}, u32[]{:S(2)}) collective-permute-start(bf16[56,3072]{1,0:T(8,128)(2,1)S(1)} %get-tuple-element.74), channel_id=1, source_target_pairs={{2,4},{4,2},{3,5},{5,3},{10,12},{12,10},{11,13},{13,11},{18,20},{2... | collective-permute-start | bytes 1032200 | tf_op jit(solution)/shard_map/ppermute | solution.py:120
  104.6 12.8 %collective-permute-start.18 = (bf16[56,3072]{1,0:T(8,128)(2,1)S(1)}, bf16[56,3072]{1,0:T(8,128)(2,1)S(1)}, u32[]{:S(2)}, u32[]{:S(2)}) collective-permute-start(bf16[56,3072]{1,0:T(8,128)(2,1)S(1)} %get-tuple-element.76), channel_id=1, source_target_pairs={{2,4},{4,2},{3,5},{5,3},{10,12},{12,10},{11,13},{13,11},{18,20},{2... | collective-permute-start | bytes 1032200 | tf_op jit(solution)/shard_map/ppermute | solution.py:120
  105.6 14.2 %collective-permute-start.21 = (bf16[56,3072]{1,0:T(8,128)(2,1)S(1)}, bf16[56,3072]{1,0:T(8,128)(2,1)S(1)}, u32[]{:S(2)}, u32[]{:S(2)}) collective-permute-start(bf16[56,3072]{1,0:T(8,128)(2,1)S(1)} %get-tuple-element.77), channel_id=1, source_target_pairs={{0,2},{2,0},{4,6},{6,4},{1,3},{3,1},{5,7},{7,5},{8,10},{10,8},{12,... | collective-permute-start | bytes 1032200 | tf_op jit(solution)/shard_map/ppermute | solution.py:120
  114.8 27.6 %collective-permute-start.30 = (bf16[56,3072]{1,0:T(8,128)(2,1)S(1)}, bf16[56,3072]{1,0:T(8,128)(2,1)S(1)}, u32[]{:S(2)}, u32[]{:S(2)}) collective-permute-start(bf16[56,3072]{1,0:T(8,128)(2,1)S(1)} %add_convert_fusion.6), channel_id=1, source_target_pairs={{0,2},{2,0},{4,6},{6,4},{1,3},{3,1},{5,7},{7,5},{8,10},{10,8},{12,... | collective-permute-start | bytes 1032200 | tf_op jit(solution)/shard_map/ppermute | solution.py:120
  127.5 17.8 %collective-permute-start.26 = (bf16[56,3072]{1,0:T(8,128)(2,1)S(1)}, bf16[56,3072]{1,0:T(8,128)(2,1)S(1)}, u32[]{:S(2)}, u32[]{:S(2)}) collective-permute-start(bf16[56,3072]{1,0:T(8,128)(2,1)S(1)} %get-tuple-element.73), channel_id=1, source_target_pairs={{0,2},{2,0},{4,6},{6,4},{1,3},{3,1},{5,7},{7,5},{8,10},{10,8},{12,... | collective-permute-start | bytes 1032200 | tf_op jit(solution)/shard_map/ppermute | solution.py:120
  132.4 13.0 %collective-permute-start.27 = (bf16[56,3072]{1,0:T(8,128)(2,1)S(1)}, bf16[56,3072]{1,0:T(8,128)(2,1)S(1)}, u32[]{:S(2)}, u32[]{:S(2)}) collective-permute-start(bf16[56,3072]{1,0:T(8,128)(2,1)S(1)} %get-tuple-element.72), channel_id=1, source_target_pairs={{2,4},{4,2},{3,5},{5,3},{10,12},{12,10},{11,13},{13,11},{18,20},{2... | collective-permute-start | bytes 1032200 | tf_op jit(solution)/shard_map/ppermute | solution.py:120
  142.6 13.7 %collective-permute-start.29 = (bf16[56,3072]{1,0:T(8,128)(2,1)S(1)}, bf16[56,3072]{1,0:T(8,128)(2,1)S(1)}, u32[]{:S(2)}, u32[]{:S(2)}) collective-permute-start(bf16[56,3072]{1,0:T(8,128)(2,1)S(1)} %get-tuple-element.70), channel_id=1, source_target_pairs={{0,2},{2,0},{4,6},{6,4},{1,3},{3,1},{5,7},{7,5},{8,10},{10,8},{12,... | collective-permute-start | bytes 1032200 | tf_op jit(solution)/shard_map/ppermute | solution.py:120
  144.5 11.8 %collective-permute-start.31 = (bf16[56,3072]{1,0:T(8,128)(2,1)S(1)}, bf16[56,3072]{1,0:T(8,128)(2,1)S(1)}, u32[]{:S(2)}, u32[]{:S(2)}) collective-permute-start(bf16[56,3072]{1,0:T(8,128)(2,1)S(1)} %get-tuple-element.71), channel_id=1, source_target_pairs={{2,4},{4,2},{3,5},{5,3},{10,12},{12,10},{11,13},{13,11},{18,20},{2... | collective-permute-start | bytes 1032200 | tf_op jit(solution)/shard_map/ppermute | solution.py:120
  145.5 22.7 %collective-permute-start.38 = (bf16[56,3072]{1,0:T(8,128)(2,1)S(1)}, bf16[56,3072]{1,0:T(8,128)(2,1)S(1)}, u32[]{:S(2)}, u32[]{:S(2)}) collective-permute-start(bf16[56,3072]{1,0:T(8,128)(2,1)S(1)} %fusion.39), channel_id=1, source_target_pairs={{2,4},{4,2},{3,5},{5,3},{10,12},{12,10},{11,13},{13,11},{18,20},{2... | collective-permute-start | bytes 1032200 | tf_op jit(solution)/shard_map/ppermute | solution.py:120
  146.4 23.7 %collective-permute-start.37 = (bf16[56,3072]{1,0:T(8,128)(2,1)S(1)}, bf16[56,3072]{1,0:T(8,128)(2,1)S(1)}, u32[]{:S(2)}, u32[]{:S(2)}) collective-permute-start(bf16[56,3072]{1,0:T(8,128)(2,1)S(1)} %fusion.39), channel_id=1, source_target_pairs={{0,2},{2,0},{4,6},{6,4},{1,3},{3,1},{5,7},{7,5},{8,10},{10,8},{12,... | collective-permute-start | bytes 1032200 | tf_op jit(solution)/shard_map/ppermute | solution.py:120
  160.1 10.8 %collective-permute-start.34 = (bf16[2,56,576]{2,1,0:T(8,128)(2,1)}, bf16[2,56,576]{2,1,0:T(8,128)(2,1)}, u32[]{:S(2)}, u32[]{:S(2)}) collective-permute-start(bf16[2,56,576]{2,1,0:T(8,128)(2,1)} %get-tuple-element.109), channel_id=1, source_target_pairs={{0,8},{16,24},{1,9},{17,25},{2,10},{18,26},{3,11},{19,27},{4,12},{... | collective-permute-start | bytes 387080 | tf_op jit(solution)/shard_map/ppermute | solution.py:200
  170.1 10.9 %collective-permute-start.42 = (bf16[56,3072]{1,0:T(8,128)(2,1)S(1)}, bf16[56,3072]{1,0:T(8,128)(2,1)S(1)}, u32[]{:S(2)}, u32[]{:S(2)}) collective-permute-start(bf16[56,3072]{1,0:T(8,128)(2,1)S(1)} %fusion.35), channel_id=1, source_target_pairs={{0,2},{2,0},{4,6},{6,4},{1,3},{3,1},{5,7},{7,5},{8,10},{10,8},{12,... | collective-permute-start | bytes 1032200 | tf_op jit(solution)/shard_map/ppermute | solution.py:120
  170.2 11.5 %collective-permute-start.43 = (bf16[56,3072]{1,0:T(8,128)(2,1)S(1)}, bf16[56,3072]{1,0:T(8,128)(2,1)S(1)}, u32[]{:S(2)}, u32[]{:S(2)}) collective-permute-start(bf16[56,3072]{1,0:T(8,128)(2,1)S(1)} %fusion.35), channel_id=1, source_target_pairs={{2,4},{4,2},{3,5},{5,3},{10,12},{12,10},{11,13},{13,11},{18,20},{2... | collective-permute-start | bytes 1032200 | tf_op jit(solution)/shard_map/ppermute | solution.py:120
  170.9 17.5 %collective-permute-start.41 = (bf16[56,3072]{1,0:T(8,128)(2,1)S(1)}, bf16[56,3072]{1,0:T(8,128)(2,1)S(1)}, u32[]{:S(2)}, u32[]{:S(2)}) collective-permute-start(bf16[56,3072]{1,0:T(8,128)(2,1)S(1)} %collective-permute-done.38), channel_id=1, source_target_pairs={{2,0},{4,6},{3,1},{5,7},{10,8},{12,14},{11,9},{13,15},{18,16},{20,... | collective-permute-start | bytes 1032200 | tf_op jit(solution)/shard_map/ppermute | solution.py:120
  181.8 14.1 %collective-permute-start.46 = (bf16[56,3072]{1,0:T(8,128)(2,1)S(1)}, bf16[56,3072]{1,0:T(8,128)(2,1)S(1)}, u32[]{:S(2)}, u32[]{:S(2)}) collective-permute-start(bf16[56,3072]{1,0:T(8,128)(2,1)S(1)} %collective-permute-done.43), channel_id=1, source_target_pairs={{2,0},{4,6},{3,1},{5,7},{10,8},{12,14},{11,9},{13,15},{18,16},{20,... | collective-permute-start | bytes 1032200 | tf_op jit(solution)/shard_map/ppermute | solution.py:120
  183.1 20.1 %collective-permute-start.40 = (bf16[56,3072]{1,0:T(8,128)(2,1)S(1)}, bf16[56,3072]{1,0:T(8,128)(2,1)S(1)}, u32[]{:S(2)}, u32[]{:S(2)}) collective-permute-start(bf16[56,3072]{1,0:T(8,128)(2,1)S(1)} %collective-permute-done.39), channel_id=1, source_target_pairs={{2,0},{4,6},{3,1},{5,7},{10,8},{12,14},{11,9},{13,15},{18,16},{20,... | collective-permute-start | bytes 1032200 | tf_op jit(solution)/shard_map/ppermute | solution.py:120
  188.5 28.7 %collective-permute-start.45 = (bf16[56,3072]{1,0:T(8,128)(2,1)S(1)}, bf16[56,3072]{1,0:T(8,128)(2,1)S(1)}, u32[]{:S(2)}, u32[]{:S(2)}) collective-permute-start(bf16[56,3072]{1,0:T(8,128)(2,1)S(1)} %collective-permute-done.44), channel_id=1, source_target_pairs={{2,0},{4,6},{3,1},{5,7},{10,8},{12,14},{11,9},{13,15},{18,16},{20,... | collective-permute-start | bytes 1032200 | tf_op jit(solution)/shard_map/ppermute | solution.py:120
  (32 other events, 348.4 us)

commit v3 on v2

--- a/solution.py
+++ b/solution.py
@@ -28,8 +28,9 @@
 
     swaps = ring & (ring - 1) == 0
 
-    def exchanged(group):
-        block = own_rows[group * rows : (group + 1) * rows]
+    def exchanged():
+        share = own_rows.shape[0] // cores
+        block = lax.dynamic_slice_in_dim(own_rows, core * share, share, axis=0)
         parts = []
         for k in range(ring):
             to = z ^ k if swaps else (z + k) % ring
@@ -38,14 +39,15 @@
                 pairs = [(i, i ^ k if swaps else (i + k) % ring) for i in range(ring)]
                 part = lax.ppermute(part, "feat", pairs)
             parts.append(part)
-        if swaps:
-            both = jnp.stack(parts)
-            parts = [
-                lax.dynamic_index_in_dim(both, z ^ ((z - k) % ring), axis=0, keepdims=False) for k in range(ring)
-            ]
-        return jnp.concatenate(parts, axis=0)
-
-    columns = [exchanged(group) for group in range(GROUPS)]
+        every = lax.all_gather(jnp.stack(parts), "tok", axis=1, tiled=True)
+        order = [z ^ ((z - k) % ring) if swaps else k for k in range(ring)]
+        every = [lax.dynamic_index_in_dim(every, i, axis=0, keepdims=False) for i in order]
+        return [
+            jnp.concatenate([part[group * rows : (group + 1) * rows] for part in every], axis=0)
+            for group in range(GROUPS)
+        ]
+
+    columns = exchanged()
 
     def partial_sums(group, chunk):
         part = jnp.dot(
@@ -79,7 +81,7 @@
 
         def piece(layer):
             def run(sent):
-                all_codes = after(codes_of[0], [sent, residuals.get(group - 1)])
+                all_codes = after(codes_of[0], sent)
                 out = lax.dot_general(
                     all_codes,
                     decoders[layer, :, chunk * width : (chunk + 1) * width],
@@ -89,7 +91,11 @@
                 key = group, layer
                 decoded[key] = out if key not in decoded else decoded[key] + out
                 left[group].remove((chunk, layer))
-                if not left[group]:
+                if group < GROUPS - 1:
+                    if not left[group]:
+                        waiting.extend([(lambda sent: scatter_cores(group, sent), True), (wait, True)])
+                        waiting.append((lambda sent: scatter_segments(group, sent), True))
+                elif not left[group]:
                     waiting.append((lambda sent: share_segments(group, sent), True))
                 elif all(other == 0 for _, other in left[group]) and layer:
                     waiting.insert(0, (lambda sent: share_cores(group, sent), True))
@@ -166,6 +172,24 @@
                 return True
             return not (i == n and k == ring - 2)
 
+    def wait(sent):
+        return sent
+
+    def scatter_cores(group, sent):
+        blocks = after([decoded[group, layer] for layer in range(layers)], sent)
+        blocks = jnp.stack([jnp.where(layer >= segment, blocks[layer], 0.0) for layer in range(layers)])
+        blocks = blocks.astype(BF16).reshape(layers, ring, rows, depth)
+        blocks = jnp.stack(
+            [lax.dynamic_index_in_dim(blocks, (z - b) % ring, axis=1, keepdims=False) for b in range(ring)], axis=1
+        )
+        totals[group] = lax.psum_scatter(blocks, "tok", scatter_dimension=1, tiled=True)
+        return blocks
+
+    def scatter_segments(group, sent):
+        total = after(totals[group], sent)
+        residuals[group] = lax.psum_scatter(total, "segment", scatter_dimension=0, tiled=True)[0].astype(F32)
+        return total
+
     def share_cores(group, sent, first=1):
         blocks = after([decoded[group, layer] for layer in range(first, layers if first else 1)], sent)
         blocks = jnp.stack(blocks).reshape(-1, ring, rows, depth)

time: 245 us -> 257 us (1.049)
  between operations: 1.59 us -> 15.8 us
  matrix products: 57 us -> 49 us
  starting transfers between devices: 108 us -> 100 us
  waiting for transfers between devices: 63.1 us -> 70.3 us
    unnamed x0 -> x4, waiting for transfers between devices: none -> 12.1 us
    dot_general x16, matrix products: 49.9 us -> 41.8 us  [run(): lax.dot_general(all_codes, decoders[layer, :, chunk * width:(chunk + 1) *...]
    ppermute x6 -> x3, starting transfers between devices: 15.4 us -> 8.41 us  [share_segments(): lax.ppermute(given[-1], 'segment', [(i, j) for i, j in pairs if i < j < s...]
    ppermute x6 -> x3, starting transfers between devices: 10.1 us -> 5.6 us  [exchanged(): part = lax.ppermute(part, 'feat', pairs)]
    ppermute x36, starting transfers between devices: 81.9 us -> 86.2 us  [swap(): return lax.ppermute(value, 'feat', pairs) if pairs else None]
    ppermute x6 -> x3, waiting for transfers between devices: 5.95 us -> 3.63 us  [share_segments(): lax.ppermute(given[-1], 'segment', [(i, j) for i, j in pairs if i < j < s...]
    ppermute x6 -> x3, waiting for transfers between devices: 7.48 us -> 5.5 us  [exchanged(): part = lax.ppermute(part, 'feat', pairs)]
  transfers between devices with their start and end apart: 52 -> 46, of which waited for: 16 -> 16; matrix products, arithmetic and copies ran while one was open for 21% -> 22% of each run, Pallas kernels for 0% -> 0%
where the time goes in v3:
time: 257 us; the launch traced here: 256 us
  starting transfers between devices  100 us (39%)
  waiting for transfers between devices  70.3 us (27%)
  matrix products  49 us (19%)
  between operations  15.8 us (6%)
  other arithmetic  11.3 us (4%)
  blocking collectives  4.68 us (2%)
  local copies, waits for them, and re-layouts  4.65 us (2%)
    ppermute x36, starting transfers between devices, swap(): return lax.ppermute(value, 'feat', pairs) if pairs else None  86.2 us
    ppermute x36, waiting for transfers between devices, swap(): return lax.ppermute(value, 'feat', pairs) if pairs else None  48.9 us
    dot_general x16, matrix products, run(): lax.dot_general(all_codes, decoders[layer, :, chunk * width:(chunk + 1) *...  41.8 us
    unnamed x4, waiting for transfers between devices  12.1 us
    ppermute x3, starting transfers between devices, share_segments(): lax.ppermute(given[-1], 'segment', [(i, j) for i, j in pairs if i < j < s...  8.41 us
    dot_general x4, matrix products, partial_sums(): jnp.dot(columns[group], weight[:, chunk * width:(chunk + 1) * width], pre...  7.17 us
    ppermute x3, starting transfers between devices, exchanged(): part = lax.ppermute(part, 'feat', pairs)  5.6 us
    ppermute x3, waiting for transfers between devices, exchanged(): part = lax.ppermute(part, 'feat', pairs)  5.5 us
  transfers between devices with their start and end apart: 46, of which 16 were waited for; matrix products, arithmetic and copies ran while one was open for 22% of the time, Pallas kernels for 0%

profile of v3, /device:TPU:0, one launch (start us, length us, event | category | flops | bytes accessed | tf_op | source)
XLA Modules:
  0.0 256.2 jit_solution(14218802033499421697)
XLA Ops:
  9.9 3.0 %collective-permute-start = (bf16[56,576]{1,0:T(8,128)(2,1)S(1)}, bf16[56,576]{1,0:T(8,128)(2,1)S(1)}, u32[]{:S(2)}, u32[]{:S(2)}) collective-permute-start(bf16[56,576]{1,0:T(8,128)(2,1)S(1)} %get-tuple-element.117), channel_id=1, source_target_pairs={{0,2},{2,0},{4,6},{6,4},{1,3},{3,1},{5,7},{7,5},{8,10},{10,8},{12,... | collective-permute-start | bytes 193544 | tf_op jit(solution)/shard_map/ppermute | solution.py:40
  12.9 2.6 %collective-permute-start.1 = (bf16[56,576]{1,0:T(8,128)(2,1)S(1)}, bf16[56,576]{1,0:T(8,128)(2,1)S(1)}, u32[]{:S(2)}, u32[]{:S(2)}) collective-permute-start(bf16[56,576]{1,0:T(8,128)(2,1)S(1)} %get-tuple-element.116), channel_id=1, source_target_pairs={{0,4},{2,6},{4,0},{6,2},{1,5},{3,7},{5,1},{7,3},{8,12},{10,14},{12... | collective-permute-start | bytes 193544 | tf_op jit(solution)/shard_map/ppermute | solution.py:40
  16.2 4.6 %collective-permute-done.1 = bf16[56,576]{1,0:T(8,128)(2,1)S(1)} collective-permute-done((bf16[56,576]{1,0:T(8,128)(2,1)S(1)}, bf16[56,576]{1,0:T(8,128)(2,1)S(1)}, u32[]{:S(2)}, u32[]{:S(2)}) %collective-permute-start.1) | collective-permute-done | bytes 64544 | tf_op jit(solution)/shard_map/ppermute | solution.py:40
  24.1 3.4 %fusion.18 = f32[224,3072]{1,0:T(8,128)S(1)} fusion(bf16[576,6144]{1,0:T(8,128)(2,1)} %bitcast.162, bf16[56,576]{1,0:T(8,128)(2,1)S(1)} %get-tuple-element.108, bf16[56,576]{1,0:T(8,128)(2,1)S(1)} %get-tuple-element.109, bf16[56,576]{1,0:T(8,128)(2,1)S(1)} %get-tuple-element.110, bf16[56,576]{1,0:T(8,128)(2,1)S(1)} %get-tuple-element.107), kind=kOutput, calls=%fused_computation.26 | convolution fusion | flops 793755648 | bytes 6549504 | tf_op jit(solution)/shard_map/dot_general | solution.py:53
  29.6 3.5 %collective-permute-start.8 = (bf16[56,3072]{1,0:T(8,128)(2,1)S(1)}, bf16[56,3072]{1,0:T(8,128)(2,1)S(1)}, u32[]{:S(2)}, u32[]{:S(2)}) collective-permute-start(bf16[56,3072]{1,0:T(8,128)(2,1)S(1)} %get-tuple-element.82), channel_id=1, source_target_pairs={{0,2},{6,4},{1,3},{7,5},{8,10},{14,12},{9,11},{15,13},{16,18},{22,... | collective-permute-start | bytes 1032200 | tf_op jit(solution)/shard_map/ppermute | solution.py:126
  42.3 13.9 %collective-permute-done.3 = bf16[56,3072]{1,0:T(8,128)(2,1)S(1)} collective-permute-done((bf16[56,3072]{1,0:T(8,128)(2,1)S(1)}, bf16[56,3072]{1,0:T(8,128)(2,1)S(1)}, u32[]{:S(2)}, u32[]{:S(2)}) %collective-permute-start.3) | collective-permute-done | bytes 344096 | tf_op jit(solution)/shard_map/ppermute | solution.py:126
  57.3 5.3 %collective-permute-start.10 = (bf16[56,3072]{1,0:T(8,128)(2,1)S(1)}, bf16[56,3072]{1,0:T(8,128)(2,1)S(1)}, u32[]{:S(2)}, u32[]{:S(2)}) collective-permute-start(bf16[56,3072]{1,0:T(8,128)(2,1)S(1)} %get-tuple-element.80), channel_id=1, source_target_pairs={{0,2},{2,0},{4,6},{6,4},{1,3},{3,1},{5,7},{7,5},{8,10},{10,8},{12,... | collective-permute-start | bytes 1032200 | tf_op jit(solution)/shard_map/ppermute | solution.py:126
  63.8 8.2 %collective-permute-start.5 = (bf16[56,3072]{1,0:T(8,128)(2,1)S(1)}, bf16[56,3072]{1,0:T(8,128)(2,1)S(1)}, u32[]{:S(2)}, u32[]{:S(2)}) collective-permute-start(bf16[56,3072]{1,0:T(8,128)(2,1)S(1)} %get-tuple-element.76), channel_id=1, source_target_pairs={{0,2},{2,0},{4,6},{6,4},{1,3},{3,1},{5,7},{7,5},{8,10},{10,8},{12,... | collective-permute-start | bytes 1032200 | tf_op jit(solution)/shard_map/ppermute | solution.py:126
  73.6 9.2 %collective-permute-start.19 = (bf16[56,3072]{1,0:T(8,128)(2,1)S(1)}, bf16[56,3072]{1,0:T(8,128)(2,1)S(1)}, u32[]{:S(2)}, u32[]{:S(2)}) collective-permute-start(bf16[56,3072]{1,0:T(8,128)(2,1)S(1)} %fusion.43), channel_id=1, source_target_pairs={{0,2},{2,0},{4,6},{6,4},{1,3},{3,1},{5,7},{7,5},{8,10},{10,8},{12,... | collective-permute-start | bytes 1032200 | tf_op jit(solution)/shard_map/ppermute | solution.py:126
  83.8 6.6 %collective-permute-start.16 = (bf16[56,3072]{1,0:T(8,128)(2,1)S(1)}, bf16[56,3072]{1,0:T(8,128)(2,1)S(1)}, u32[]{:S(2)}, u32[]{:S(2)}) collective-permute-start(bf16[56,3072]{1,0:T(8,128)(2,1)S(1)} %fusion.47), channel_id=1, source_target_pairs={{0,2},{2,0},{4,6},{6,4},{1,3},{3,1},{5,7},{7,5},{8,10},{10,8},{12,... | collective-permute-start | bytes 1032200 | tf_op jit(solution)/shard_map/ppermute | solution.py:126
  90.5 3.5 %collective-permute-start.22 = (bf16[56,3072]{1,0:T(8,128)(2,1)S(1)}, bf16[56,3072]{1,0:T(8,128)(2,1)S(1)}, u32[]{:S(2)}, u32[]{:S(2)}) collective-permute-start(bf16[56,3072]{1,0:T(8,128)(2,1)S(1)} %add_convert_fusion.5), channel_id=1, source_target_pairs={{0,2},{2,0},{4,6},{6,4},{1,3},{3,1},{5,7},{7,5},{8,10},{10,8},{12,... | collective-permute-start | bytes 1032200 | tf_op jit(solution)/shard_map/ppermute | solution.py:126
  94.1 5.3 %collective-permute-done.16 = bf16[56,3072]{1,0:T(8,128)(2,1)S(1)} collective-permute-done((bf16[56,3072]{1,0:T(8,128)(2,1)S(1)}, bf16[56,3072]{1,0:T(8,128)(2,1)S(1)}, u32[]{:S(2)}, u32[]{:S(2)}) %collective-permute-start.16) | collective-permute-done | bytes 344096 | tf_op jit(solution)/shard_map/ppermute | solution.py:126
  102.4 4.0 %collective-permute-done.22 = bf16[56,3072]{1,0:T(8,128)(2,1)S(1)} collective-permute-done((bf16[56,3072]{1,0:T(8,128)(2,1)S(1)}, bf16[56,3072]{1,0:T(8,128)(2,1)S(1)}, u32[]{:S(2)}, u32[]{:S(2)}) %collective-permute-start.22) | collective-permute-done | bytes 344096 | tf_op jit(solution)/shard_map/ppermute | solution.py:126
  111.2 6.6 %collective-permute-start.18 = (bf16[56,3072]{1,0:T(8,128)(2,1)S(1)}, bf16[56,3072]{1,0:T(8,128)(2,1)S(1)}, u32[]{:S(2)}, u32[]{:S(2)}) collective-permute-start(bf16[56,3072]{1,0:T(8,128)(2,1)S(1)} %get-tuple-element.73), channel_id=1, source_target_pairs={{0,2},{2,0},{4,6},{6,4},{1,3},{3,1},{5,7},{7,5},{8,10},{10,8},{12,... | collective-permute-start | bytes 1032200 | tf_op jit(solution)/shard_map/ppermute | solution.py:126
  118.0 4.2 %collective-permute-start.27 = (bf16[56,3072]{1,0:T(8,128)(2,1)S(1)}, bf16[56,3072]{1,0:T(8,128)(2,1)S(1)}, u32[]{:S(2)}, u32[]{:S(2)}) collective-permute-start(bf16[56,3072]{1,0:T(8,128)(2,1)S(1)} %add_convert_fusion.6), channel_id=1, source_target_pairs={{0,2},{2,0},{4,6},{6,4},{1,3},{3,1},{5,7},{7,5},{8,10},{10,8},{12,... | collective-permute-start | bytes 1032200 | tf_op jit(solution)/shard_map/ppermute | solution.py:126
  127.2 8.5 %collective-permute-start.23 = (bf16[56,3072]{1,0:T(8,128)(2,1)S(1)}, bf16[56,3072]{1,0:T(8,128)(2,1)S(1)}, u32[]{:S(2)}, u32[]{:S(2)}) collective-permute-start(bf16[56,3072]{1,0:T(8,128)(2,1)S(1)} %get-tuple-element.69), channel_id=1, source_target_pairs={{0,2},{2,0},{4,6},{6,4},{1,3},{3,1},{5,7},{7,5},{8,10},{10,8},{12,... | collective-permute-start | bytes 1032200 | tf_op jit(solution)/shard_map/ppermute | solution.py:126
  144.9 4.7 %collective-permute-start.31 = (bf16[56,3072]{1,0:T(8,128)(2,1)S(1)}, bf16[56,3072]{1,0:T(8,128)(2,1)S(1)}, u32[]{:S(2)}, u32[]{:S(2)}) collective-permute-start(bf16[56,3072]{1,0:T(8,128)(2,1)S(1)} %fusion.39), channel_id=1, source_target_pairs={{0,2},{2,0},{4,6},{6,4},{1,3},{3,1},{5,7},{7,5},{8,10},{10,8},{12,... | collective-permute-start | bytes 1032200 | tf_op jit(solution)/shard_map/ppermute | solution.py:126
  163.1 3.8 %collective-permute-done.32 = bf16[56,3072]{1,0:T(8,128)(2,1)} collective-permute-done((bf16[56,3072]{1,0:T(8,128)(2,1)S(1)}, bf16[56,3072]{1,0:T(8,128)(2,1)}, u32[]{:S(2)}, u32[]{:S(2)}) %collective-permute-start.32) | collective-permute-done | bytes 344096 | tf_op jit(solution)/shard_map/ppermute | solution.py:126
  168.9 5.2 %collective-permute-done.35 = bf16[56,3072]{1,0:T(8,128)(2,1)S(1)} collective-permute-done((bf16[56,3072]{1,0:T(8,128)(2,1)S(1)}, bf16[56,3072]{1,0:T(8,128)(2,1)S(1)}, u32[]{:S(2)}, u32[]{:S(2)}) %collective-permute-start.35) | collective-permute-done | bytes 344096 | tf_op jit(solution)/shard_map/ppermute | solution.py:126
  174.1 12.0 %all-reduce.4.cloned.1.call-done = bf16[4,4,56,576]{3,2,1,0:T(8,128)(2,1)} async-done(((bf16[4,4,56,576]{3,2,1,0:T(8,128)(2,1)}), bf16[4,4,56,576]{3,2,1,0:T(8,128)(2,1)}) %all-reduce.4.cloned.1.call-update) | async-done | bytes 1032208
  190.7 10.2 %collective-permute-done.34 = bf16[56,3072]{1,0:T(8,128)(2,1)} collective-permute-done((bf16[56,3072]{1,0:T(8,128)(2,1)S(1)}, bf16[56,3072]{1,0:T(8,128)(2,1)}, u32[]{:S(2)}, u32[]{:S(2)}) %collective-permute-start.34) | collective-permute-done | bytes 344096 | tf_op jit(solution)/shard_map/ppermute | solution.py:126
  202.2 3.5 %fusion = f32[224,576]{1,0:T(8,128)S(1)} fusion(bf16[224,3072]{1,0:T(8,128)(2,1)S(1)} %pad_maximum_fusion.3, bf16[4,576,6144]{2,1,0:T(8,128)(2,1)} %bitcast.144), kind=kOutput, calls=%fused_computation.8 | convolution fusion | flops 792723456 | bytes 5431296 | tf_op jit(solution)/shard_map/dot_general | solution.py:85
  208.8 3.5 %fusion.27 = f32[224,576]{1,0:T(8,128)S(1)} fusion(f32[224,576]{1,0:T(8,128)S(1)} %fusion, bf16[4,576,6144]{2,1,0:T(8,128)(2,1)} %bitcast.145, bf16[56,3072]{1,0:T(8,128)(2,1)S(1)} %get-tuple-element.97, bf16[56,3072]{1,0:T(8,128)(2,1)S(1)} %select_select_fusion.1, bf16[56,3072]{1,0:T(8,128)(2,1)S(1)} %get-tuple-element.96, bf16[56,3072]{1,0:T(8,128)(2,1)S(1)} %fusion.35), kind=kOutput, calls=%fused_computation.41 | convolution fusion | flops 798357504 | bytes 5947392 | tf_op jit(solution)/shard_map/dot_general | solution.py:85
  212.3 3.5 %fusion.4 = f32[224,576]{1,0:T(8,128)S(1)} fusion(bf16[4,576,6144]{2,1,0:T(8,128)(2,1)} %bitcast.146, bf16[56,3072]{1,0:T(8,128)(2,1)S(1)} %get-tuple-element.99, bf16[56,3072]{1,0:T(8,128)(2,1)S(1)} %select_select_fusion.4, bf16[56,3072]{1,0:T(8,128)(2,1)S(1)} %get-tuple-element.98, bf16[56,3072]{1,0:T(8,128)(2,1)S(1)} %fusion.39), kind=kOutput, calls=%fused_computation.12 | convolution fusion | flops 798228480 | bytes 5431296 | tf_op jit(solution)/shard_map/dot_general | solution.py:85
  215.8 3.5 %fusion.31 = f32[224,576]{1,0:T(8,128)S(1)} fusion(f32[224,576]{1,0:T(8,128)S(1)} %fusion.4, bf16[4,576,6144]{2,1,0:T(8,128)(2,1)} %bitcast.147, bf16[56,3072]{1,0:T(8,128)(2,1)S(1)} %get-tuple-element.97, bf16[56,3072]{1,0:T(8,128)(2,1)S(1)} %select_select_fusion.1, bf16[56,3072]{1,0:T(8,128)(2,1)S(1)} %get-tuple-element.96, bf16[56,3072]{1,0:T(8,128)(2,1)S(1)} %fusion.35), kind=kOutput, calls=%fused_computation.45 | convolution fusion | flops 798357504 | bytes 5947392 | tf_op jit(solution)/shard_map/dot_general | solution.py:85
  219.3 3.4 %fusion.2 = f32[224,576]{1,0:T(8,128)S(1)} fusion(bf16[224,3072]{1,0:T(8,128)(2,1)S(1)} %pad_maximum_fusion.3, bf16[4,576,6144]{2,1,0:T(8,128)(2,1)} %bitcast.148), kind=kOutput, calls=%fused_computation.10 | convolution fusion | flops 792723456 | bytes 5431296 | tf_op jit(solution)/shard_map/dot_general | solution.py:85
  222.7 3.5 %fusion.25 = f32[224,576]{1,0:T(8,128)S(1)} fusion(f32[224,576]{1,0:T(8,128)S(1)} %fusion.2, bf16[224,3072]{1,0:T(8,128)(2,1)S(1)} %pad_maximum_fusion.4, bf16[4,576,6144]{2,1,0:T(8,128)(2,1)} %bitcast.149), kind=kOutput, calls=%fused_computation.39 | convolution fusion | flops 792852480 | bytes 5947392 | tf_op jit(solution)/shard_map/dot_general | solution.py:85
  226.6 3.4 %fusion.6 = f32[224,576]{1,0:T(8,128)S(1)} fusion(bf16[224,3072]{1,0:T(8,128)(2,1)S(1)} %pad_maximum_fusion.3, bf16[4,576,6144]{2,1,0:T(8,128)(2,1)} %bitcast.150), kind=kOutput, calls=%fused_computation.14 | convolution fusion | flops 792723456 | bytes 5431296 | tf_op jit(solution)/shard_map/dot_general | solution.py:85
  230.1 3.5 %fusion.29 = f32[224,576]{1,0:T(8,128)S(1)} fusion(f32[224,576]{1,0:T(8,128)S(1)} %fusion.6, bf16[4,576,6144]{2,1,0:T(8,128)(2,1)} %bitcast.151, bf16[56,3072]{1,0:T(8,128)(2,1)S(1)} %get-tuple-element.97, bf16[56,3072]{1,0:T(8,128)(2,1)S(1)} %select_select_fusion.1, bf16[56,3072]{1,0:T(8,128)(2,1)S(1)} %get-tuple-element.96, bf16[56,3072]{1,0:T(8,128)(2,1)S(1)} %fusion.35), kind=kOutput, calls=%fused_computation.43 | convolution fusion | flops 798357504 | bytes 5947392 | tf_op jit(solution)/shard_map/dot_general | solution.py:85
  233.7 3.7 %collective-permute-start.41 = (bf16[2,56,576]{2,1,0:T(8,128)(2,1)S(1)}, bf16[2,56,576]{2,1,0:T(8,128)(2,1)S(1)}, u32[]{:S(2)}, u32[]{:S(2)}) collective-permute-start(bf16[2,56,576]{2,1,0:T(8,128)(2,1)S(1)} %get-tuple-element.102), channel_id=1, source_target_pairs={{0,8},{16,24},{1,9},{17,25},{2,10},{18,26},{3,11},{19,27},{4,12},{... | collective-permute-start | bytes 387080 | tf_op jit(solution)/shard_map/ppermute | solution.py:224
  237.5 3.4 %collective-permute-start.42 = (bf16[2,56,576]{2,1,0:T(8,128)(2,1)S(1)}, bf16[2,56,576]{2,1,0:T(8,128)(2,1)S(1)}, u32[]{:S(2)}, u32[]{:S(2)}) collective-permute-start(bf16[2,56,576]{2,1,0:T(8,128)(2,1)S(1)} %get-tuple-element.101), channel_id=1, source_target_pairs={{0,16},{8,24},{1,17},{9,25},{2,18},{10,26},{3,19},{11,27},{4,20},{... | collective-permute-start | bytes 387080 | tf_op jit(solution)/shard_map/ppermute | solution.py:224
  243.7 3.6 %collective-permute-done.42 = bf16[2,56,576]{2,1,0:T(8,128)(2,1)S(1)} collective-permute-done((bf16[2,56,576]{2,1,0:T(8,128)(2,1)S(1)}, bf16[2,56,576]{2,1,0:T(8,128)(2,1)S(1)}, u32[]{:S(2)}, u32[]{:S(2)}) %collective-permute-start.42) | collective-permute-done | bytes 129056 | tf_op jit(solution)/shard_map/ppermute | solution.py:224
  (167 shorter events, 73.5 us)
Async XLA Ops:
  7.2 179.0 %all-reduce.4.cloned.1.call-start = ((), (), s32[]{:S(2)}) async-start(), calls=%async_computation.1 | async-start | bytes 2293760
  29.6 11.9 %collective-permute-start.8 = (bf16[56,3072]{1,0:T(8,128)(2,1)S(1)}, bf16[56,3072]{1,0:T(8,128)(2,1)S(1)}, u32[]{:S(2)}, u32[]{:S(2)}) collective-permute-start(bf16[56,3072]{1,0:T(8,128)(2,1)S(1)} %get-tuple-element.82), channel_id=1, source_target_pairs={{0,2},{6,4},{1,3},{7,5},{8,10},{14,12},{9,11},{15,13},{16,18},{22,... | collective-permute-start | bytes 1032200 | tf_op jit(solution)/shard_map/ppermute | solution.py:126
  33.1 24.0 %collective-permute-start.11 = (bf16[56,3072]{1,0:T(8,128)(2,1)S(1)}, bf16[56,3072]{1,0:T(8,128)(2,1)S(1)}, u32[]{:S(2)}, u32[]{:S(2)}) collective-permute-start(bf16[56,3072]{1,0:T(8,128)(2,1)S(1)} %get-tuple-element.83), channel_id=1, source_target_pairs={{0,2},{6,4},{1,3},{7,5},{8,10},{14,12},{9,11},{15,13},{16,18},{22,... | collective-permute-start | bytes 1032200 | tf_op jit(solution)/shard_map/ppermute | solution.py:126
  34.6 21.6 %collective-permute-start.3 = (bf16[56,3072]{1,0:T(8,128)(2,1)S(1)}, bf16[56,3072]{1,0:T(8,128)(2,1)S(1)}, u32[]{:S(2)}, u32[]{:S(2)}) collective-permute-start(bf16[56,3072]{1,0:T(8,128)(2,1)S(1)} %get-tuple-element.78), channel_id=1, source_target_pairs={{0,2},{6,4},{1,3},{7,5},{8,10},{14,12},{9,11},{15,13},{16,18},{22,... | collective-permute-start | bytes 1032200 | tf_op jit(solution)/shard_map/ppermute | solution.py:126
  35.9 27.7 %collective-permute-start.6 = (bf16[56,3072]{1,0:T(8,128)(2,1)S(1)}, bf16[56,3072]{1,0:T(8,128)(2,1)S(1)}, u32[]{:S(2)}, u32[]{:S(2)}) collective-permute-start(bf16[56,3072]{1,0:T(8,128)(2,1)S(1)} %get-tuple-element.79), channel_id=1, source_target_pairs={{0,2},{6,4},{1,3},{7,5},{8,10},{14,12},{9,11},{15,13},{16,18},{22,... | collective-permute-start | bytes 1032200 | tf_op jit(solution)/shard_map/ppermute | solution.py:126
  41.6 15.5 %collective-permute-start.9 = (bf16[56,3072]{1,0:T(8,128)(2,1)S(1)}, bf16[56,3072]{1,0:T(8,128)(2,1)S(1)}, u32[]{:S(2)}, u32[]{:S(2)}) collective-permute-start(bf16[56,3072]{1,0:T(8,128)(2,1)S(1)} %add_convert_fusion.14), channel_id=1, source_target_pairs={{2,4},{4,2},{3,5},{5,3},{10,12},{12,10},{11,13},{13,11},{18,20},{2... | collective-permute-start | bytes 1032200 | tf_op jit(solution)/shard_map/ppermute | solution.py:126
  57.3 15.4 %collective-permute-start.10 = (bf16[56,3072]{1,0:T(8,128)(2,1)S(1)}, bf16[56,3072]{1,0:T(8,128)(2,1)S(1)}, u32[]{:S(2)}, u32[]{:S(2)}) collective-permute-start(bf16[56,3072]{1,0:T(8,128)(2,1)S(1)} %get-tuple-element.80), channel_id=1, source_target_pairs={{0,2},{2,0},{4,6},{6,4},{1,3},{3,1},{5,7},{7,5},{8,10},{10,8},{12,... | collective-permute-start | bytes 1032200 | tf_op jit(solution)/shard_map/ppermute | solution.py:126
  63.8 18.9 %collective-permute-start.5 = (bf16[56,3072]{1,0:T(8,128)(2,1)S(1)}, bf16[56,3072]{1,0:T(8,128)(2,1)S(1)}, u32[]{:S(2)}, u32[]{:S(2)}) collective-permute-start(bf16[56,3072]{1,0:T(8,128)(2,1)S(1)} %get-tuple-element.76), channel_id=1, source_target_pairs={{0,2},{2,0},{4,6},{6,4},{1,3},{3,1},{5,7},{7,5},{8,10},{10,8},{12,... | collective-permute-start | bytes 1032200 | tf_op jit(solution)/shard_map/ppermute | solution.py:126
  72.9 17.5 %collective-permute-start.21 = (bf16[56,3072]{1,0:T(8,128)(2,1)S(1)}, bf16[56,3072]{1,0:T(8,128)(2,1)S(1)}, u32[]{:S(2)}, u32[]{:S(2)}) collective-permute-start(bf16[56,3072]{1,0:T(8,128)(2,1)S(1)} %fusion.43), channel_id=1, source_target_pairs={{2,4},{4,2},{3,5},{5,3},{10,12},{12,10},{11,13},{13,11},{18,20},{2... | collective-permute-start | bytes 1032200 | tf_op jit(solution)/shard_map/ppermute | solution.py:126
  73.6 28.8 %collective-permute-start.19 = (bf16[56,3072]{1,0:T(8,128)(2,1)S(1)}, bf16[56,3072]{1,0:T(8,128)(2,1)S(1)}, u32[]{:S(2)}, u32[]{:S(2)}) collective-permute-start(bf16[56,3072]{1,0:T(8,128)(2,1)S(1)} %fusion.43), channel_id=1, source_target_pairs={{0,2},{2,0},{4,6},{6,4},{1,3},{3,1},{5,7},{7,5},{8,10},{10,8},{12,... | collective-permute-start | bytes 1032200 | tf_op jit(solution)/shard_map/ppermute | solution.py:126
  82.9 11.1 %collective-permute-start.13 = (bf16[56,3072]{1,0:T(8,128)(2,1)S(1)}, bf16[56,3072]{1,0:T(8,128)(2,1)S(1)}, u32[]{:S(2)}, u32[]{:S(2)}) collective-permute-start(bf16[56,3072]{1,0:T(8,128)(2,1)S(1)} %fusion.47), channel_id=1, source_target_pairs={{2,4},{4,2},{3,5},{5,3},{10,12},{12,10},{11,13},{13,11},{18,20},{2... | collective-permute-start | bytes 1032200 | tf_op jit(solution)/shard_map/ppermute | solution.py:126
  83.8 15.6 %collective-permute-start.16 = (bf16[56,3072]{1,0:T(8,128)(2,1)S(1)}, bf16[56,3072]{1,0:T(8,128)(2,1)S(1)}, u32[]{:S(2)}, u32[]{:S(2)}) collective-permute-start(bf16[56,3072]{1,0:T(8,128)(2,1)S(1)} %fusion.47), channel_id=1, source_target_pairs={{0,2},{2,0},{4,6},{6,4},{1,3},{3,1},{5,7},{7,5},{8,10},{10,8},{12,... | collective-permute-start | bytes 1032200 | tf_op jit(solution)/shard_map/ppermute | solution.py:126
  90.5 15.9 %collective-permute-start.22 = (bf16[56,3072]{1,0:T(8,128)(2,1)S(1)}, bf16[56,3072]{1,0:T(8,128)(2,1)S(1)}, u32[]{:S(2)}, u32[]{:S(2)}) collective-permute-start(bf16[56,3072]{1,0:T(8,128)(2,1)S(1)} %add_convert_fusion.5), channel_id=1, source_target_pairs={{0,2},{2,0},{4,6},{6,4},{1,3},{3,1},{5,7},{7,5},{8,10},{10,8},{12,... | collective-permute-start | bytes 1032200 | tf_op jit(solution)/shard_map/ppermute | solution.py:126
  106.7 11.1 %collective-permute-start.20 = (bf16[56,3072]{1,0:T(8,128)(2,1)S(1)}, bf16[56,3072]{1,0:T(8,128)(2,1)S(1)}, u32[]{:S(2)}, u32[]{:S(2)}) collective-permute-start(bf16[56,3072]{1,0:T(8,128)(2,1)S(1)} %get-tuple-element.71), channel_id=1, source_target_pairs={{2,4},{4,2},{3,5},{5,3},{10,12},{12,10},{11,13},{13,11},{18,20},{2... | collective-permute-start | bytes 1032200 | tf_op jit(solution)/shard_map/ppermute | solution.py:126
  107.4 33.5 %collective-permute-start.25 = (bf16[56,3072]{1,0:T(8,128)(2,1)S(1)}, bf16[56,3072]{1,0:T(8,128)(2,1)S(1)}, u32[]{:S(2)}, u32[]{:S(2)}) collective-permute-start(bf16[56,3072]{1,0:T(8,128)(2,1)S(1)} %get-tuple-element.70), channel_id=1, source_target_pairs={{2,4},{4,2},{3,5},{5,3},{10,12},{12,10},{11,13},{13,11},{18,20},{2... | collective-permute-start | bytes 1032200 | tf_op jit(solution)/shard_map/ppermute | solution.py:126
  110.3 11.9 %collective-permute-start.15 = (bf16[56,3072]{1,0:T(8,128)(2,1)S(1)}, bf16[56,3072]{1,0:T(8,128)(2,1)S(1)}, u32[]{:S(2)}, u32[]{:S(2)}) collective-permute-start(bf16[56,3072]{1,0:T(8,128)(2,1)S(1)} %get-tuple-element.72), channel_id=1, source_target_pairs={{2,4},{4,2},{3,5},{5,3},{10,12},{12,10},{11,13},{13,11},{18,20},{2... | collective-permute-start | bytes 1032200 | tf_op jit(solution)/shard_map/ppermute | solution.py:126
  111.2 11.8 %collective-permute-start.18 = (bf16[56,3072]{1,0:T(8,128)(2,1)S(1)}, bf16[56,3072]{1,0:T(8,128)(2,1)S(1)}, u32[]{:S(2)}, u32[]{:S(2)}) collective-permute-start(bf16[56,3072]{1,0:T(8,128)(2,1)S(1)} %get-tuple-element.73), channel_id=1, source_target_pairs={{0,2},{2,0},{4,6},{6,4},{1,3},{3,1},{5,7},{7,5},{8,10},{10,8},{12,... | collective-permute-start | bytes 1032200 | tf_op jit(solution)/shard_map/ppermute | solution.py:126
  118.0 22.9 %collective-permute-start.27 = (bf16[56,3072]{1,0:T(8,128)(2,1)S(1)}, bf16[56,3072]{1,0:T(8,128)(2,1)S(1)}, u32[]{:S(2)}, u32[]{:S(2)}) collective-permute-start(bf16[56,3072]{1,0:T(8,128)(2,1)S(1)} %add_convert_fusion.6), channel_id=1, source_target_pairs={{0,2},{2,0},{4,6},{6,4},{1,3},{3,1},{5,7},{7,5},{8,10},{10,8},{12,... | collective-permute-start | bytes 1032200 | tf_op jit(solution)/shard_map/ppermute | solution.py:126
  127.2 16.8 %collective-permute-start.23 = (bf16[56,3072]{1,0:T(8,128)(2,1)S(1)}, bf16[56,3072]{1,0:T(8,128)(2,1)S(1)}, u32[]{:S(2)}, u32[]{:S(2)}) collective-permute-start(bf16[56,3072]{1,0:T(8,128)(2,1)S(1)} %get-tuple-element.69), channel_id=1, source_target_pairs={{0,2},{2,0},{4,6},{6,4},{1,3},{3,1},{5,7},{7,5},{8,10},{10,8},{12,... | collective-permute-start | bytes 1032200 | tf_op jit(solution)/shard_map/ppermute | solution.py:126
  141.1 14.4 %collective-permute-start.26 = (bf16[56,3072]{1,0:T(8,128)(2,1)S(1)}, bf16[56,3072]{1,0:T(8,128)(2,1)S(1)}, u32[]{:S(2)}, u32[]{:S(2)}) collective-permute-start(bf16[56,3072]{1,0:T(8,128)(2,1)S(1)} %get-tuple-element.66), channel_id=1, source_target_pairs={{0,2},{2,0},{4,6},{6,4},{1,3},{3,1},{5,7},{7,5},{8,10},{10,8},{12,... | collective-permute-start | bytes 1032200 | tf_op jit(solution)/shard_map/ppermute | solution.py:126
  143.1 12.4 %collective-permute-start.28 = (bf16[56,3072]{1,0:T(8,128)(2,1)S(1)}, bf16[56,3072]{1,0:T(8,128)(2,1)S(1)}, u32[]{:S(2)}, u32[]{:S(2)}) collective-permute-start(bf16[56,3072]{1,0:T(8,128)(2,1)S(1)} %get-tuple-element.67), channel_id=1, source_target_pairs={{2,4},{4,2},{3,5},{5,3},{10,12},{12,10},{11,13},{13,11},{18,20},{2... | collective-permute-start | bytes 1032200 | tf_op jit(solution)/shard_map/ppermute | solution.py:126
  144.2 15.4 %collective-permute-start.30 = (bf16[56,3072]{1,0:T(8,128)(2,1)S(1)}, bf16[56,3072]{1,0:T(8,128)(2,1)S(1)}, u32[]{:S(2)}, u32[]{:S(2)}) collective-permute-start(bf16[56,3072]{1,0:T(8,128)(2,1)S(1)} %fusion.39), channel_id=1, source_target_pairs={{2,4},{4,2},{3,5},{5,3},{10,12},{12,10},{11,13},{13,11},{18,20},{2... | collective-permute-start | bytes 1032200 | tf_op jit(solution)/shard_map/ppermute | solution.py:126
  144.9 14.7 %collective-permute-start.31 = (bf16[56,3072]{1,0:T(8,128)(2,1)S(1)}, bf16[56,3072]{1,0:T(8,128)(2,1)S(1)}, u32[]{:S(2)}, u32[]{:S(2)}) collective-permute-start(bf16[56,3072]{1,0:T(8,128)(2,1)S(1)} %fusion.39), channel_id=1, source_target_pairs={{0,2},{2,0},{4,6},{6,4},{1,3},{3,1},{5,7},{7,5},{8,10},{10,8},{12,... | collective-permute-start | bytes 1032200 | tf_op jit(solution)/shard_map/ppermute | solution.py:126
  155.7 11.2 %collective-permute-start.32 = (bf16[56,3072]{1,0:T(8,128)(2,1)S(1)}, bf16[56,3072]{1,0:T(8,128)(2,1)}, u32[]{:S(2)}, u32[]{:S(2)}) collective-permute-start(bf16[56,3072]{1,0:T(8,128)(2,1)S(1)} %fusion.35), channel_id=1, source_target_pairs={{0,2},{2,0},{4,6},{6,4},{1,3},{3,1},{5,7},{7,5},{8,10},{10,8},{12,... | collective-permute-start | bytes 1032200 | tf_op jit(solution)/shard_map/ppermute | solution.py:126
  156.3 11.2 %collective-permute-start.29 = (bf16[56,3072]{1,0:T(8,128)(2,1)S(1)}, bf16[56,3072]{1,0:T(8,128)(2,1)}, u32[]{:S(2)}, u32[]{:S(2)}) collective-permute-start(bf16[56,3072]{1,0:T(8,128)(2,1)S(1)} %fusion.35), channel_id=1, source_target_pairs={{2,4},{4,2},{3,5},{5,3},{10,12},{12,10},{11,13},{13,11},{18,20},{2... | collective-permute-start | bytes 1032200 | tf_op jit(solution)/shard_map/ppermute | solution.py:126
  159.6 14.5 %collective-permute-start.35 = (bf16[56,3072]{1,0:T(8,128)(2,1)S(1)}, bf16[56,3072]{1,0:T(8,128)(2,1)S(1)}, u32[]{:S(2)}, u32[]{:S(2)}) collective-permute-start(bf16[56,3072]{1,0:T(8,128)(2,1)S(1)} %collective-permute-done.30), channel_id=1, source_target_pairs={{2,0},{4,6},{3,1},{5,7},{10,8},{12,14},{11,9},{13,15},{18,16},{20,... | collective-permute-start | bytes 1032200 | tf_op jit(solution)/shard_map/ppermute | solution.py:126
  160.9 13.2 %collective-permute-start.33 = (bf16[56,3072]{1,0:T(8,128)(2,1)S(1)}, bf16[56,3072]{1,0:T(8,128)(2,1)S(1)}, u32[]{:S(2)}, u32[]{:S(2)}) collective-permute-start(bf16[56,3072]{1,0:T(8,128)(2,1)S(1)} %collective-permute-done.31), channel_id=1, source_target_pairs={{2,4},{4,2},{3,5},{5,3},{10,12},{12,10},{11,13},{13,11},{18,20},{2... | collective-permute-start | bytes 1032200 | tf_op jit(solution)/shard_map/ppermute | solution.py:126
  161.6 85.8 %reduce-scatter.5.cloned.1.call-start = ((), (), s32[]{:S(2)}) async-start(), calls=%async_computation.2 | async-start | bytes 716800
  166.9 22.5 %collective-permute-start.36 = (bf16[56,3072]{1,0:T(8,128)(2,1)}, bf16[56,3072]{1,0:T(8,128)(2,1)S(1)}, u32[]{:S(2)}, u32[]{:S(2)}) collective-permute-start(bf16[56,3072]{1,0:T(8,128)(2,1)} %collective-permute-done.32), channel_id=1, source_target_pairs={{2,4},{4,2},{3,5},{5,3},{10,12},{12,10},{11,13},{13,11},{18,20},{2... | collective-permute-start | bytes 1032200 | tf_op jit(solution)/shard_map/ppermute | solution.py:126
  167.6 21.8 %collective-permute-start.38 = (bf16[56,3072]{1,0:T(8,128)(2,1)}, bf16[56,3072]{1,0:T(8,128)(2,1)S(1)}, u32[]{:S(2)}, u32[]{:S(2)}) collective-permute-start(bf16[56,3072]{1,0:T(8,128)(2,1)} %collective-permute-done.29), channel_id=1, source_target_pairs={{2,0},{4,6},{3,1},{5,7},{10,8},{12,14},{11,9},{13,15},{18,16},{20,... | collective-permute-start | bytes 1032200 | tf_op jit(solution)/shard_map/ppermute | solution.py:126
  188.1 12.9 %collective-permute-start.34 = (bf16[56,3072]{1,0:T(8,128)(2,1)S(1)}, bf16[56,3072]{1,0:T(8,128)(2,1)}, u32[]{:S(2)}, u32[]{:S(2)}) collective-permute-start(bf16[56,3072]{1,0:T(8,128)(2,1)S(1)} %collective-permute-done.33), channel_id=1, source_target_pairs={{2,0},{4,6},{3,1},{5,7},{10,8},{12,14},{11,9},{13,15},{18,16},{20,... | collective-permute-start | bytes 1032200 | tf_op jit(solution)/shard_map/ppermute | solution.py:126
  189.4 18.1 %collective-permute-start.37 = (bf16[56,3072]{1,0:T(8,128)(2,1)S(1)}, bf16[56,3072]{1,0:T(8,128)(2,1)S(1)}, u32[]{:S(2)}, u32[]{:S(2)}) collective-permute-start(bf16[56,3072]{1,0:T(8,128)(2,1)S(1)} %collective-permute-done.36), channel_id=1, source_target_pairs={{2,0},{4,6},{3,1},{5,7},{10,8},{12,14},{11,9},{13,15},{18,16},{20,... | collective-permute-start | bytes 1032200 | tf_op jit(solution)/shard_map/ppermute | solution.py:126
  (28 other events, 624.1 us)
Sparse Core Ops, SparseCore 0:
  161.7 24.3 all-reduce.3
  189.6 28.1 reduce-scatter.4

commit v4 on v3

--- a/solution.py
+++ b/solution.py
@@ -1,6 +1,8 @@
 import jax
 import jax.numpy as jnp
 from jax import lax
+from jax.experimental import pallas as pl
+from jax.experimental.pallas import tpu as pltpu
 from jax.sharding import PartitionSpec as P
 
 BF16 = jnp.bfloat16
@@ -8,7 +10,47 @@
 GROUPS = 2
 CHUNKS = 2
 STREAMS = 2
-PIECES = 2
+
+
+def decode_targets(codes, dec_weight, earlier, first, targets, chunk):
+    tokens, width = codes.shape
+    depth = dec_weight.shape[2]
+    steps = width // 1024 if width % 1024 == 0 else 1
+    block = width // steps
+
+    def kernel(codes_ref, weight_ref, *refs):
+        out_ref = refs[-1]
+        product = lax.dot_general(
+            codes_ref[...], weight_ref[...], (((1,), (1,)), ((), ())), preferred_element_type=F32
+        )
+
+        @pl.when(pl.program_id(1) == 0)
+        def _():
+            out_ref[...] = product if earlier is None else refs[0][...] + product
+
+        @pl.when(pl.program_id(1) > 0)
+        def _():
+            out_ref[...] += product
+
+    total = pl.BlockSpec((None, tokens, depth), lambda t, k: (t, 0, 0))
+    given = [] if earlier is None else [earlier]
+    return pl.pallas_call(
+        kernel,
+        grid=(targets, steps),
+        in_specs=[
+            pl.BlockSpec((tokens, block), lambda t, k: (0, k)),
+            pl.BlockSpec((None, None, depth, block), lambda t, k: (0, first + t, 0, chunk * steps + k)),
+        ]
+        + [total] * len(given),
+        out_specs=total,
+        out_shape=jax.ShapeDtypeStruct((targets, tokens, depth), F32),
+        compiler_params=pltpu.CompilerParams(vmem_limit_bytes=20 * 1024 * 1024),
+        cost_estimate=pl.CostEstimate(
+            flops=2 * targets * tokens * width * depth,
+            bytes_accessed=2 * targets * width * depth + 8 * targets * tokens * depth,
+            transcendentals=0,
+        ),
+    )(codes, dec_weight, *given)
 
 
 def local(segments, ring, cores, layer_inputs, targets, enc_weight, enc_bias, dec_weight):
@@ -60,7 +102,7 @@
     decoded = {}
     waiting = []
     ordered = [None]
-    left = {g: [(c, t) for c in range(CHUNKS) for t in range(layers)] for g in range(GROUPS)}
+    low = []
     totals = {}
     residuals = {}
 
@@ -69,42 +111,25 @@
         return lax.optimization_barrier((values, others))[0] if others else values
 
     def background(sent):
-        for _ in range(PIECES):
-            if waiting:
-                work, alone = waiting.pop(0)
-                ordered[0] = sent = work(sent)
-                if alone:
-                    break
+        if waiting:
+            ordered[0] = waiting.pop(0)(sent)
 
     def decode(unit, codes):
         group, chunk = unit
-
-        def piece(layer):
+        all_codes = jnp.concatenate(codes, axis=0)
+
+        def piece(first, targets):
             def run(sent):
-                all_codes = after(codes_of[0], sent)
-                out = lax.dot_general(
-                    all_codes,
-                    decoders[layer, :, chunk * width : (chunk + 1) * width],
-                    (((1,), (1,)), ((), ())),
-                    preferred_element_type=F32,
+                key = group, first
+                decoded[key] = decode_targets(
+                    after(all_codes, sent), dec_weight, decoded.get(key), first, targets, chunk
                 )
-                key = group, layer
-                decoded[key] = out if key not in decoded else decoded[key] + out
-                left[group].remove((chunk, layer))
-                if group < GROUPS - 1:
-                    if not left[group]:
-                        waiting.extend([(lambda sent: scatter_cores(group, sent), True), (wait, True)])
-                        waiting.append((lambda sent: scatter_segments(group, sent), True))
-                elif not left[group]:
-                    waiting.append((lambda sent: share_segments(group, sent), True))
-                elif all(other == 0 for _, other in left[group]) and layer:
-                    waiting.insert(0, (lambda sent: share_cores(group, sent), True))
                 return decoded[key]
 
             return run
 
-        codes_of = [jnp.concatenate(codes, axis=0)]
-        waiting.extend((piece(layer), False) for layer in reversed(range(layers)))
+        waiting.append(piece(1, layers - 1))
+        (low if group == GROUPS - 1 else waiting).append(piece(0, 1))
 
     class Stream:
         def __init__(self, own):
@@ -148,7 +173,8 @@
                 got = self.swap(sent[side], side) if sent[side] is not None else None
                 if got is not None:
                     self.got[side][k] = got
-            background(sent)
+            if i < n or k < ring - 2:
+                background(sent)
             if i and k == ring - 2:
                 unit = self.own[i - 1]
                 codes = [finished[unit]]
@@ -160,6 +186,7 @@
                     codes.append(jnp.where(m <= z, left, right))
                 decode(unit, codes)
             self.slot += 1
+            self.sent = sent
             if i < n and k == ring - 1:
                 chunk = self.own[i][1]
                 bias = enc_bias[0, chunk * width : (chunk + 1) * width][None, :]
@@ -172,27 +199,8 @@
                 return True
             return not (i == n and k == ring - 2)
 
-    def wait(sent):
-        return sent
-
-    def scatter_cores(group, sent):
-        blocks = after([decoded[group, layer] for layer in range(layers)], sent)
-        blocks = jnp.stack([jnp.where(layer >= segment, blocks[layer], 0.0) for layer in range(layers)])
-        blocks = blocks.astype(BF16).reshape(layers, ring, rows, depth)
-        blocks = jnp.stack(
-            [lax.dynamic_index_in_dim(blocks, (z - b) % ring, axis=1, keepdims=False) for b in range(ring)], axis=1
-        )
-        totals[group] = lax.psum_scatter(blocks, "tok", scatter_dimension=1, tiled=True)
-        return blocks
-
-    def scatter_segments(group, sent):
-        total = after(totals[group], sent)
-        residuals[group] = lax.psum_scatter(total, "segment", scatter_dimension=0, tiled=True)[0].astype(F32)
-        return total
-
     def share_cores(group, sent, first=1):
-        blocks = after([decoded[group, layer] for layer in range(first, layers if first else 1)], sent)
-        blocks = jnp.stack(blocks).reshape(-1, ring, rows, depth)
+        blocks = after(decoded[group, first], sent).reshape(-1, ring, rows, depth)
 
         def share(index):
             begin = index * per_core
@@ -223,7 +231,6 @@
             pairs = [(i, i ^ k if paired else i + k) for i in range(segments)]
             got = lax.ppermute(given[-1], "segment", [(i, j) for i, j in pairs if i < j < segments])
             received.append(got)
-        share_cores(group, given, 0)
         own = jnp.where(
             segment == 0,
             totals[group, 0][0],
@@ -238,8 +245,21 @@
         for i, stream in enumerate(streams):
             if going[i]:
                 going[i] = stream.advance()
-    while waiting:
-        background(None)
+    sent = [stream.sent for stream in streams]
+    last = waiting[-STREAMS:]
+    for work in waiting[:-STREAMS]:
+        sent = work(sent)
+    for group in range(GROUPS - 1):
+        sent = share_cores(group, sent)
+        share_cores(group, sent, 0)
+        sent = share_segments(group, sent)
+    for work in last:
+        sent = work(sent)
+    sent = share_cores(GROUPS - 1, sent)
+    for work in low:
+        sent = work([sent, residuals.get(GROUPS - 2)])
+    share_cores(GROUPS - 1, sent, 0)
+    share_segments(GROUPS - 1, sent)
     own = jnp.stack([residuals[group] for group in range(GROUPS)], axis=1)
     residual = targets[0].astype(F32) - own.reshape(targets.shape[1:])
     features = jnp.concatenate(

time: 257 us -> 298 us (1.16)
  local copies, waits for them, and re-layouts: 4.65 us -> 66.4 us
  matrix products: 49 us -> 7.16 us
  Pallas kernels: 0 us -> 38 us
  waiting for transfers between devices: 70.3 us -> 55 us
  between operations: 15.8 us -> 1.68 us
  starting transfers between devices: 100 us -> 111 us
    unnamed x29 -> x30, local copies, waits for them, and re-layouts: 1.32 us -> 64.8 us
    dot_general x16 -> x0, matrix products: 41.8 us -> none  [run(): lax.dot_general(all_codes, decoders[layer, :, chunk * width:(chunk + 1) *...]
    pallas_call x0 -> x8, Pallas kernels: none -> 38 us  [decode_targets(): pl.pallas_call(kernel, grid=(targets, steps), in_specs=[pl.BlockSpec((tok...]
    unnamed x4 -> x0, waiting for transfers between devices: 12.1 us -> none
    ppermute x3 -> x6, starting transfers between devices: 8.41 us -> 14.1 us  [share_segments(): lax.ppermute(given[-1], 'segment', [(i, j) for i, j in pairs if i < j < s...]
    ppermute x36, starting transfers between devices: 86.2 us -> 90.3 us  [swap(): return lax.ppermute(value, 'feat', pairs) if pairs else None]
  transfers between devices with their start and end apart: 46 -> 49, of which waited for: 16 -> 14; matrix products, arithmetic and copies ran while one was open for 22% -> 5% of each run, Pallas kernels for 0% -> 13%
where the time goes in v4:
time: 298 us; the launch traced here: 297 us
  starting transfers between devices  111 us (37%)
  local copies, waits for them, and re-layouts  66.4 us (22%)
  waiting for transfers between devices  55 us (18%)
  Pallas kernels  38 us (13%)
  other arithmetic  12.6 us (4%)
  matrix products  7.16 us (2%)
  blocking collectives  4.68 us (2%)
    ppermute x36, starting transfers between devices, swap(): return lax.ppermute(value, 'feat', pairs) if pairs else None  90.3 us
    unnamed x30, local copies, waits for them, and re-layouts  64.8 us
    ppermute x36, waiting for transfers between devices, swap(): return lax.ppermute(value, 'feat', pairs) if pairs else None  46.7 us
    pallas_call x8, Pallas kernels, decode_targets(): pl.pallas_call(kernel, grid=(targets, steps), in_specs=[pl.BlockSpec((tok...  38 us
    ppermute x6, starting transfers between devices, share_segments(): lax.ppermute(given[-1], 'segment', [(i, j) for i, j in pairs if i < j < s...  14.1 us
    dot_general x4, matrix products, partial_sums(): jnp.dot(columns[group], weight[:, chunk * width:(chunk + 1) * width], pre...  7.16 us
  transfers between devices with their start and end apart: 49, of which 14 were waited for; matrix products, arithmetic and copies ran while one was open for 5% of the time, Pallas kernels for 13%

profile of v4, /device:TPU:0, one launch (start us, length us, event | category | flops | bytes accessed | tf_op | source)
XLA Modules:
  0.0 296.8 jit_solution(5546855702017186444)
XLA Ops:
  9.7 4.6 %collective-permute-done.1 = bf16[56,576]{1,0:T(8,128)(2,1)S(1)} collective-permute-done((bf16[56,576]{1,0:T(8,128)(2,1)S(1)}, bf16[56,576]{1,0:T(8,128)(2,1)S(1)}, u32[]{:S(2)}, u32[]{:S(2)}) %collective-permute-start.1) | collective-permute-done | bytes 64544 | tf_op jit(solution)/shard_map/ppermute | solution.py:82
  17.5 3.4 %fusion.2 = f32[224,3072]{1,0:T(8,128)S(1)} fusion(bf16[576,6144]{1,0:T(8,128)(2,1)} %bitcast.85, bf16[56,576]{1,0:T(8,128)(2,1)S(1)} %get-tuple-element.97, bf16[56,576]{1,0:T(8,128)(2,1)S(1)} %get-tuple-element.98, bf16[56,576]{1,0:T(8,128)(2,1)S(1)} %get-tuple-element.99, bf16[56,576]{1,0:T(8,128)(2,1)S(1)} %get-tuple-element.96), kind=kOutput, calls=%fused_computation.2 | convolution fusion | flops 793755648 | bytes 6549504 | tf_op jit(solution)/shard_map/dot_general | solution.py:95
  23.0 3.2 %collective-permute-start.8 = (bf16[56,3072]{1,0:T(8,128)(2,1)S(1)}, bf16[56,3072]{1,0:T(8,128)(2,1)S(1)}, u32[]{:S(2)}, u32[]{:S(2)}) collective-permute-start(bf16[56,3072]{1,0:T(8,128)(2,1)S(1)} %get-tuple-element.64), channel_id=1, source_target_pairs={{0,2},{6,4},{1,3},{7,5},{8,10},{14,12},{9,11},{15,13},{16,18},{22,... | collective-permute-start | bytes 1032200 | tf_op jit(solution)/shard_map/ppermute | solution.py:151
  35.4 13.9 %collective-permute-done.3 = bf16[56,3072]{1,0:T(8,128)(2,1)S(1)} collective-permute-done((bf16[56,3072]{1,0:T(8,128)(2,1)S(1)}, bf16[56,3072]{1,0:T(8,128)(2,1)S(1)}, u32[]{:S(2)}, u32[]{:S(2)}) %collective-permute-start.3) | collective-permute-done | bytes 344096 | tf_op jit(solution)/shard_map/ppermute | solution.py:151
  50.4 5.3 %collective-permute-start.10 = (bf16[56,3072]{1,0:T(8,128)(2,1)S(1)}, bf16[56,3072]{1,0:T(8,128)(2,1)S(1)}, u32[]{:S(2)}, u32[]{:S(2)}) collective-permute-start(bf16[56,3072]{1,0:T(8,128)(2,1)S(1)} %get-tuple-element.62), channel_id=1, source_target_pairs={{0,2},{2,0},{4,6},{6,4},{1,3},{3,1},{5,7},{7,5},{8,10},{10,8},{12,... | collective-permute-start | bytes 1032200 | tf_op jit(solution)/shard_map/ppermute | solution.py:151
  57.0 8.2 %collective-permute-start.5 = (bf16[56,3072]{1,0:T(8,128)(2,1)S(1)}, bf16[56,3072]{1,0:T(8,128)(2,1)S(1)}, u32[]{:S(2)}, u32[]{:S(2)}) collective-permute-start(bf16[56,3072]{1,0:T(8,128)(2,1)S(1)} %get-tuple-element.58), channel_id=1, source_target_pairs={{0,2},{2,0},{4,6},{6,4},{1,3},{3,1},{5,7},{7,5},{8,10},{10,8},{12,... | collective-permute-start | bytes 1032200 | tf_op jit(solution)/shard_map/ppermute | solution.py:151
  66.7 9.2 %collective-permute-start.19 = (bf16[56,3072]{1,0:T(8,128)(2,1)S(1)}, bf16[56,3072]{1,0:T(8,128)(2,1)S(1)}, u32[]{:S(2)}, u32[]{:S(2)}) collective-permute-start(bf16[56,3072]{1,0:T(8,128)(2,1)S(1)} %fusion.19), channel_id=1, source_target_pairs={{0,2},{2,0},{4,6},{6,4},{1,3},{3,1},{5,7},{7,5},{8,10},{10,8},{12,... | collective-permute-start | bytes 1032200 | tf_op jit(solution)/shard_map/ppermute | solution.py:151
  76.8 6.5 %collective-permute-start.16 = (bf16[56,3072]{1,0:T(8,128)(2,1)S(1)}, bf16[56,3072]{1,0:T(8,128)(2,1)S(1)}, u32[]{:S(2)}, u32[]{:S(2)}) collective-permute-start(bf16[56,3072]{1,0:T(8,128)(2,1)S(1)} %fusion.23), channel_id=1, source_target_pairs={{0,2},{2,0},{4,6},{6,4},{1,3},{3,1},{5,7},{7,5},{8,10},{10,8},{12,... | collective-permute-start | bytes 1032200 | tf_op jit(solution)/shard_map/ppermute | solution.py:151
  83.4 3.8 %collective-permute-start.22 = (bf16[56,3072]{1,0:T(8,128)(2,1)S(1)}, bf16[56,3072]{1,0:T(8,128)(2,1)S(1)}, u32[]{:S(2)}, u32[]{:S(2)}) collective-permute-start(bf16[56,3072]{1,0:T(8,128)(2,1)S(1)} %add_convert_fusion.5), channel_id=1, source_target_pairs={{0,2},{2,0},{4,6},{6,4},{1,3},{3,1},{5,7},{7,5},{8,10},{10,8},{12,... | collective-permute-start | bytes 1032200 | tf_op jit(solution)/shard_map/ppermute | solution.py:151
  87.2 5.1 %collective-permute-done.16 = bf16[56,3072]{1,0:T(8,128)(2,1)S(1)} collective-permute-done((bf16[56,3072]{1,0:T(8,128)(2,1)S(1)}, bf16[56,3072]{1,0:T(8,128)(2,1)S(1)}, u32[]{:S(2)}, u32[]{:S(2)}) %collective-permute-start.16) | collective-permute-done | bytes 344096 | tf_op jit(solution)/shard_map/ppermute | solution.py:151
  95.3 4.3 %collective-permute-done.22 = bf16[56,3072]{1,0:T(8,128)(2,1)S(1)} collective-permute-done((bf16[56,3072]{1,0:T(8,128)(2,1)S(1)}, bf16[56,3072]{1,0:T(8,128)(2,1)S(1)}, u32[]{:S(2)}, u32[]{:S(2)}) %collective-permute-start.22) | collective-permute-done | bytes 344096 | tf_op jit(solution)/shard_map/ppermute | solution.py:151
  104.2 6.3 %collective-permute-start.18 = (bf16[56,3072]{1,0:T(8,128)(2,1)S(1)}, bf16[56,3072]{1,0:T(8,128)(2,1)S(1)}, u32[]{:S(2)}, u32[]{:S(2)}) collective-permute-start(bf16[56,3072]{1,0:T(8,128)(2,1)S(1)} %get-tuple-element.55), channel_id=1, source_target_pairs={{0,2},{2,0},{4,6},{6,4},{1,3},{3,1},{5,7},{7,5},{8,10},{10,8},{12,... | collective-permute-start | bytes 1032200 | tf_op jit(solution)/shard_map/ppermute | solution.py:151
  110.6 4.4 %collective-permute-start.27 = (bf16[56,3072]{1,0:T(8,128)(2,1)S(1)}, bf16[56,3072]{1,0:T(8,128)(2,1)S(1)}, u32[]{:S(2)}, u32[]{:S(2)}) collective-permute-start(bf16[56,3072]{1,0:T(8,128)(2,1)S(1)} %add_convert_fusion.6), channel_id=1, source_target_pairs={{0,2},{2,0},{4,6},{6,4},{1,3},{3,1},{5,7},{7,5},{8,10},{10,8},{12,... | collective-permute-start | bytes 1032200 | tf_op jit(solution)/shard_map/ppermute | solution.py:151
  116.2 9.0 %copy-done = bf16[1,4,576,6144]{3,2,1,0:T(8,128)(2,1)S(1)} copy-done((bf16[1,4,576,6144]{3,2,1,0:T(8,128)(2,1)S(1)}, bf16[1,4,576,6144]{3,2,1,0:T(8,128)(2,1)}, u32[]{:S(2)}) %copy-start) | copy-done | bytes 28311576
  125.2 7.1 %shard_map.68.refs_0_ = f32[3,224,576]{2,1,0:T(8,128)S(1)} custom-call(bf16[224,3072]{1,0:T(8,128)(2,1)S(1)} %pad_maximum_fusion.codes_ref, bf16[1,4,576,6144]{3,2,1,0:T(8,128)(2,1)S(1)} %copy-done), custom_call_target="tpu_custom_call" | custom-call | flops 2378170368 | bytes 13713408 | tf_op jit(solution)/shard_map/pallas_call | solution.py:37
  132.6 8.9 %collective-permute-start.23 = (bf16[56,3072]{1,0:T(8,128)(2,1)S(1)}, bf16[56,3072]{1,0:T(8,128)(2,1)S(1)}, u32[]{:S(2)}, u32[]{:S(2)}) collective-permute-start(bf16[56,3072]{1,0:T(8,128)(2,1)S(1)} %get-tuple-element.51), channel_id=1, source_target_pairs={{0,2},{2,0},{4,6},{6,4},{1,3},{3,1},{5,7},{7,5},{8,10},{10,8},{12,... | collective-permute-start | bytes 1032200 | tf_op jit(solution)/shard_map/ppermute | solution.py:151
  147.6 4.3 %collective-permute-start.29 = (bf16[56,3072]{1,0:T(8,128)(2,1)S(1)}, bf16[56,3072]{1,0:T(8,128)(2,1)}, u32[]{:S(2)}, u32[]{:S(2)}) collective-permute-start(bf16[56,3072]{1,0:T(8,128)(2,1)S(1)} %fusion.15), channel_id=1, source_target_pairs={{0,2},{2,0},{4,6},{6,4},{1,3},{3,1},{5,7},{7,5},{8,10},{10,8},{12,... | collective-permute-start | bytes 1032200 | tf_op jit(solution)/shard_map/ppermute | solution.py:151
  155.7 9.0 %copy-done.1 = bf16[1,4,576,6144]{3,2,1,0:T(8,128)(2,1)S(1)} copy-done((bf16[1,4,576,6144]{3,2,1,0:T(8,128)(2,1)S(1)}, bf16[1,4,576,6144]{3,2,1,0:T(8,128)(2,1)}, u32[]{:S(2)}) %copy-start.1) | copy-done | bytes 28311576
  170.2 4.7 %collective-permute-start.31 = (bf16[56,3072]{1,0:T(8,128)(2,1)}, bf16[56,3072]{1,0:T(8,128)(2,1)}, u32[]{:S(2)}, u32[]{:S(2)}) collective-permute-start(bf16[56,3072]{1,0:T(8,128)(2,1)} %fusion.11), channel_id=1, source_target_pairs={{0,2},{2,0},{4,6},{6,4},{1,3},{3,1},{5,7},{7,5},{8,10},{10,8},{12,... | collective-permute-start | bytes 1032200 | tf_op jit(solution)/shard_map/ppermute | solution.py:151
  177.7 9.0 %copy-done.2 = bf16[1,4,576,6144]{3,2,1,0:T(8,128)(2,1)S(1)} copy-done((bf16[1,4,576,6144]{3,2,1,0:T(8,128)(2,1)S(1)}, bf16[1,4,576,6144]{3,2,1,0:T(8,128)(2,1)}, u32[]{:S(2)}) %copy-start.2) | copy-done | bytes 28311576
  186.8 7.2 %shard_map.71 = f32[3,224,576]{2,1,0:T(8,128)S(1)} custom-call(bf16[224,3072]{1,0:T(8,128)(2,1)S(1)} %pad_maximum_fusion.1.codes_ref, bf16[1,4,576,6144]{3,2,1,0:T(8,128)(2,1)S(1)} %copy-done.2, f32[3,224,576]{2,1,0:T(8,128)S(1)} %shard_map.68.refs_0_), custom_call_target="tpu_custom_call" | custom-call | flops 2378170368 | bytes 13713408 | tf_op jit(solution)/shard_map/pallas_call | solution.py:37
  200.8 5.9 %collective-permute-done.42 = bf16[56,3072]{1,0:T(8,128)(2,1)S(1)} collective-permute-done((bf16[56,3072]{1,0:T(8,128)(2,1)}, bf16[56,3072]{1,0:T(8,128)(2,1)S(1)}, u32[]{:S(2)}, u32[]{:S(2)}) %collective-permute-start.42) | collective-permute-done | bytes 344096 | tf_op jit(solution)/shard_map/ppermute | solution.py:151
  211.2 6.6 %collective-permute-done.39 = bf16[56,3072]{1,0:T(8,128)(2,1)S(1)} collective-permute-done((bf16[56,3072]{1,0:T(8,128)(2,1)S(1)}, bf16[56,3072]{1,0:T(8,128)(2,1)S(1)}, u32[]{:S(2)}, u32[]{:S(2)}) %collective-permute-start.39) | collective-permute-done | bytes 344096 | tf_op jit(solution)/shard_map/ppermute | solution.py:151
  220.1 3.4 %collective-permute-start.35 = (bf16[2,56,576]{2,1,0:T(8,128)(2,1)S(1)}, bf16[2,56,576]{2,1,0:T(8,128)(2,1)S(1)}, u32[]{:S(2)}, u32[]{:S(2)}) collective-permute-start(bf16[2,56,576]{2,1,0:T(8,128)(2,1)S(1)} %get-tuple-element.87), channel_id=1, source_target_pairs={{0,8},{16,24},{1,9},{17,25},{2,10},{18,26},{3,11},{19,27},{4,12},{... | collective-permute-start | bytes 387080 | tf_op jit(solution)/shard_map/ppermute | solution.py:232
  223.5 3.4 %collective-permute-start.36 = (bf16[2,56,576]{2,1,0:T(8,128)(2,1)S(1)}, bf16[2,56,576]{2,1,0:T(8,128)(2,1)S(1)}, u32[]{:S(2)}, u32[]{:S(2)}) collective-permute-start(bf16[2,56,576]{2,1,0:T(8,128)(2,1)S(1)} %get-tuple-element.86), channel_id=1, source_target_pairs={{0,16},{8,24},{1,17},{9,25},{2,18},{10,26},{3,19},{11,27},{4,20},{... | collective-permute-start | bytes 387080 | tf_op jit(solution)/shard_map/ppermute | solution.py:232
  228.3 9.0 %copy-done.3 = bf16[1,4,576,6144]{3,2,1,0:T(8,128)(2,1)S(1)} copy-done((bf16[1,4,576,6144]{3,2,1,0:T(8,128)(2,1)S(1)}, bf16[1,4,576,6144]{3,2,1,0:T(8,128)(2,1)}, u32[]{:S(2)}) %copy-start.3) | copy-done | bytes 28311576
  237.3 7.0 %shard_map.72.refs_0_ = f32[3,224,576]{2,1,0:T(8,128)S(1)} custom-call(bf16[224,3072]{1,0:T(8,128)(2,1)S(1)} %pad_maximum_fusion.3.codes_ref, bf16[1,4,576,6144]{3,2,1,0:T(8,128)(2,1)S(1)} %copy-done.3), custom_call_target="tpu_custom_call" | custom-call | flops 2378170368 | bytes 13713408 | tf_op jit(solution)/shard_map/pallas_call | solution.py:37
  244.4 9.0 %copy-done.4 = bf16[1,4,576,6144]{3,2,1,0:T(8,128)(2,1)S(1)} copy-done((bf16[1,4,576,6144]{3,2,1,0:T(8,128)(2,1)S(1)}, bf16[1,4,576,6144]{3,2,1,0:T(8,128)(2,1)}, u32[]{:S(2)}) %copy-start.4) | copy-done | bytes 28311576
  253.4 7.2 %shard_map.73 = f32[3,224,576]{2,1,0:T(8,128)S(1)} custom-call(bf16[224,3072]{1,0:T(8,128)(2,1)S(1)} %pad_maximum_fusion.2.codes_ref, bf16[1,4,576,6144]{3,2,1,0:T(8,128)(2,1)S(1)} %copy-done.4, f32[3,224,576]{2,1,0:T(8,128)S(1)} %shard_map.72.refs_0_), custom_call_target="tpu_custom_call" | custom-call | flops 2378170368 | bytes 13713408 | tf_op jit(solution)/shard_map/pallas_call | solution.py:37
  261.1 9.0 %copy-done.5 = bf16[1,4,576,6144]{3,2,1,0:T(8,128)(2,1)S(1)} copy-done((bf16[1,4,576,6144]{3,2,1,0:T(8,128)(2,1)S(1)}, bf16[1,4,576,6144]{3,2,1,0:T(8,128)(2,1)}, u32[]{:S(2)}) %copy-start.5) | copy-done | bytes 28311576
  272.5 9.0 %copy-done.6 = bf16[1,4,576,6144]{3,2,1,0:T(8,128)(2,1)S(1)} copy-done((bf16[1,4,576,6144]{3,2,1,0:T(8,128)(2,1)S(1)}, bf16[1,4,576,6144]{3,2,1,0:T(8,128)(2,1)}, u32[]{:S(2)}) %copy-start.6) | copy-done | bytes 28311576
  284.8 3.4 %collective-permute-start.46 = (bf16[2,56,576]{2,1,0:T(8,128)(2,1)S(1)}, bf16[2,56,576]{2,1,0:T(8,128)(2,1)S(1)}, u32[]{:S(2)}, u32[]{:S(2)}) collective-permute-start(bf16[2,56,576]{2,1,0:T(8,128)(2,1)S(1)} %get-tuple-element.82), channel_id=1, source_target_pairs={{0,8},{16,24},{1,9},{17,25},{2,10},{18,26},{3,11},{19,27},{4,12},{... | collective-permute-start | bytes 387080 | tf_op jit(solution)/shard_map/ppermute | solution.py:232
  (165 shorter events, 84.6 us)
Async XLA Ops:
  23.0 11.6 %collective-permute-start.8 = (bf16[56,3072]{1,0:T(8,128)(2,1)S(1)}, bf16[56,3072]{1,0:T(8,128)(2,1)S(1)}, u32[]{:S(2)}, u32[]{:S(2)}) collective-permute-start(bf16[56,3072]{1,0:T(8,128)(2,1)S(1)} %get-tuple-element.64), channel_id=1, source_target_pairs={{0,2},{6,4},{1,3},{7,5},{8,10},{14,12},{9,11},{15,13},{16,18},{22,... | collective-permute-start | bytes 1032200 | tf_op jit(solution)/shard_map/ppermute | solution.py:151
  26.2 24.0 %collective-permute-start.11 = (bf16[56,3072]{1,0:T(8,128)(2,1)S(1)}, bf16[56,3072]{1,0:T(8,128)(2,1)S(1)}, u32[]{:S(2)}, u32[]{:S(2)}) collective-permute-start(bf16[56,3072]{1,0:T(8,128)(2,1)S(1)} %get-tuple-element.65), channel_id=1, source_target_pairs={{0,2},{6,4},{1,3},{7,5},{8,10},{14,12},{9,11},{15,13},{16,18},{22,... | collective-permute-start | bytes 1032200 | tf_op jit(solution)/shard_map/ppermute | solution.py:151
  27.7 21.6 %collective-permute-start.3 = (bf16[56,3072]{1,0:T(8,128)(2,1)S(1)}, bf16[56,3072]{1,0:T(8,128)(2,1)S(1)}, u32[]{:S(2)}, u32[]{:S(2)}) collective-permute-start(bf16[56,3072]{1,0:T(8,128)(2,1)S(1)} %get-tuple-element.60), channel_id=1, source_target_pairs={{0,2},{6,4},{1,3},{7,5},{8,10},{14,12},{9,11},{15,13},{16,18},{22,... | collective-permute-start | bytes 1032200 | tf_op jit(solution)/shard_map/ppermute | solution.py:151
  29.1 27.7 %collective-permute-start.6 = (bf16[56,3072]{1,0:T(8,128)(2,1)S(1)}, bf16[56,3072]{1,0:T(8,128)(2,1)S(1)}, u32[]{:S(2)}, u32[]{:S(2)}) collective-permute-start(bf16[56,3072]{1,0:T(8,128)(2,1)S(1)} %get-tuple-element.61), channel_id=1, source_target_pairs={{0,2},{6,4},{1,3},{7,5},{8,10},{14,12},{9,11},{15,13},{16,18},{22,... | collective-permute-start | bytes 1032200 | tf_op jit(solution)/shard_map/ppermute | solution.py:151
  34.8 15.5 %collective-permute-start.9 = (bf16[56,3072]{1,0:T(8,128)(2,1)S(1)}, bf16[56,3072]{1,0:T(8,128)(2,1)S(1)}, u32[]{:S(2)}, u32[]{:S(2)}) collective-permute-start(bf16[56,3072]{1,0:T(8,128)(2,1)S(1)} %add_convert_fusion.14), channel_id=1, source_target_pairs={{2,4},{4,2},{3,5},{5,3},{10,12},{12,10},{11,13},{13,11},{18,20},{2... | collective-permute-start | bytes 1032200 | tf_op jit(solution)/shard_map/ppermute | solution.py:151
  50.4 15.4 %collective-permute-start.10 = (bf16[56,3072]{1,0:T(8,128)(2,1)S(1)}, bf16[56,3072]{1,0:T(8,128)(2,1)S(1)}, u32[]{:S(2)}, u32[]{:S(2)}) collective-permute-start(bf16[56,3072]{1,0:T(8,128)(2,1)S(1)} %get-tuple-element.62), channel_id=1, source_target_pairs={{0,2},{2,0},{4,6},{6,4},{1,3},{3,1},{5,7},{7,5},{8,10},{10,8},{12,... | collective-permute-start | bytes 1032200 | tf_op jit(solution)/shard_map/ppermute | solution.py:151
  57.0 18.9 %collective-permute-start.5 = (bf16[56,3072]{1,0:T(8,128)(2,1)S(1)}, bf16[56,3072]{1,0:T(8,128)(2,1)S(1)}, u32[]{:S(2)}, u32[]{:S(2)}) collective-permute-start(bf16[56,3072]{1,0:T(8,128)(2,1)S(1)} %get-tuple-element.58), channel_id=1, source_target_pairs={{0,2},{2,0},{4,6},{6,4},{1,3},{3,1},{5,7},{7,5},{8,10},{10,8},{12,... | collective-permute-start | bytes 1032200 | tf_op jit(solution)/shard_map/ppermute | solution.py:151
  66.0 17.3 %collective-permute-start.21 = (bf16[56,3072]{1,0:T(8,128)(2,1)S(1)}, bf16[56,3072]{1,0:T(8,128)(2,1)S(1)}, u32[]{:S(2)}, u32[]{:S(2)}) collective-permute-start(bf16[56,3072]{1,0:T(8,128)(2,1)S(1)} %fusion.19), channel_id=1, source_target_pairs={{2,4},{4,2},{3,5},{5,3},{10,12},{12,10},{11,13},{13,11},{18,20},{2... | collective-permute-start | bytes 1032200 | tf_op jit(solution)/shard_map/ppermute | solution.py:151
  66.7 28.5 %collective-permute-start.19 = (bf16[56,3072]{1,0:T(8,128)(2,1)S(1)}, bf16[56,3072]{1,0:T(8,128)(2,1)S(1)}, u32[]{:S(2)}, u32[]{:S(2)}) collective-permute-start(bf16[56,3072]{1,0:T(8,128)(2,1)S(1)} %fusion.19), channel_id=1, source_target_pairs={{0,2},{2,0},{4,6},{6,4},{1,3},{3,1},{5,7},{7,5},{8,10},{10,8},{12,... | collective-permute-start | bytes 1032200 | tf_op jit(solution)/shard_map/ppermute | solution.py:151
  76.8 15.5 %collective-permute-start.16 = (bf16[56,3072]{1,0:T(8,128)(2,1)S(1)}, bf16[56,3072]{1,0:T(8,128)(2,1)S(1)}, u32[]{:S(2)}, u32[]{:S(2)}) collective-permute-start(bf16[56,3072]{1,0:T(8,128)(2,1)S(1)} %fusion.23), channel_id=1, source_target_pairs={{0,2},{2,0},{4,6},{6,4},{1,3},{3,1},{5,7},{7,5},{8,10},{10,8},{12,... | collective-permute-start | bytes 1032200 | tf_op jit(solution)/shard_map/ppermute | solution.py:151
  83.4 16.1 %collective-permute-start.22 = (bf16[56,3072]{1,0:T(8,128)(2,1)S(1)}, bf16[56,3072]{1,0:T(8,128)(2,1)S(1)}, u32[]{:S(2)}, u32[]{:S(2)}) collective-permute-start(bf16[56,3072]{1,0:T(8,128)(2,1)S(1)} %add_convert_fusion.5), channel_id=1, source_target_pairs={{0,2},{2,0},{4,6},{6,4},{1,3},{3,1},{5,7},{7,5},{8,10},{10,8},{12,... | collective-permute-start | bytes 1032200 | tf_op jit(solution)/shard_map/ppermute | solution.py:151
  100.5 44.1 %collective-permute-start.25 = (bf16[56,3072]{1,0:T(8,128)(2,1)S(1)}, bf16[56,3072]{1,0:T(8,128)(2,1)S(1)}, u32[]{:S(2)}, u32[]{:S(2)}) collective-permute-start(bf16[56,3072]{1,0:T(8,128)(2,1)S(1)} %get-tuple-element.52), channel_id=1, source_target_pairs={{2,4},{4,2},{3,5},{5,3},{10,12},{12,10},{11,13},{13,11},{18,20},{2... | collective-permute-start | bytes 1032200 | tf_op jit(solution)/shard_map/ppermute | solution.py:151
  104.2 11.8 %collective-permute-start.18 = (bf16[56,3072]{1,0:T(8,128)(2,1)S(1)}, bf16[56,3072]{1,0:T(8,128)(2,1)S(1)}, u32[]{:S(2)}, u32[]{:S(2)}) collective-permute-start(bf16[56,3072]{1,0:T(8,128)(2,1)S(1)} %get-tuple-element.55), channel_id=1, source_target_pairs={{0,2},{2,0},{4,6},{6,4},{1,3},{3,1},{5,7},{7,5},{8,10},{10,8},{12,... | collective-permute-start | bytes 1032200 | tf_op jit(solution)/shard_map/ppermute | solution.py:151
  110.6 42.6 %collective-permute-start.27 = (bf16[56,3072]{1,0:T(8,128)(2,1)S(1)}, bf16[56,3072]{1,0:T(8,128)(2,1)S(1)}, u32[]{:S(2)}, u32[]{:S(2)}) collective-permute-start(bf16[56,3072]{1,0:T(8,128)(2,1)S(1)} %add_convert_fusion.6), channel_id=1, source_target_pairs={{0,2},{2,0},{4,6},{6,4},{1,3},{3,1},{5,7},{7,5},{8,10},{10,8},{12,... | collective-permute-start | bytes 1032200 | tf_op jit(solution)/shard_map/ppermute | solution.py:151
  132.6 14.8 %collective-permute-start.23 = (bf16[56,3072]{1,0:T(8,128)(2,1)S(1)}, bf16[56,3072]{1,0:T(8,128)(2,1)S(1)}, u32[]{:S(2)}, u32[]{:S(2)}) collective-permute-start(bf16[56,3072]{1,0:T(8,128)(2,1)S(1)} %get-tuple-element.51), channel_id=1, source_target_pairs={{0,2},{2,0},{4,6},{6,4},{1,3},{3,1},{5,7},{7,5},{8,10},{10,8},{12,... | collective-permute-start | bytes 1032200 | tf_op jit(solution)/shard_map/ppermute | solution.py:151
  147.6 20.3 %collective-permute-start.29 = (bf16[56,3072]{1,0:T(8,128)(2,1)S(1)}, bf16[56,3072]{1,0:T(8,128)(2,1)}, u32[]{:S(2)}, u32[]{:S(2)}) collective-permute-start(bf16[56,3072]{1,0:T(8,128)(2,1)S(1)} %fusion.15), channel_id=1, source_target_pairs={{0,2},{2,0},{4,6},{6,4},{1,3},{3,1},{5,7},{7,5},{8,10},{10,8},{12,... | collective-permute-start | bytes 1032200 | tf_op jit(solution)/shard_map/ppermute | solution.py:151
  151.8 24.5 %collective-permute-start.41 = (bf16[56,3072]{1,0:T(8,128)(2,1)S(1)}, bf16[56,3072]{1,0:T(8,128)(2,1)}, u32[]{:S(2)}, u32[]{:S(2)}) collective-permute-start(bf16[56,3072]{1,0:T(8,128)(2,1)S(1)} %fusion.15), channel_id=1, source_target_pairs={{2,4},{4,2},{3,5},{5,3},{10,12},{12,10},{11,13},{13,11},{18,20},{2... | collective-permute-start | bytes 1032200 | tf_op jit(solution)/shard_map/ppermute | solution.py:151
  153.4 15.9 %collective-permute-start.26 = (bf16[56,3072]{1,0:T(8,128)(2,1)S(1)}, bf16[56,3072]{1,0:T(8,128)(2,1)S(1)}, u32[]{:S(2)}, u32[]{:S(2)}) collective-permute-start(bf16[56,3072]{1,0:T(8,128)(2,1)S(1)} %get-tuple-element.48), channel_id=1, source_target_pairs={{0,2},{2,0},{4,6},{6,4},{1,3},{3,1},{5,7},{7,5},{8,10},{10,8},{12,... | collective-permute-start | bytes 1032200 | tf_op jit(solution)/shard_map/ppermute | solution.py:151
  154.6 14.7 %collective-permute-start.28 = (bf16[56,3072]{1,0:T(8,128)(2,1)S(1)}, bf16[56,3072]{1,0:T(8,128)(2,1)S(1)}, u32[]{:S(2)}, u32[]{:S(2)}) collective-permute-start(bf16[56,3072]{1,0:T(8,128)(2,1)S(1)} %get-tuple-element.49), channel_id=1, source_target_pairs={{2,4},{4,2},{3,5},{5,3},{10,12},{12,10},{11,13},{13,11},{18,20},{2... | collective-permute-start | bytes 1032200 | tf_op jit(solution)/shard_map/ppermute | solution.py:151
  167.9 26.1 %collective-permute-start.30 = (bf16[56,3072]{1,0:T(8,128)(2,1)}, bf16[56,3072]{1,0:T(8,128)(2,1)}, u32[]{:S(2)}, u32[]{:S(2)}) collective-permute-start(bf16[56,3072]{1,0:T(8,128)(2,1)} %collective-permute-done.29), channel_id=1, source_target_pairs={{2,4},{4,2},{3,5},{5,3},{10,12},{12,10},{11,13},{13,11},{18,20},{2... | collective-permute-start | bytes 1032200 | tf_op jit(solution)/shard_map/ppermute | solution.py:151
  170.2 23.8 %collective-permute-start.31 = (bf16[56,3072]{1,0:T(8,128)(2,1)}, bf16[56,3072]{1,0:T(8,128)(2,1)}, u32[]{:S(2)}, u32[]{:S(2)}) collective-permute-start(bf16[56,3072]{1,0:T(8,128)(2,1)} %fusion.11), channel_id=1, source_target_pairs={{0,2},{2,0},{4,6},{6,4},{1,3},{3,1},{5,7},{7,5},{8,10},{10,8},{12,... | collective-permute-start | bytes 1032200 | tf_op jit(solution)/shard_map/ppermute | solution.py:151
  174.9 21.3 %collective-permute-start.38 = (bf16[56,3072]{1,0:T(8,128)(2,1)}, bf16[56,3072]{1,0:T(8,128)(2,1)}, u32[]{:S(2)}, u32[]{:S(2)}) collective-permute-start(bf16[56,3072]{1,0:T(8,128)(2,1)} %fusion.11), channel_id=1, source_target_pairs={{2,4},{4,2},{3,5},{5,3},{10,12},{12,10},{11,13},{13,11},{18,20},{2... | collective-permute-start | bytes 1032200 | tf_op jit(solution)/shard_map/ppermute | solution.py:151
  176.3 21.2 %collective-permute-start.43 = (bf16[56,3072]{1,0:T(8,128)(2,1)}, bf16[56,3072]{1,0:T(8,128)(2,1)}, u32[]{:S(2)}, u32[]{:S(2)}) collective-permute-start(bf16[56,3072]{1,0:T(8,128)(2,1)} %collective-permute-done.41), channel_id=1, source_target_pairs={{2,0},{4,6},{3,1},{5,7},{10,8},{12,14},{11,9},{13,15},{18,16},{20,... | collective-permute-start | bytes 1032200 | tf_op jit(solution)/shard_map/ppermute | solution.py:151
  194.9 11.8 %collective-permute-start.42 = (bf16[56,3072]{1,0:T(8,128)(2,1)}, bf16[56,3072]{1,0:T(8,128)(2,1)S(1)}, u32[]{:S(2)}, u32[]{:S(2)}) collective-permute-start(bf16[56,3072]{1,0:T(8,128)(2,1)} %collective-permute-done.30), channel_id=1, source_target_pairs={{2,0},{4,6},{3,1},{5,7},{10,8},{12,14},{11,9},{13,15},{18,16},{20,... | collective-permute-start | bytes 1032200 | tf_op jit(solution)/shard_map/ppermute | solution.py:151
  196.2 14.8 %collective-permute-start.40 = (bf16[56,3072]{1,0:T(8,128)(2,1)}, bf16[56,3072]{1,0:T(8,128)(2,1)S(1)}, u32[]{:S(2)}, u32[]{:S(2)}) collective-permute-start(bf16[56,3072]{1,0:T(8,128)(2,1)} %collective-permute-done.38), channel_id=1, source_target_pairs={{2,0},{4,6},{3,1},{5,7},{10,8},{12,14},{11,9},{13,15},{18,16},{20,... | collective-permute-start | bytes 1032200 | tf_op jit(solution)/shard_map/ppermute | solution.py:151
  198.8 21.2 %collective-permute-start.34 = (bf16[3,2,56,576]{3,2,1,0:T(8,128)(2,1)S(1)}, bf16[3,2,56,576]{3,2,1,0:T(8,128)(2,1)S(1)}, u32[]{:S(2)}, u32[]{:S(2)}) collective-permute-start(bf16[3,2,56,576]{3,2,1,0:T(8,128)(2,1)S(1)} %pad_maximum_fusion.5), channel_id=1, source_target_pairs={{0,1},{1,0},{2,3},{3,2},{4,5},{5,4},{6,7},{7,6},{8,9},{9,8},{10,11... | collective-permute-start | bytes 1161224 | tf_op jit(solution)/shard_map/ppermute | solution.py:219
  198.9 18.9 %collective-permute-start.39 = (bf16[56,3072]{1,0:T(8,128)(2,1)S(1)}, bf16[56,3072]{1,0:T(8,128)(2,1)S(1)}, u32[]{:S(2)}, u32[]{:S(2)}) collective-permute-start(bf16[56,3072]{1,0:T(8,128)(2,1)S(1)} %collective-permute-done.32), channel_id=1, source_target_pairs={{2,0},{4,6},{3,1},{5,7},{10,8},{12,14},{11,9},{13,15},{18,16},{20,... | collective-permute-start | bytes 1032200 | tf_op jit(solution)/shard_map/ppermute | solution.py:151
  200.2 60.7 %collective-permute-start.33 = (bf16[1,2,56,576]{3,2,1,0:T(8,128)(2,1)S(1)}, bf16[1,2,56,576]{3,2,1,0:T(8,128)(2,1)S(1)}, u32[]{:S(2)}, u32[]{:S(2)}) collective-permute-start(bf16[1,2,56,576]{3,2,1,0:T(8,128)(2,1)S(1)} %pad_maximum_fusion.10), channel_id=1, source_target_pairs={{0,1},{1,0},{2,3},{3,2},{4,5},{5,4},{6,7},{7,6},{8,9},{9,8},{10,11... | collective-permute-start | bytes 387080 | tf_op jit(solution)/shard_map/ppermute | solution.py:219
  220.1 40.8 %collective-permute-start.35 = (bf16[2,56,576]{2,1,0:T(8,128)(2,1)S(1)}, bf16[2,56,576]{2,1,0:T(8,128)(2,1)S(1)}, u32[]{:S(2)}, u32[]{:S(2)}) collective-permute-start(bf16[2,56,576]{2,1,0:T(8,128)(2,1)S(1)} %get-tuple-element.87), channel_id=1, source_target_pairs={{0,8},{16,24},{1,9},{17,25},{2,10},{18,26},{3,11},{19,27},{4,12},{... | collective-permute-start | bytes 387080 | tf_op jit(solution)/shard_map/ppermute | solution.py:232
  223.5 37.4 %collective-permute-start.36 = (bf16[2,56,576]{2,1,0:T(8,128)(2,1)S(1)}, bf16[2,56,576]{2,1,0:T(8,128)(2,1)S(1)}, u32[]{:S(2)}, u32[]{:S(2)}) collective-permute-start(bf16[2,56,576]{2,1,0:T(8,128)(2,1)S(1)} %get-tuple-element.86), channel_id=1, source_target_pairs={{0,16},{8,24},{1,17},{9,25},{2,18},{10,26},{3,19},{11,27},{4,20},{... | collective-permute-start | bytes 387080 | tf_op jit(solution)/shard_map/ppermute | solution.py:232
  227.0 34.0 %collective-permute-start.37 = (bf16[2,56,576]{2,1,0:T(8,128)(2,1)S(1)}, bf16[2,56,576]{2,1,0:T(8,128)(2,1)S(1)}, u32[]{:S(2)}, u32[]{:S(2)}) collective-permute-start(bf16[2,56,576]{2,1,0:T(8,128)(2,1)S(1)} %get-tuple-element.85), channel_id=1, source_target_pairs={{0,24},{8,16},{1,25},{9,17},{2,26},{10,18},{3,27},{11,19},{4,28},{... | collective-permute-start | bytes 387080 | tf_op jit(solution)/shard_map/ppermute | solution.py:232
  260.8 23.8 %collective-permute-start.45 = (bf16[3,2,56,576]{3,2,1,0:T(8,128)(2,1)S(1)}, bf16[3,2,56,576]{3,2,1,0:T(8,128)(2,1)S(1)}, u32[]{:S(2)}, u32[]{:S(2)}) collective-permute-start(bf16[3,2,56,576]{3,2,1,0:T(8,128)(2,1)S(1)} %pad_maximum_fusion.6), channel_id=1, source_target_pairs={{0,1},{1,0},{2,3},{3,2},{4,5},{5,4},{6,7},{7,6},{8,9},{9,8},{10,11... | collective-permute-start | bytes 1161224 | tf_op jit(solution)/shard_map/ppermute | solution.py:219
  (32 other events, 286.0 us)

commit v5 on v3

--- a/solution.py
+++ b/solution.py
@@ -52,7 +52,7 @@
     def partial_sums(group, chunk):
         part = jnp.dot(
             columns[group], weight[:, chunk * width : (chunk + 1) * width], preferred_element_type=F32
-        )
+        ).astype(BF16)
         return [part[k * rows : (k + 1) * rows] for k in range(ring)]
 
     units = [(group, chunk) for group in range(GROUPS) for chunk in range(CHUNKS)]
@@ -60,7 +60,7 @@
     decoded = {}
     waiting = []
     ordered = [None]
-    left = {g: [(c, t) for c in range(CHUNKS) for t in range(layers)] for g in range(GROUPS)}
+    last = []
     totals = {}
     residuals = {}
 
@@ -69,42 +69,43 @@
         return lax.optimization_barrier((values, others))[0] if others else values
 
     def background(sent):
-        for _ in range(PIECES):
-            if waiting:
-                work, alone = waiting.pop(0)
-                ordered[0] = sent = work(sent)
-                if alone:
-                    break
-
-    def decode(unit, codes):
+        for _ in range(min(PIECES, len(waiting))):
+            ordered[0] = sent = waiting.pop(0)(sent)
+
+    def decode(unit, own, got):
         group, chunk = unit
+        codes = []
+
+        def selected(sent):
+            mine, (even, other) = after((own, got), sent)
+            parts = [mine]
+            zero = jnp.zeros_like(mine)
+            for m in range(1, ring):
+                a, b = m - 1, ring - m - 1
+                left = jnp.where(odd, even.get(a, zero), other.get(a, zero))
+                right = jnp.where(odd, other.get(b, zero), even.get(b, zero))
+                parts.append(jnp.where(m <= z, left, right))
+            return jnp.concatenate(parts, axis=0)
 
         def piece(layer):
             def run(sent):
-                all_codes = after(codes_of[0], sent)
+                if not codes:
+                    codes.append(selected(sent))
                 out = lax.dot_general(
-                    all_codes,
+                    after(codes[0], sent),
                     decoders[layer, :, chunk * width : (chunk + 1) * width],
                     (((1,), (1,)), ((), ())),
                     preferred_element_type=F32,
                 )
                 key = group, layer
                 decoded[key] = out if key not in decoded else decoded[key] + out
-                left[group].remove((chunk, layer))
-                if group < GROUPS - 1:
-                    if not left[group]:
-                        waiting.extend([(lambda sent: scatter_cores(group, sent), True), (wait, True)])
-                        waiting.append((lambda sent: scatter_segments(group, sent), True))
-                elif not left[group]:
-                    waiting.append((lambda sent: share_segments(group, sent), True))
-                elif all(other == 0 for _, other in left[group]) and layer:
-                    waiting.insert(0, (lambda sent: share_cores(group, sent), True))
                 return decoded[key]
 
             return run
 
-        codes_of = [jnp.concatenate(codes, axis=0)]
-        waiting.extend((piece(layer), False) for layer in reversed(range(layers)))
+        (waiting if group < GROUPS - 1 else last).append(piece)
+        if group < GROUPS - 1:
+            waiting[-1:] = [piece(layer) for layer in reversed(range(layers))]
 
     class Stream:
         def __init__(self, own):
@@ -137,33 +138,29 @@
                     value = after(value, ordered)
                 if i < n:
                     rightward = odd == (side == 1)
+                    zero = jnp.zeros_like(self.sums[k])
                     own = jnp.where(
                         rightward,
-                        jnp.where(k > z, self.sums[k], 0.0),
-                        jnp.where(k > ring - 1 - z, self.sums[ring - k], 0.0),
+                        jnp.where(k > z, self.sums[k], zero),
+                        jnp.where(k > ring - 1 - z, self.sums[ring - k], zero),
                     )
-                    value = (own if value is None else own + value.astype(F32)).astype(BF16)
+                    value = own if value is None else (own.astype(F32) + value.astype(F32)).astype(BF16)
                 sent.append(value)
             for side in range(2):
                 got = self.swap(sent[side], side) if sent[side] is not None else None
                 if got is not None:
                     self.got[side][k] = got
-            background(sent)
+            if i < n or k < ring - 2:
+                background(sent)
+            self.sent = sent
             if i and k == ring - 2:
                 unit = self.own[i - 1]
-                codes = [finished[unit]]
-                zero = jnp.zeros_like(codes[0])
-                for m in range(1, ring):
-                    a, b = m - 1, ring - m - 1
-                    left = jnp.where(odd, self.got[0].get(a, zero), self.got[1].get(a, zero))
-                    right = jnp.where(odd, self.got[1].get(b, zero), self.got[0].get(b, zero))
-                    codes.append(jnp.where(m <= z, left, right))
-                decode(unit, codes)
+                decode(unit, finished[unit], tuple(dict(got) for got in self.got))
             self.slot += 1
             if i < n and k == ring - 1:
                 chunk = self.own[i][1]
                 bias = enc_bias[0, chunk * width : (chunk + 1) * width][None, :]
-                total = self.sums[0] + self.got[0][k].astype(F32) + self.got[1][k].astype(F32)
+                total = self.sums[0].astype(F32) + self.got[0][k].astype(F32) + self.got[1][k].astype(F32)
                 finished[self.own[i]] = jax.nn.relu(total + bias).astype(BF16)
                 self.slot, self.step = 0, i + 1
                 if i + 1 < n:
@@ -171,24 +168,6 @@
                 self.got = [{}, {}]
                 return True
             return not (i == n and k == ring - 2)
-
-    def wait(sent):
-        return sent
-
-    def scatter_cores(group, sent):
-        blocks = after([decoded[group, layer] for layer in range(layers)], sent)
-        blocks = jnp.stack([jnp.where(layer >= segment, blocks[layer], 0.0) for layer in range(layers)])
-        blocks = blocks.astype(BF16).reshape(layers, ring, rows, depth)
-        blocks = jnp.stack(
-            [lax.dynamic_index_in_dim(blocks, (z - b) % ring, axis=1, keepdims=False) for b in range(ring)], axis=1
-        )
-        totals[group] = lax.psum_scatter(blocks, "tok", scatter_dimension=1, tiled=True)
-        return blocks
-
-    def scatter_segments(group, sent):
-        total = after(totals[group], sent)
-        residuals[group] = lax.psum_scatter(total, "segment", scatter_dimension=0, tiled=True)[0].astype(F32)
-        return total
 
     def share_cores(group, sent, first=1):
         blocks = after([decoded[group, layer] for layer in range(first, layers if first else 1)], sent)
@@ -223,7 +202,6 @@
             pairs = [(i, i ^ k if paired else i + k) for i in range(segments)]
             got = lax.ppermute(given[-1], "segment", [(i, j) for i, j in pairs if i < j < segments])
             received.append(got)
-        share_cores(group, given, 0)
         own = jnp.where(
             segment == 0,
             totals[group, 0][0],
@@ -238,8 +216,20 @@
         for i, stream in enumerate(streams):
             if going[i]:
                 going[i] = stream.advance()
-    while waiting:
-        background(None)
+    sent = [stream.sent for stream in streams]
+    for work in waiting:
+        sent = work(sent)
+    for group in range(GROUPS - 1):
+        sent = share_cores(group, sent)
+        share_cores(group, sent, 0)
+        sent = share_segments(group, sent)
+    for layer in reversed(range(layers)):
+        for piece in last:
+            sent = piece(layer)([sent, residuals.get(GROUPS - 2)] if layer == 0 else sent)
+        if layer == 1:
+            sent = share_cores(GROUPS - 1, sent)
+    share_cores(GROUPS - 1, sent, 0)
+    share_segments(GROUPS - 1, sent)
     own = jnp.stack([residuals[group] for group in range(GROUPS)], axis=1)
     residual = targets[0].astype(F32) - own.reshape(targets.shape[1:])
     features = jnp.concatenate(

time: 257 us -> 220 us (0.86)
  matrix products: 49 us -> 30.4 us
  between operations: 15.8 us -> 1.59 us
  starting transfers between devices: 100 us -> 113 us
  waiting for transfers between devices: 70.3 us -> 60.5 us
  other arithmetic: 11.3 us -> 7.08 us
    dot_general x16, matrix products: 41.8 us -> 23.2 us  [run(): lax.dot_general(after(codes[0], sent), decoders[layer, :, chunk * width:(...]
    unnamed x4 -> x0, waiting for transfers between devices: 12.1 us -> none
    ppermute x3 -> x6, starting transfers between devices: 8.41 us -> 15.1 us  [share_segments(): lax.ppermute(given[-1], 'segment', [(i, j) for i, j in pairs if i < j < s...]
    ppermute x36, starting transfers between devices: 86.2 us -> 91.1 us  [swap(): return lax.ppermute(value, 'feat', pairs) if pairs else None]
  transfers between devices with their start and end apart: 46 -> 49, of which waited for: 16 -> 15; matrix products, arithmetic and copies ran while one was open for 22% -> 15% of each run, Pallas kernels for 0% -> 0%
where the time goes in v5:
time: 220 us; the launch traced here: 219 us
  starting transfers between devices  113 us (51%)
  waiting for transfers between devices  60.5 us (28%)
  matrix products  30.4 us (14%)
  other arithmetic  7.08 us (3%)
  blocking collectives  4.68 us (2%)
  local copies, waits for them, and re-layouts  2.23 us (1%)
    ppermute x36, starting transfers between devices, swap(): return lax.ppermute(value, 'feat', pairs) if pairs else None  91.1 us
    ppermute x36, waiting for transfers between devices, swap(): return lax.ppermute(value, 'feat', pairs) if pairs else None  48.9 us
    dot_general x16, matrix products, run(): lax.dot_general(after(codes[0], sent), decoders[layer, :, chunk * width:(...  23.2 us
    ppermute x6, starting transfers between devices, share_segments(): lax.ppermute(given[-1], 'segment', [(i, j) for i, j in pairs if i < j < s...  15.1 us
    dot_general x4, matrix products, partial_sums(): jnp.dot(columns[group], weight[:, chunk * width:(chunk + 1) * width], pre...  7.18 us
    ppermute x3, starting transfers between devices, exchanged(): part = lax.ppermute(part, 'feat', pairs)  5.6 us
    ppermute x3, waiting for transfers between devices, exchanged(): part = lax.ppermute(part, 'feat', pairs)  5.4 us
    ppermute x6, waiting for transfers between devices, share_segments(): lax.ppermute(given[-1], 'segment', [(i, j) for i, j in pairs if i < j < s...  4.64 us
  transfers between devices with their start and end apart: 49, of which 15 were waited for; matrix products, arithmetic and copies ran while one was open for 15% of the time, Pallas kernels for 0%

profile of v5, /device:TPU:0, one launch (start us, length us, event | category | flops | bytes accessed | tf_op | source)
XLA Modules:
  0.0 219.2 jit_solution(15394632780316039041)
XLA Ops:
  0.7 2.5 %all-gather = bf16[1,112,2304]{2,1,0:T(8,128)(2,1)S(1)} all-gather(bf16[1,112,1152]{2,1,0:T(8,128)(2,1)} %param.5), channel_id=2, replica_groups=mesh['segment'=4,'feat'=4,'tok'=2] {'tok'}, dimensions={2}, use_global_device_ids=true | all-gather | bytes 774144 | tf_op jit(solution)/shard_map/all_gather | solution.py:27
  3.3 4.0 %collective-permute-start.1 = (bf16[56,576]{1,0:T(8,128)(2,1)S(1)}, bf16[56,576]{1,0:T(8,128)(2,1)S(1)}, u32[]{:S(2)}, u32[]{:S(2)}) collective-permute-start(bf16[56,576]{1,0:T(8,128)(2,1)S(1)} %get-tuple-element.185), channel_id=1, source_target_pairs={{0,4},{2,6},{4,0},{6,2},{1,5},{3,7},{5,1},{7,3},{8,12},{10,14},{12... | collective-permute-start | bytes 193544 | tf_op jit(solution)/shard_map/ppermute | solution.py:40
  7.3 1.6 collective-permute-start
  11.8 3.3 %collective-permute-done.2 = bf16[56,576]{1,0:T(8,128)(2,1)S(1)} collective-permute-done((bf16[56,576]{1,0:T(8,128)(2,1)S(1)}, bf16[56,576]{1,0:T(8,128)(2,1)S(1)}, u32[]{:S(2)}, u32[]{:S(2)}) %collective-permute-start.2) | collective-permute-done | bytes 64544 | tf_op jit(solution)/shard_map/ppermute | solution.py:40
  15.1 2.2 %all_gather.7 = bf16[4,112,576]{2,1,0:T(8,128)(2,1)S(1)} all-gather(bf16[4,56,576]{2,1,0:T(8,128)(2,1)S(1)} %pad_maximum_fusion.9), channel_id=1, replica_groups=mesh['segment'=4,'feat'=4,'tok'=2] {'tok'}, dimensions={1}, use_global_device_ids=true | all-gather | bytes 774144 | tf_op jit(solution)/shard_map/all_gather | solution.py:42
  17.4 3.4 %convolution_convert_fusion.2 = bf16[224,3072]{1,0:T(8,128)(2,1)S(1)} fusion(bf16[576,6144]{1,0:T(8,128)(2,1)} %bitcast.174, bf16[56,576]{1,0:T(8,128)(2,1)S(1)} %get-tuple-element.177, bf16[56,576]{1,0:T(8,128)(2,1)S(1)} %get-tuple-element.178, bf16[56,576]{1,0:T(8,128)(2,1)S(1)} %get-tuple-element.179, bf16[56,576]{1,0:T(8,128)(2,1)S(1)} %get-tuple-element.180), kind=kOutput, calls=%fused_computation.2 | convolution fusion | flops 794443776 | bytes 5173248 | tf_op jit(solution)/shard_map/dot_general | solution.py:53
  22.8 2.3 %collective-permute-start.8 = (bf16[56,3072]{1,0:T(8,128)(2,1)S(1)}, bf16[56,3072]{1,0:T(8,128)(2,1)S(1)}, u32[]{:S(2)}, u32[]{:S(2)}) collective-permute-start(bf16[56,3072]{1,0:T(8,128)(2,1)S(1)} %get-tuple-element.156), channel_id=1, source_target_pairs={{0,2},{6,4},{1,3},{7,5},{8,10},{14,12},{9,11},{15,13},{16,18},{22,... | collective-permute-start | bytes 1032200 | tf_op jit(solution)/shard_map/ppermute | solution.py:127
  31.7 16.5 %collective-permute-done.3 = bf16[56,3072]{1,0:T(8,128)(2,1)S(1)} collective-permute-done((bf16[56,3072]{1,0:T(8,128)(2,1)S(1)}, bf16[56,3072]{1,0:T(8,128)(2,1)S(1)}, u32[]{:S(2)}, u32[]{:S(2)}) %collective-permute-start.3) | collective-permute-done | bytes 344096 | tf_op jit(solution)/shard_map/ppermute | solution.py:127
  49.9 4.9 %collective-permute-done.6 = bf16[56,3072]{1,0:T(8,128)(2,1)S(1)} collective-permute-done((bf16[56,3072]{1,0:T(8,128)(2,1)S(1)}, bf16[56,3072]{1,0:T(8,128)(2,1)S(1)}, u32[]{:S(2)}, u32[]{:S(2)}) %collective-permute-start.6) | collective-permute-done | bytes 344096 | tf_op jit(solution)/shard_map/ppermute | solution.py:127
  55.1 9.5 %collective-permute-start.5 = (bf16[56,3072]{1,0:T(8,128)(2,1)S(1)}, bf16[56,3072]{1,0:T(8,128)(2,1)S(1)}, u32[]{:S(2)}, u32[]{:S(2)}) collective-permute-start(bf16[56,3072]{1,0:T(8,128)(2,1)S(1)} %get-tuple-element.150), channel_id=1, source_target_pairs={{0,2},{2,0},{4,6},{6,4},{1,3},{3,1},{5,7},{7,5},{8,10},{10,8},{12,... | collective-permute-start | bytes 1032200 | tf_op jit(solution)/shard_map/ppermute | solution.py:127
  65.6 6.3 %collective-permute-start.10 = (bf16[56,3072]{1,0:T(8,128)(2,1)S(1)}, bf16[56,3072]{1,0:T(8,128)(2,1)S(1)}, u32[]{:S(2)}, u32[]{:S(2)}) collective-permute-start(bf16[56,3072]{1,0:T(8,128)(2,1)S(1)} %get-tuple-element.154), channel_id=1, source_target_pairs={{0,2},{2,0},{4,6},{6,4},{1,3},{3,1},{5,7},{7,5},{8,10},{10,8},{12,... | collective-permute-start | bytes 1032200 | tf_op jit(solution)/shard_map/ppermute | solution.py:127
  72.8 6.4 %collective-permute-start.16 = (bf16[56,3072]{1,0:T(8,128)(2,1)S(1)}, bf16[56,3072]{1,0:T(8,128)(2,1)S(1)}, u32[]{:S(2)}, u32[]{:S(2)}) collective-permute-start(bf16[56,3072]{1,0:T(8,128)(2,1)S(1)} %maximum_convert_fusion.3), channel_id=1, source_target_pairs={{0,2},{2,0},{4,6},{6,4},{1,3},{3,1},{5,7},{7,5},{8,10},{10,8},{12,... | collective-permute-start | bytes 1032200 | tf_op jit(solution)/shard_map/ppermute | solution.py:127
  80.8 9.7 %collective-permute-start.19 = (bf16[56,3072]{1,0:T(8,128)(2,1)S(1)}, bf16[56,3072]{1,0:T(8,128)(2,1)S(1)}, u32[]{:S(2)}, u32[]{:S(2)}) collective-permute-start(bf16[56,3072]{1,0:T(8,128)(2,1)S(1)} %maximum_convert_fusion.2), channel_id=1, source_target_pairs={{0,2},{2,0},{4,6},{6,4},{1,3},{3,1},{5,7},{7,5},{8,10},{10,8},{12,... | collective-permute-start | bytes 1032200 | tf_op jit(solution)/shard_map/ppermute | solution.py:127
  91.5 6.5 %collective-permute-start.14 = (bf16[56,3072]{1,0:T(8,128)(2,1)S(1)}, bf16[56,3072]{1,0:T(8,128)(2,1)S(1)}, u32[]{:S(2)}, u32[]{:S(2)}) collective-permute-start(bf16[56,3072]{1,0:T(8,128)(2,1)S(1)} %get-tuple-element.149), channel_id=1, source_target_pairs={{0,2},{2,0},{4,6},{6,4},{1,3},{3,1},{5,7},{7,5},{8,10},{10,8},{12,... | collective-permute-start | bytes 1032200 | tf_op jit(solution)/shard_map/ppermute | solution.py:127
  98.2 3.2 %collective-permute-start.22 = (bf16[56,3072]{1,0:T(8,128)(2,1)S(1)}, bf16[56,3072]{1,0:T(8,128)(2,1)S(1)}, u32[]{:S(2)}, u32[]{:S(2)}) collective-permute-start(bf16[56,3072]{1,0:T(8,128)(2,1)S(1)} %get-tuple-element.144), channel_id=1, source_target_pairs={{0,2},{2,0},{4,6},{6,4},{1,3},{3,1},{5,7},{7,5},{8,10},{10,8},{12,... | collective-permute-start | bytes 1032200 | tf_op jit(solution)/shard_map/ppermute | solution.py:127
  102.2 4.6 %collective-permute-done.14 = bf16[56,3072]{1,0:T(8,128)(2,1)S(1)} collective-permute-done((bf16[56,3072]{1,0:T(8,128)(2,1)S(1)}, bf16[56,3072]{1,0:T(8,128)(2,1)S(1)}, u32[]{:S(2)}, u32[]{:S(2)}) %collective-permute-start.14) | collective-permute-done | bytes 344096 | tf_op jit(solution)/shard_map/ppermute | solution.py:127
  107.7 5.0 %collective-permute-start.18 = (bf16[56,3072]{1,0:T(8,128)(2,1)S(1)}, bf16[56,3072]{1,0:T(8,128)(2,1)S(1)}, u32[]{:S(2)}, u32[]{:S(2)}) collective-permute-start(bf16[56,3072]{1,0:T(8,128)(2,1)S(1)} %get-tuple-element.147), channel_id=1, source_target_pairs={{0,2},{2,0},{4,6},{6,4},{1,3},{3,1},{5,7},{7,5},{8,10},{10,8},{12,... | collective-permute-start | bytes 1032200 | tf_op jit(solution)/shard_map/ppermute | solution.py:127
  113.8 6.4 %collective-permute-start.27 = (bf16[56,3072]{1,0:T(8,128)(2,1)S(1)}, bf16[56,3072]{1,0:T(8,128)(2,1)S(1)}, u32[]{:S(2)}, u32[]{:S(2)}) collective-permute-start(bf16[56,3072]{1,0:T(8,128)(2,1)S(1)} %get-tuple-element.143), channel_id=1, source_target_pairs={{0,2},{2,0},{4,6},{6,4},{1,3},{3,1},{5,7},{7,5},{8,10},{10,8},{12,... | collective-permute-start | bytes 1032200 | tf_op jit(solution)/shard_map/ppermute | solution.py:127
  124.5 6.3 %collective-permute-start.23 = (bf16[56,3072]{1,0:T(8,128)(2,1)S(1)}, bf16[56,3072]{1,0:T(8,128)(2,1)S(1)}, u32[]{:S(2)}, u32[]{:S(2)}) collective-permute-start(bf16[56,3072]{1,0:T(8,128)(2,1)S(1)} %get-tuple-element.139), channel_id=1, source_target_pairs={{0,2},{2,0},{4,6},{6,4},{1,3},{3,1},{5,7},{7,5},{8,10},{10,8},{12,... | collective-permute-start | bytes 1032200 | tf_op jit(solution)/shard_map/ppermute | solution.py:127
  136.4 2.1 collective-permute-done.23
  139.3 4.5 %collective-permute-start.29 = (bf16[56,3072]{1,0:T(8,128)(2,1)S(1)}, bf16[56,3072]{1,0:T(8,128)(2,1)S(1)}, u32[]{:S(2)}, u32[]{:S(2)}) collective-permute-start(bf16[56,3072]{1,0:T(8,128)(2,1)S(1)} %maximum_convert_fusion.1), channel_id=1, source_target_pairs={{0,2},{2,0},{4,6},{6,4},{1,3},{3,1},{5,7},{7,5},{8,10},{10,8},{12,... | collective-permute-start | bytes 1032200 | tf_op jit(solution)/shard_map/ppermute | solution.py:127
  143.8 2.0 collective-permute-done.26
  146.7 4.4 %collective-permute-start.31 = (bf16[56,3072]{1,0:T(8,128)(2,1)S(1)}, bf16[56,3072]{1,0:T(8,128)(2,1)S(1)}, u32[]{:S(2)}, u32[]{:S(2)}) collective-permute-start(bf16[56,3072]{1,0:T(8,128)(2,1)S(1)} %maximum_convert_fusion), channel_id=1, source_target_pairs={{0,2},{2,0},{4,6},{6,4},{1,3},{3,1},{5,7},{7,5},{8,10},{10,8},{12,... | collective-permute-start | bytes 1032200 | tf_op jit(solution)/shard_map/ppermute | solution.py:127
  154.0 2.9 %collective-permute-done.31 = bf16[56,3072]{1,0:T(8,128)(2,1)S(1)} collective-permute-done((bf16[56,3072]{1,0:T(8,128)(2,1)S(1)}, bf16[56,3072]{1,0:T(8,128)(2,1)S(1)}, u32[]{:S(2)}, u32[]{:S(2)}) %collective-permute-start.31) | collective-permute-done | bytes 344096 | tf_op jit(solution)/shard_map/ppermute | solution.py:127
  165.7 1.6 collective-permute-done.34
  167.6 8.3 %collective-permute-done.39 = bf16[56,3072]{1,0:T(8,128)(2,1)S(1)} collective-permute-done((bf16[56,3072]{1,0:T(8,128)(2,1)S(1)}, bf16[56,3072]{1,0:T(8,128)(2,1)S(1)}, u32[]{:S(2)}, u32[]{:S(2)}) %collective-permute-start.39) | collective-permute-done | bytes 344096 | tf_op jit(solution)/shard_map/ppermute | solution.py:127
  175.9 4.4 %collective-permute-start.37 = (bf16[2,56,576]{2,1,0:T(8,128)(2,1)S(1)}, bf16[2,56,576]{2,1,0:T(8,128)(2,1)S(1)}, u32[]{:S(2)}, u32[]{:S(2)}) collective-permute-start(bf16[2,56,576]{2,1,0:T(8,128)(2,1)S(1)} %get-tuple-element.165), channel_id=1, source_target_pairs={{0,24},{8,16},{1,25},{9,17},{2,26},{10,18},{3,27},{11,19},{4,28},{... | collective-permute-start | bytes 387080 | tf_op jit(solution)/shard_map/ppermute | solution.py:203
  180.2 7.6 %collective-permute-done.40 = bf16[56,3072]{1,0:T(8,128)(2,1)S(1)} collective-permute-done((bf16[56,3072]{1,0:T(8,128)(2,1)S(1)}, bf16[56,3072]{1,0:T(8,128)(2,1)S(1)}, u32[]{:S(2)}, u32[]{:S(2)}) %collective-permute-start.40) | collective-permute-done | bytes 344096 | tf_op jit(solution)/shard_map/ppermute | solution.py:127
  187.8 3.4 %collective-permute-start.36 = (bf16[2,56,576]{2,1,0:T(8,128)(2,1)S(1)}, bf16[2,56,576]{2,1,0:T(8,128)(2,1)S(1)}, u32[]{:S(2)}, u32[]{:S(2)}) collective-permute-start(bf16[2,56,576]{2,1,0:T(8,128)(2,1)S(1)} %get-tuple-element.166), channel_id=1, source_target_pairs={{0,16},{8,24},{1,17},{9,25},{2,18},{10,26},{3,19},{11,27},{4,20},{... | collective-permute-start | bytes 387080 | tf_op jit(solution)/shard_map/ppermute | solution.py:203
  193.0 3.5 %collective-permute-start.35 = (bf16[2,56,576]{2,1,0:T(8,128)(2,1)S(1)}, bf16[2,56,576]{2,1,0:T(8,128)(2,1)S(1)}, u32[]{:S(2)}, u32[]{:S(2)}) collective-permute-start(bf16[2,56,576]{2,1,0:T(8,128)(2,1)S(1)} %get-tuple-element.167), channel_id=1, source_target_pairs={{0,8},{16,24},{1,9},{17,25},{2,10},{18,26},{3,11},{19,27},{4,12},{... | collective-permute-start | bytes 387080 | tf_op jit(solution)/shard_map/ppermute | solution.py:203
  213.7 2.5 %collective-permute-done.48 = bf16[2,56,576]{2,1,0:T(8,128)(2,1)S(1)} collective-permute-done((bf16[2,56,576]{2,1,0:T(8,128)(2,1)S(1)}, bf16[2,56,576]{2,1,0:T(8,128)(2,1)S(1)}, u32[]{:S(2)}, u32[]{:S(2)}) %collective-permute-start.48) | collective-permute-done | bytes 129056 | tf_op jit(solution)/shard_map/ppermute | solution.py:203
  216.2 1.9 collective-permute-done.47
  (162 shorter events, 64.1 us)
Async XLA Ops:
  22.8 26.3 %collective-permute-start.8 = (bf16[56,3072]{1,0:T(8,128)(2,1)S(1)}, bf16[56,3072]{1,0:T(8,128)(2,1)S(1)}, u32[]{:S(2)}, u32[]{:S(2)}) collective-permute-start(bf16[56,3072]{1,0:T(8,128)(2,1)S(1)} %get-tuple-element.156), channel_id=1, source_target_pairs={{0,2},{6,4},{1,3},{7,5},{8,10},{14,12},{9,11},{15,13},{16,18},{22,... | collective-permute-start | bytes 1032200 | tf_op jit(solution)/shard_map/ppermute | solution.py:127
  25.1 40.3 %collective-permute-start.11 = (bf16[56,3072]{1,0:T(8,128)(2,1)S(1)}, bf16[56,3072]{1,0:T(8,128)(2,1)S(1)}, u32[]{:S(2)}, u32[]{:S(2)}) collective-permute-start(bf16[56,3072]{1,0:T(8,128)(2,1)S(1)} %get-tuple-element.157), channel_id=1, source_target_pairs={{0,2},{6,4},{1,3},{7,5},{8,10},{14,12},{9,11},{15,13},{16,18},{22,... | collective-permute-start | bytes 1032200 | tf_op jit(solution)/shard_map/ppermute | solution.py:127
  26.5 21.7 %collective-permute-start.3 = (bf16[56,3072]{1,0:T(8,128)(2,1)S(1)}, bf16[56,3072]{1,0:T(8,128)(2,1)S(1)}, u32[]{:S(2)}, u32[]{:S(2)}) collective-permute-start(bf16[56,3072]{1,0:T(8,128)(2,1)S(1)} %get-tuple-element.152), channel_id=1, source_target_pairs={{0,2},{6,4},{1,3},{7,5},{8,10},{14,12},{9,11},{15,13},{16,18},{22,... | collective-permute-start | bytes 1032200 | tf_op jit(solution)/shard_map/ppermute | solution.py:127
  27.8 27.0 %collective-permute-start.6 = (bf16[56,3072]{1,0:T(8,128)(2,1)S(1)}, bf16[56,3072]{1,0:T(8,128)(2,1)S(1)}, u32[]{:S(2)}, u32[]{:S(2)}) collective-permute-start(bf16[56,3072]{1,0:T(8,128)(2,1)S(1)} %get-tuple-element.153), channel_id=1, source_target_pairs={{0,2},{6,4},{1,3},{7,5},{8,10},{14,12},{9,11},{15,13},{16,18},{22,... | collective-permute-start | bytes 1032200 | tf_op jit(solution)/shard_map/ppermute | solution.py:127
  49.2 16.1 %collective-permute-start.9 = (bf16[56,3072]{1,0:T(8,128)(2,1)S(1)}, bf16[56,3072]{1,0:T(8,128)(2,1)S(1)}, u32[]{:S(2)}, u32[]{:S(2)}) collective-permute-start(bf16[56,3072]{1,0:T(8,128)(2,1)S(1)} %add_convert_fusion.14), channel_id=1, source_target_pairs={{2,4},{4,2},{3,5},{5,3},{10,12},{12,10},{11,13},{13,11},{18,20},{2... | collective-permute-start | bytes 1032200 | tf_op jit(solution)/shard_map/ppermute | solution.py:127
  55.1 17.5 %collective-permute-start.5 = (bf16[56,3072]{1,0:T(8,128)(2,1)S(1)}, bf16[56,3072]{1,0:T(8,128)(2,1)S(1)}, u32[]{:S(2)}, u32[]{:S(2)}) collective-permute-start(bf16[56,3072]{1,0:T(8,128)(2,1)S(1)} %get-tuple-element.150), channel_id=1, source_target_pairs={{0,2},{2,0},{4,6},{6,4},{1,3},{3,1},{5,7},{7,5},{8,10},{10,8},{12,... | collective-permute-start | bytes 1032200 | tf_op jit(solution)/shard_map/ppermute | solution.py:127
  65.6 14.3 %collective-permute-start.10 = (bf16[56,3072]{1,0:T(8,128)(2,1)S(1)}, bf16[56,3072]{1,0:T(8,128)(2,1)S(1)}, u32[]{:S(2)}, u32[]{:S(2)}) collective-permute-start(bf16[56,3072]{1,0:T(8,128)(2,1)S(1)} %get-tuple-element.154), channel_id=1, source_target_pairs={{0,2},{2,0},{4,6},{6,4},{1,3},{3,1},{5,7},{7,5},{8,10},{10,8},{12,... | collective-permute-start | bytes 1032200 | tf_op jit(solution)/shard_map/ppermute | solution.py:127
  72.8 17.7 %collective-permute-start.16 = (bf16[56,3072]{1,0:T(8,128)(2,1)S(1)}, bf16[56,3072]{1,0:T(8,128)(2,1)S(1)}, u32[]{:S(2)}, u32[]{:S(2)}) collective-permute-start(bf16[56,3072]{1,0:T(8,128)(2,1)S(1)} %maximum_convert_fusion.3), channel_id=1, source_target_pairs={{0,2},{2,0},{4,6},{6,4},{1,3},{3,1},{5,7},{7,5},{8,10},{10,8},{12,... | collective-permute-start | bytes 1032200 | tf_op jit(solution)/shard_map/ppermute | solution.py:127
  80.1 17.9 %collective-permute-start.21 = (bf16[56,3072]{1,0:T(8,128)(2,1)S(1)}, bf16[56,3072]{1,0:T(8,128)(2,1)S(1)}, u32[]{:S(2)}, u32[]{:S(2)}) collective-permute-start(bf16[56,3072]{1,0:T(8,128)(2,1)S(1)} %maximum_convert_fusion.2), channel_id=1, source_target_pairs={{2,4},{4,2},{3,5},{5,3},{10,12},{12,10},{11,13},{13,11},{18,20},{2... | collective-permute-start | bytes 1032200 | tf_op jit(solution)/shard_map/ppermute | solution.py:127
  80.8 17.2 %collective-permute-start.19 = (bf16[56,3072]{1,0:T(8,128)(2,1)S(1)}, bf16[56,3072]{1,0:T(8,128)(2,1)S(1)}, u32[]{:S(2)}, u32[]{:S(2)}) collective-permute-start(bf16[56,3072]{1,0:T(8,128)(2,1)S(1)} %maximum_convert_fusion.2), channel_id=1, source_target_pairs={{0,2},{2,0},{4,6},{6,4},{1,3},{3,1},{5,7},{7,5},{8,10},{10,8},{12,... | collective-permute-start | bytes 1032200 | tf_op jit(solution)/shard_map/ppermute | solution.py:127
  90.8 11.4 %collective-permute-start.17 = (bf16[56,3072]{1,0:T(8,128)(2,1)S(1)}, bf16[56,3072]{1,0:T(8,128)(2,1)S(1)}, u32[]{:S(2)}, u32[]{:S(2)}) collective-permute-start(bf16[56,3072]{1,0:T(8,128)(2,1)S(1)} %get-tuple-element.148), channel_id=1, source_target_pairs={{2,4},{4,2},{3,5},{5,3},{10,12},{12,10},{11,13},{13,11},{18,20},{2... | collective-permute-start | bytes 1032200 | tf_op jit(solution)/shard_map/ppermute | solution.py:127
  91.5 15.3 %collective-permute-start.14 = (bf16[56,3072]{1,0:T(8,128)(2,1)S(1)}, bf16[56,3072]{1,0:T(8,128)(2,1)S(1)}, u32[]{:S(2)}, u32[]{:S(2)}) collective-permute-start(bf16[56,3072]{1,0:T(8,128)(2,1)S(1)} %get-tuple-element.149), channel_id=1, source_target_pairs={{0,2},{2,0},{4,6},{6,4},{1,3},{3,1},{5,7},{7,5},{8,10},{10,8},{12,... | collective-permute-start | bytes 1032200 | tf_op jit(solution)/shard_map/ppermute | solution.py:127
  98.2 14.5 %collective-permute-start.22 = (bf16[56,3072]{1,0:T(8,128)(2,1)S(1)}, bf16[56,3072]{1,0:T(8,128)(2,1)S(1)}, u32[]{:S(2)}, u32[]{:S(2)}) collective-permute-start(bf16[56,3072]{1,0:T(8,128)(2,1)S(1)} %get-tuple-element.144), channel_id=1, source_target_pairs={{0,2},{2,0},{4,6},{6,4},{1,3},{3,1},{5,7},{7,5},{8,10},{10,8},{12,... | collective-permute-start | bytes 1032200 | tf_op jit(solution)/shard_map/ppermute | solution.py:127
  107.0 13.2 %collective-permute-start.15 = (bf16[56,3072]{1,0:T(8,128)(2,1)S(1)}, bf16[56,3072]{1,0:T(8,128)(2,1)S(1)}, u32[]{:S(2)}, u32[]{:S(2)}) collective-permute-start(bf16[56,3072]{1,0:T(8,128)(2,1)S(1)} %get-tuple-element.146), channel_id=1, source_target_pairs={{2,4},{4,2},{3,5},{5,3},{10,12},{12,10},{11,13},{13,11},{18,20},{2... | collective-permute-start | bytes 1032200 | tf_op jit(solution)/shard_map/ppermute | solution.py:127
  107.7 12.5 %collective-permute-start.18 = (bf16[56,3072]{1,0:T(8,128)(2,1)S(1)}, bf16[56,3072]{1,0:T(8,128)(2,1)S(1)}, u32[]{:S(2)}, u32[]{:S(2)}) collective-permute-start(bf16[56,3072]{1,0:T(8,128)(2,1)S(1)} %get-tuple-element.147), channel_id=1, source_target_pairs={{0,2},{2,0},{4,6},{6,4},{1,3},{3,1},{5,7},{7,5},{8,10},{10,8},{12,... | collective-permute-start | bytes 1032200 | tf_op jit(solution)/shard_map/ppermute | solution.py:127
  112.9 20.7 %collective-permute-start.25 = (bf16[56,3072]{1,0:T(8,128)(2,1)S(1)}, bf16[56,3072]{1,0:T(8,128)(2,1)S(1)}, u32[]{:S(2)}, u32[]{:S(2)}) collective-permute-start(bf16[56,3072]{1,0:T(8,128)(2,1)S(1)} %get-tuple-element.142), channel_id=1, source_target_pairs={{2,4},{4,2},{3,5},{5,3},{10,12},{12,10},{11,13},{13,11},{18,20},{2... | collective-permute-start | bytes 1032200 | tf_op jit(solution)/shard_map/ppermute | solution.py:127
  113.8 19.8 %collective-permute-start.27 = (bf16[56,3072]{1,0:T(8,128)(2,1)S(1)}, bf16[56,3072]{1,0:T(8,128)(2,1)S(1)}, u32[]{:S(2)}, u32[]{:S(2)}) collective-permute-start(bf16[56,3072]{1,0:T(8,128)(2,1)S(1)} %get-tuple-element.143), channel_id=1, source_target_pairs={{0,2},{2,0},{4,6},{6,4},{1,3},{3,1},{5,7},{7,5},{8,10},{10,8},{12,... | collective-permute-start | bytes 1032200 | tf_op jit(solution)/shard_map/ppermute | solution.py:127
  123.8 12.6 %collective-permute-start.24 = (bf16[56,3072]{1,0:T(8,128)(2,1)S(1)}, bf16[56,3072]{1,0:T(8,128)(2,1)S(1)}, u32[]{:S(2)}, u32[]{:S(2)}) collective-permute-start(bf16[56,3072]{1,0:T(8,128)(2,1)S(1)} %get-tuple-element.138), channel_id=1, source_target_pairs={{2,4},{4,2},{3,5},{5,3},{10,12},{12,10},{11,13},{13,11},{18,20},{2... | collective-permute-start | bytes 1032200 | tf_op jit(solution)/shard_map/ppermute | solution.py:127
  124.5 14.0 %collective-permute-start.23 = (bf16[56,3072]{1,0:T(8,128)(2,1)S(1)}, bf16[56,3072]{1,0:T(8,128)(2,1)S(1)}, u32[]{:S(2)}, u32[]{:S(2)}) collective-permute-start(bf16[56,3072]{1,0:T(8,128)(2,1)S(1)} %get-tuple-element.139), channel_id=1, source_target_pairs={{0,2},{2,0},{4,6},{6,4},{1,3},{3,1},{5,7},{7,5},{8,10},{10,8},{12,... | collective-permute-start | bytes 1032200 | tf_op jit(solution)/shard_map/ppermute | solution.py:127
  133.9 11.9 %collective-permute-start.26 = (bf16[56,3072]{1,0:T(8,128)(2,1)S(1)}, bf16[56,3072]{1,0:T(8,128)(2,1)S(1)}, u32[]{:S(2)}, u32[]{:S(2)}) collective-permute-start(bf16[56,3072]{1,0:T(8,128)(2,1)S(1)} %get-tuple-element.136), channel_id=1, source_target_pairs={{0,2},{2,0},{4,6},{6,4},{1,3},{3,1},{5,7},{7,5},{8,10},{10,8},{12,... | collective-permute-start | bytes 1032200 | tf_op jit(solution)/shard_map/ppermute | solution.py:127
  134.0 11.9 %collective-permute-start.28 = (bf16[56,3072]{1,0:T(8,128)(2,1)S(1)}, bf16[56,3072]{1,0:T(8,128)(2,1)S(1)}, u32[]{:S(2)}, u32[]{:S(2)}) collective-permute-start(bf16[56,3072]{1,0:T(8,128)(2,1)S(1)} %get-tuple-element.137), channel_id=1, source_target_pairs={{2,4},{4,2},{3,5},{5,3},{10,12},{12,10},{11,13},{13,11},{18,20},{2... | collective-permute-start | bytes 1032200 | tf_op jit(solution)/shard_map/ppermute | solution.py:127
  138.6 21.1 %collective-permute-start.38 = (bf16[56,3072]{1,0:T(8,128)(2,1)S(1)}, bf16[56,3072]{1,0:T(8,128)(2,1)S(1)}, u32[]{:S(2)}, u32[]{:S(2)}) collective-permute-start(bf16[56,3072]{1,0:T(8,128)(2,1)S(1)} %maximum_convert_fusion.1), channel_id=1, source_target_pairs={{2,4},{4,2},{3,5},{5,3},{10,12},{12,10},{11,13},{13,11},{18,20},{2... | collective-permute-start | bytes 1032200 | tf_op jit(solution)/shard_map/ppermute | solution.py:127
  139.3 17.5 %collective-permute-start.29 = (bf16[56,3072]{1,0:T(8,128)(2,1)S(1)}, bf16[56,3072]{1,0:T(8,128)(2,1)S(1)}, u32[]{:S(2)}, u32[]{:S(2)}) collective-permute-start(bf16[56,3072]{1,0:T(8,128)(2,1)S(1)} %maximum_convert_fusion.1), channel_id=1, source_target_pairs={{0,2},{2,0},{4,6},{6,4},{1,3},{3,1},{5,7},{7,5},{8,10},{10,8},{12,... | collective-permute-start | bytes 1032200 | tf_op jit(solution)/shard_map/ppermute | solution.py:127
  146.0 13.7 %collective-permute-start.41 = (bf16[56,3072]{1,0:T(8,128)(2,1)S(1)}, bf16[56,3072]{1,0:T(8,128)(2,1)S(1)}, u32[]{:S(2)}, u32[]{:S(2)}) collective-permute-start(bf16[56,3072]{1,0:T(8,128)(2,1)S(1)} %maximum_convert_fusion), channel_id=1, source_target_pairs={{2,4},{4,2},{3,5},{5,3},{10,12},{12,10},{11,13},{13,11},{18,20},{2... | collective-permute-start | bytes 1032200 | tf_op jit(solution)/shard_map/ppermute | solution.py:127
  159.7 16.2 %collective-permute-start.39 = (bf16[56,3072]{1,0:T(8,128)(2,1)S(1)}, bf16[56,3072]{1,0:T(8,128)(2,1)S(1)}, u32[]{:S(2)}, u32[]{:S(2)}) collective-permute-start(bf16[56,3072]{1,0:T(8,128)(2,1)S(1)} %collective-permute-done.38), channel_id=1, source_target_pairs={{2,0},{4,6},{3,1},{5,7},{10,8},{12,14},{11,9},{13,15},{18,16},{20,... | collective-permute-start | bytes 1032200 | tf_op jit(solution)/shard_map/ppermute | solution.py:127
  161.0 31.9 %collective-permute-start.42 = (bf16[56,3072]{1,0:T(8,128)(2,1)S(1)}, bf16[56,3072]{1,0:T(8,128)(2,1)S(1)}, u32[]{:S(2)}, u32[]{:S(2)}) collective-permute-start(bf16[56,3072]{1,0:T(8,128)(2,1)S(1)} %collective-permute-done.41), channel_id=1, source_target_pairs={{2,0},{4,6},{3,1},{5,7},{10,8},{12,14},{11,9},{13,15},{18,16},{20,... | collective-permute-start | bytes 1032200 | tf_op jit(solution)/shard_map/ppermute | solution.py:127
  162.3 25.5 %collective-permute-start.40 = (bf16[56,3072]{1,0:T(8,128)(2,1)S(1)}, bf16[56,3072]{1,0:T(8,128)(2,1)S(1)}, u32[]{:S(2)}, u32[]{:S(2)}) collective-permute-start(bf16[56,3072]{1,0:T(8,128)(2,1)S(1)} %collective-permute-done.30), channel_id=1, source_target_pairs={{2,0},{4,6},{3,1},{5,7},{10,8},{12,14},{11,9},{13,15},{18,16},{20,... | collective-permute-start | bytes 1032200 | tf_op jit(solution)/shard_map/ppermute | solution.py:127
  163.6 32.8 %collective-permute-start.43 = (bf16[56,3072]{1,0:T(8,128)(2,1)S(1)}, bf16[56,3072]{1,0:T(8,128)(2,1)S(1)}, u32[]{:S(2)}, u32[]{:S(2)}) collective-permute-start(bf16[56,3072]{1,0:T(8,128)(2,1)S(1)} %collective-permute-done.32), channel_id=1, source_target_pairs={{2,0},{4,6},{3,1},{5,7},{10,8},{12,14},{11,9},{13,15},{18,16},{20,... | collective-permute-start | bytes 1032200 | tf_op jit(solution)/shard_map/ppermute | solution.py:127
  167.2 37.2 %collective-permute-start.33 = (bf16[1,2,56,576]{3,2,1,0:T(8,128)(2,1)S(1)}, bf16[1,2,56,576]{3,2,1,0:T(8,128)(2,1)S(1)}, u32[]{:S(2)}, u32[]{:S(2)}) collective-permute-start(bf16[1,2,56,576]{3,2,1,0:T(8,128)(2,1)S(1)} %pad_maximum_fusion.12), channel_id=1, source_target_pairs={{0,1},{1,0},{2,3},{3,2},{4,5},{5,4},{6,7},{7,6},{8,9},{9,8},{10,11... | collective-permute-start | bytes 387080 | tf_op jit(solution)/shard_map/ppermute | solution.py:190
  175.9 28.6 %collective-permute-start.37 = (bf16[2,56,576]{2,1,0:T(8,128)(2,1)S(1)}, bf16[2,56,576]{2,1,0:T(8,128)(2,1)S(1)}, u32[]{:S(2)}, u32[]{:S(2)}) collective-permute-start(bf16[2,56,576]{2,1,0:T(8,128)(2,1)S(1)} %get-tuple-element.165), channel_id=1, source_target_pairs={{0,24},{8,16},{1,25},{9,17},{2,26},{10,18},{3,27},{11,19},{4,28},{... | collective-permute-start | bytes 387080 | tf_op jit(solution)/shard_map/ppermute | solution.py:203
  187.8 16.7 %collective-permute-start.36 = (bf16[2,56,576]{2,1,0:T(8,128)(2,1)S(1)}, bf16[2,56,576]{2,1,0:T(8,128)(2,1)S(1)}, u32[]{:S(2)}, u32[]{:S(2)}) collective-permute-start(bf16[2,56,576]{2,1,0:T(8,128)(2,1)S(1)} %get-tuple-element.166), channel_id=1, source_target_pairs={{0,16},{8,24},{1,17},{9,25},{2,18},{10,26},{3,19},{11,27},{4,20},{... | collective-permute-start | bytes 387080 | tf_op jit(solution)/shard_map/ppermute | solution.py:203
  193.0 11.5 %collective-permute-start.35 = (bf16[2,56,576]{2,1,0:T(8,128)(2,1)S(1)}, bf16[2,56,576]{2,1,0:T(8,128)(2,1)S(1)}, u32[]{:S(2)}, u32[]{:S(2)}) collective-permute-start(bf16[2,56,576]{2,1,0:T(8,128)(2,1)S(1)} %get-tuple-element.167), channel_id=1, source_target_pairs={{0,8},{16,24},{1,9},{17,25},{2,10},{18,26},{3,11},{19,27},{4,12},{... | collective-permute-start | bytes 387080 | tf_op jit(solution)/shard_map/ppermute | solution.py:203
  (26 other events, 681.8 us)
